TPU v7x, 256 devices: a whole 4x4x8 slice. The times are simulated.
256 devices in a mesh: ctx: 32 (over y_lo, z, core), ch: 8 (over x, y_hi).
Axes of the slice: x: 4, y: 4 (y_hi: 2, y_lo: 2; y = y_hi * 2 + y_lo), z: 8, core: 2. Of those that a mesh axis runs over, the one named last changes fastest.
Arguments:
- outer_gate: bfloat16 [8192, 4096], P('ctx', 'ch'), may hold values from -6 to 6
- inner_gate: bfloat16 [8192, 4096], P('ctx', 'ch'), may hold values from -6 to 6
- values: bfloat16 [8192, 4096], P('ctx', 'ch'), may hold values from -6 to 6
- residues: float32 [16, 4096], P(None, 'ch'), may hold values from -0.18 to 0.18
- decays: float32 [16, 4096], P(None, 'ch'), may hold values from 1.2207031e-05 to 0.05
- out_weight: bfloat16 [4096, 8192], P('ch', 'ctx'), may hold values from -0.1875 to 0.1875
Outputs:
- projected: bfloat16 [8192, 8192], P('ctx', 'ch')
All inputs are finite; a program needn't handle non-finite values.
Results may differ from a plain program's by a relative error of at most 0.015.
Values may be sent and summed in bfloat16 or wider, within the bound.
No kernel may reach another device: no remote copies, remote signals or barrier semaphores. Data moves between devices by JAX's collectives and lax.ppermute only.
A program may use at most 64 MiB of HBM per device.

v0:
```python
import jax
import jax.numpy as jnp
from jax import lax
from jax.sharding import PartitionSpec as P

SPLIT = lax.Precision.HIGH


def entering(value, axis, combine, identity):
    count, index = (lax.axis_size(axis), lax.axis_index(axis))
    everything = jax.tree.map(lambda part: lax.all_gather(part, axis), value)
    start = jax.tree.map(
        lambda part, zero: jnp.broadcast_to(jnp.asarray(zero, part.dtype), part.shape),
        value,
        identity,
    )

    def hop(k, before):
        reached = k < index
        new = combine(before, jax.tree.map(lambda part: part[k], everything))
        return jax.tree.map(lambda a, b: jnp.where(reached, a, b), new, before)

    return lax.fori_loop(0, count, hop, start)


def dft_tables(length, count):
    frequency = lax.broadcasted_iota(jnp.int32, (length, count), 0)
    position = lax.broadcasted_iota(jnp.int32, (length, count), 1)
    angles = (frequency * position % length).astype(jnp.float32) * (2.0 * jnp.pi / length)
    return (jnp.cos(angles), jnp.sin(angles))


def combine_states(earlier, later):
    return (earlier[0] * later[0], earlier[1] * later[0] + later[1])


def shards(outer_gate, inner_gate, values, residues, decays, out_weight):
    block_rows = values.shape[0]
    width_local = values.shape[1]
    length = 2 * block_rows
    signal = (inner_gate.astype(jnp.float32) * values.astype(jnp.float32)).astype(jnp.bfloat16)
    widened = signal.astype(jnp.float32)
    position = lax.broadcasted_iota(jnp.int32, (block_rows, 1), 0).astype(jnp.float32)
    fade_end = jnp.exp(-decays[:, None, :] * (block_rows - 1.0 - position)[None, :, :])
    summary = jnp.sum(fade_end * widened[None, :, :], axis=1)
    block_fade = jnp.exp(-decays * block_rows)
    identity = (jnp.ones_like(block_fade), jnp.zeros_like(summary))
    carried = entering((block_fade, summary), "ctx", combine_states, identity)
    state = carried[1]
    fade_start = jnp.exp(-decays[:, None, :] * (position + 1.0)[None, :, :])
    carried_in = jnp.sum(residues[:, None, :] * fade_start * state[:, None, :], axis=0)
    kernel = jnp.sum(
        residues[:, None, :] * jnp.exp(-decays[:, None, :] * position[None, :, :]), axis=0
    )
    cosine_in, sine_in = dft_tables(length, block_rows)
    stacked = jnp.concatenate([widened, kernel], axis=1)
    spec_real = jnp.dot(cosine_in, stacked, precision=SPLIT)
    spec_imag = -jnp.dot(sine_in, stacked, precision=SPLIT)
    sig_real, ker_real = (spec_real[:, :width_local], spec_real[:, width_local:])
    sig_imag, ker_imag = (spec_imag[:, :width_local], spec_imag[:, width_local:])
    real_part = ker_real * sig_real - ker_imag * sig_imag
    imag_part = ker_real * sig_imag + ker_imag * sig_real
    local_part = (
        jnp.dot(cosine_in.T, real_part, precision=SPLIT)
        - jnp.dot(sine_in.T, imag_part, precision=SPLIT)
    ) / length
    convolved = local_part + carried_in
    gated = (outer_gate.astype(jnp.float32) * convolved).astype(jnp.bfloat16)
    partial_value = jnp.dot(
        gated,
        lax.all_gather(out_weight, "ctx", axis=1, tiled=True),
        preferred_element_type=jnp.float32,
    )
    summed = lax.psum(partial_value, "ch")
    width = summed.shape[1] // lax.axis_size("ch")
    result = lax.dynamic_slice_in_dim(summed, lax.axis_index("ch") * width, width, 1)
    return result.astype(jnp.bfloat16)


def solution(mesh):
    return jax.shard_map(
        shards,
        mesh=mesh,
        in_specs=(
            P("ctx", "ch"),
            P("ctx", "ch"),
            P("ctx", "ch"),
            P(None, "ch"),
            P(None, "ch"),
            P("ch", "ctx"),
        ),
        out_specs=P("ctx", "ch"),
        check_vma=False,
    )
```

profile of v0, /device:TPU:1, one launch (start us, length us, event | category | flops | bytes accessed | tf_op | source)
XLA Modules:
  0.0 579.3 jit_solution(11067300352035612797)
XLA Ops:
  6.5 1.4 multiply_exponential_fusion
  8.0 1.1 fusion.27
  9.1 2.1 multiply_reduce_fusion.1
  12.0 65.1 %all-gather.8.cloned.1.call-done = f32[512,512]{1,0:T(8,128)} async-done(((f32[16,512]{1,0:T(8,128)}), f32[512,512]{1,0:T(8,128)}) %all-gather.8.cloned.1.call-update) | async-done | bytes 1048592 | tf_op jit(solution)/shard_map/all_gather | solution.py:11
  77.1 65.2 %all-gather.10.cloned.1.call-done = f32[512,512]{1,0:T(8,128)} async-done(((f32[16,512]{1,0:T(8,128)}), f32[512,512]{1,0:T(8,128)}) %all-gather.10.cloned.1.call-update) | async-done | bytes 1048592 | tf_op jit(solution)/shard_map/all_gather | solution.py:11
  142.2 26.0 %while.14 = (s32[]{:T(128)}, f32[16,512]{1,0:T(8,128)S(1)}, s32[]{:T(128)}, f32[32,16,512]{2,1,0:T(8,128)}, f32[32,16,512]{2,1,0:T(8,128)}, /*index=5*/s32[]{:T(128)}, s32[]{:T(128)}) while((s32[]{:T(128)}, f32[16,512]{1,0:T(8,128)S(1)}, s32[]{:T(128)}, f32[32,16,512]{2,1,0:T(8,128)}, f32[32,16,512]{2,1,0:T(8,128)}, ...), condition=%wide.region_3.4_spmd.clone, body=%wide.region_2.3_spmd.clone.sunk | while | flops 32772 | bytes 131181 | solution.py:23
  143.0 0.8 fusion.58
  143.9 0.8 fusion.58
  144.7 0.8 fusion.58
  145.5 0.8 fusion.58
  154.4 0.8 fusion.58
  155.2 0.8 fusion.58
  160.9 0.8 fusion.58
  165.8 0.8 fusion.58
  166.6 0.8 fusion.58
  168.2 4.3 multiply_reduce_fusion.2
  172.6 2.9 convolution_negate_fusion
  175.5 2.9 fusion.20
  178.4 2.6 fusion.8
  181.0 2.7 fusion.4
  183.7 49.8 %all-gather.6.cloned.1.call-done = bf16[512,8192]{1,0:T(8,128)(2,1)} async-done(((bf16[512,256]{1,0:T(8,128)(2,1)}), bf16[512,8192]{1,0:T(8,128)(2,1)}) %all-gather.6.cloned.1.call-update) | async-done | bytes 8388624 | tf_op jit(solution)/shard_map/all_gather | solution.py:71
  233.5 8.9 %fusion.54 = f32[256,8192]{1,0:T(8,128)} fusion(bf16[256,512]{1,0:T(8,128)(2,1)S(1)} %fusion.4, bf16[512,8192]{1,0:T(8,128)(2,1)} %all-gather.6.cloned.1.call-done), kind=kOutput, calls=%fused_computation.65 | convolution fusion | flops 2147483648 | bytes 17039360 | tf_op jit(solution)/shard_map/dot_general | solution.py:69
  242.5 328.4 %all-reduce.1 = bf16[256,8192]{1,0:T(8,128)(2,1)} all-reduce(f32[256,8192]{1,0:T(8,128)} %fusion.54), channel_id=1, replica_groups=mesh['ctx'=32,'ch'=8] {'ch'}, use_global_device_ids=true, to_apply=%region_5.6 | all-reduce | flops 2097152 | bytes 12582912 | tf_op jit(solution)/shard_map/psum | solution.py:74
  570.9 1.9 dynamic-slice_convert_fusion
  (35 shorter events, 18.9 us)
Async XLA Ops:
  6.5 70.5 %all-gather.8.cloned.1.call-start = ((), (), s32[]{:S(2)}) async-start(), calls=%async_computation.1 | async-start | bytes 1081344 | tf_op jit(solution)/shard_map/all_gather | solution.py:11
  7.9 134.3 %all-gather.10.cloned.1.call-start = ((), (), s32[]{:S(2)}) async-start(), calls=%async_computation.2 | async-start | bytes 1081344 | tf_op jit(solution)/shard_map/all_gather | solution.py:11
  11.2 222.3 %all-gather.6.cloned.1.call-start = ((), (), s32[]{:S(2)}) async-start(), calls=%async_computation | async-start | bytes 8650752 | tf_op jit(solution)/shard_map/all_gather | solution.py:71
  168.2 12.8 %copy-start = (bf16[256,512]{1,0:T(8,128)(2,1)S(1)}, bf16[256,512]{1,0:T(8,128)(2,1)}, u32[]{:S(2)}) copy-start(bf16[256,512]{1,0:T(8,128)(2,1)} %param.8) | copy-start | bytes 786436
Sparse Core Ops, SparseCore 0:
  9.2 67.7 all-gather.7
  78.9 63.2 all-gather.9
  144.0 89.4 all-gather.5
where the time goes:
time: 582 us; the launch traced here: 579 us
  blocking collectives  328 us (56%)
  waiting for transfers between devices  181 us (31%)
  other arithmetic  34.1 us (6%)
  matrix products  20.1 us (3%)
  between operations  13.2 us (2%)
    psum x1, blocking collectives, shards(): summed = lax.psum(partial_value, 'ch')  328 us
    all_gather x2, waiting for transfers between devices, entering(): everything = jax.tree.map(lambda part: lax.all_gather(part, axis), value)  130 us
    all_gather x1, waiting for transfers between devices, shards(): lax.all_gather(out_weight, 'ctx', axis=1, tiled=True)  49.8 us
    select_n x32, other arithmetic, hop(): return jax.tree.map(lambda a, b: jnp.where(reached, a, b), new, before)  25.2 us
  transfers between devices with their start and end apart: 3, of which 3 were waited for; matrix products, arithmetic and copies ran while one was open for 8% of the time, Pallas kernels for 0%

commit v1 on v0

v1 whole, which is shorter than its diff:
```python
import jax
import jax.numpy as jnp
from jax import lax
from jax.experimental import pallas as pl
from jax.experimental.pallas import tpu as pltpu
from jax.sharding import Mesh
from jax.sharding import PartitionSpec as P

ROWS, CHANS, MODES = 256, 512, 16
SUB = 16
BLOCKS = ROWS // SUB
LANES = 128
TILES = CHANS // LANES
HALF = CHANS // 2
F32, BF16 = jnp.float32, jnp.bfloat16
VMEM_LIMIT = 48 * 1024 * 1024


def whole(n):
    return [pl.BlockSpec(memory_space=pltpu.VMEM)] * n


def call(body, outs, scratch, flops, moved, *args):
    return pl.pallas_call(
        body,
        out_shape=outs,
        in_specs=whole(len(args)),
        out_specs=whole(len(outs)) if isinstance(outs, (list, tuple)) else whole(1)[0],
        scratch_shapes=scratch,
        compiler_params=pltpu.CompilerParams(vmem_limit_bytes=VMEM_LIMIT),
        cost_estimate=pl.CostEstimate(flops=flops, bytes_accessed=moved, transcendentals=0),
    )(*args)


def signal_into(inner, values, sig):
    for lt in range(TILES):
        cols = slice(lt * LANES, (lt + 1) * LANES)
        product = inner[:, cols].astype(F32) * values[:, cols].astype(F32)
        sig[lt] = product.astype(BF16).astype(F32)


def sums_body(inner, values, decays, sums, keep, send, sig):
    signal_into(inner, values, sig)
    for lt in range(TILES):
        cols = slice(lt * LANES, (lt + 1) * LANES)
        fade = jnp.exp(-decays[:, cols])
        for group in range(0, MODES, 8):
            step = [jnp.broadcast_to(fade[r : r + 1], (BLOCKS, LANES)) for r in range(group, group + 8)]
            total = [sig[lt, pl.ds(0, BLOCKS, stride=SUB), :]] * 8
            for b in range(1, SUB):
                row = sig[lt, pl.ds(b, BLOCKS, stride=SUB), :]
                total = [t * e + row for t, e in zip(total, step)]
            for i in range(8):
                sums[lt, pl.ds(group + i, BLOCKS, stride=MODES), :] = total[i]
    core = lax.axis_index("core")
    for lt in range(TILES):
        cols = slice(lt * LANES, (lt + 1) * LANES)
        fade = jnp.exp(-decays[:, cols] * SUB)
        state = sums[lt, 0:MODES, :]
        for a in range(1, BLOCKS):
            state = state * fade + sums[lt, a * MODES : (a + 1) * MODES, :]
        place = slice((lt % 2) * LANES, (lt % 2 + 1) * LANES)

        @pl.when(core == lt // 2)
        def _():
            keep[:, place] = state

        @pl.when(core != lt // 2)
        def _():
            send[:, place] = state


def taps_body(inner, values, residues, decays, local, sig):
    signal_into(inner, values, sig)
    for lt in range(TILES):
        cols = slice(lt * LANES, (lt + 1) * LANES)
        fade = jnp.exp(-decays[:, cols])
        weight = residues[:, cols]
        taps = []
        for lag in range(SUB):
            taps.append(jnp.broadcast_to(jnp.sum(weight, axis=0, keepdims=True), (BLOCKS, LANES)))
            weight = weight * fade
        rows = [sig[lt, pl.ds(b, BLOCKS, stride=SUB), :] for b in range(SUB)]
        for b in range(SUB):
            total = taps[0] * rows[b]
            for lag in range(1, b + 1):
                total = total + taps[lag] * rows[b - lag]
            local[lt, pl.ds(b, BLOCKS, stride=SUB), :] = total


def gate_body(outer, sums, local, near, far, residues, decays, gated, states, out):
    core = lax.axis_index("core")
    for lt in range(TILES):
        cols = slice(lt * LANES, (lt + 1) * LANES)
        place = slice((lt % 2) * LANES, (lt % 2 + 1) * LANES)
        fade = jnp.exp(-decays[:, cols] * SUB)
        weight = residues[:, cols]
        state = jnp.where(core == lt // 2, near[:, place], far[:, place])
        for a in range(BLOCKS):
            states[lt, a * MODES : (a + 1) * MODES, :] = state * weight
            if a + 1 < BLOCKS:
                state = state * fade + sums[lt, a * MODES : (a + 1) * MODES, :]
    for lt in range(TILES):
        cols = slice(lt * LANES, (lt + 1) * LANES)
        fade = jnp.exp(-decays[:, cols])
        step = [jnp.broadcast_to(fade[r : r + 1], (BLOCKS, LANES)) for r in range(MODES)]
        part = [states[lt, pl.ds(r, BLOCKS, stride=MODES), :] for r in range(MODES)]
        for b in range(SUB):
            part = [t * e for t, e in zip(part, step)]
            total = part
            while len(total) > 1:
                total = [total[i] + total[i + 1] for i in range(0, len(total), 2)]
            out[lt, pl.ds(b, BLOCKS, stride=SUB), :] = total[0] + local[lt, pl.ds(b, BLOCKS, stride=SUB), :]
    for lt in range(TILES):
        cols = slice(lt * LANES, (lt + 1) * LANES)
        result = (outer[:, cols].astype(F32) * out[lt]).astype(BF16)
        for copy in range(gated.shape[0]):
            gated[copy, :, cols] = result


def project_body(places, *refs):
    own, other = refs[0], refs[1]
    blocks = refs[2 : 2 + len(places)]
    mine, theirs, acc = refs[2 + len(places) :]
    z, y = lax.axis_index("z"), lax.axis_index("ylo")
    acc[...] = jnp.zeros_like(acc)
    for block, (turn, shift) in zip(blocks, places):
        at = lax.rem(z + shift, 8)
        rank = lax.rem(y + turn, 2) * 4 + at // 2
        odd = lax.rem(at, 2)
        weight = block[...]
        acc[0, odd] += jnp.dot(own[rank], weight, preferred_element_type=F32)
        acc[1, odd] += jnp.dot(other[rank], weight, preferred_element_type=F32)
    mine[...] = acc[0].astype(BF16)
    theirs[...] = acc[1].astype(BF16)


def ring(size, shift):
    return [(i, (i + shift) % size) for i in range(size)]


def gather_weight(block):
    pairs = []
    for a in range(8):
        for b in range(4):
            for c in range(8):
                pairs.append(((a * 4 + b) * 8 + c, (c * 4 + b) * 8 + a))
    first = lax.ppermute(block, ("ylo", "z", "core", "x", "yhi"), pairs)
    second = lax.ppermute(first, "ylo", ring(2, 1))
    blocks, places = [first, second], [(0, 0), (1, 0)]
    up, down = [first, second], [first, second]
    for step in range(1, 5):
        for turn in range(2):
            up[turn] = lax.ppermute(up[turn], "z", ring(8, 1))
            blocks.append(up[turn])
            places.append((turn, 8 - step))
            if step < 4:
                down[turn] = lax.ppermute(down[turn], "z", ring(8, -1))
                blocks.append(down[turn])
                places.append((turn, step))
    return blocks, places


def shards(outer_gate, inner_gate, values, residues, decays, out_weight):
    blocks, places = gather_weight(out_weight)
    tiled = jax.ShapeDtypeStruct((TILES, ROWS, LANES), F32)
    half = jax.ShapeDtypeStruct((MODES, HALF), F32)
    tile_scratch = pltpu.VMEM((TILES, ROWS, LANES), F32)
    work = ROWS * CHANS * MODES * 2
    sums, keep, send = call(
        sums_body, [tiled, half, half], [tile_scratch], work, 1 << 20, inner_gate, values, decays
    )
    core, z, y = lax.axis_index("core"), lax.axis_index("z"), lax.axis_index("ylo")
    came = lax.ppermute(send, "core", ring(2, 1))
    mine = lax.dynamic_slice_in_dim(decays, core * HALF, HALF, 1)
    fade = jnp.exp(-mine * ROWS)
    first = jnp.where(core == 0, keep, came)
    chip = fade * first + jnp.where(core == 0, came, keep)
    everyone = lax.all_to_all(jnp.broadcast_to(chip[None], (16, MODES, HALF)), ("ylo", "z"), 0, 0)
    local = call(
        taps_body, tiled, [tile_scratch], ROWS * CHANS * SUB, 1 << 20, inner_gate, values, residues, decays
    )
    place = y * 8 + z
    chip_fade = fade * fade
    state = jnp.zeros_like(chip)
    for k in range(15):
        state = jnp.where(k < place, state * chip_fade + everyone[k], state)
    after = fade * state + first
    near = jnp.where(core == 0, state, after)
    far = lax.ppermute(jnp.where(core == 0, after, state), "core", ring(2, 1))
    copies = jax.ShapeDtypeStruct((8, ROWS, CHANS), BF16)
    gated = call(
        gate_body, copies, [tile_scratch, tile_scratch], work, 4 << 20,
        outer_gate, sums, local, near, far, residues, decays,
    )
    own = lax.all_to_all(gated, ("x", "yhi"), 0, 0)
    other = lax.ppermute(own, "core", ring(2, 1))
    part = jax.ShapeDtypeStruct((2, ROWS, 256), BF16)
    kept, sent = call(
        lambda *refs: project_body(places, *refs),
        [part, part],
        [pltpu.VMEM((2, 2, ROWS, 256), F32)],
        2 * 512 * 512 * 4096, 10 << 20,
        own, other, *blocks,
    )
    swapped = lax.ppermute(sent, "core", ring(2, 1))
    even = jnp.where(core == 0, kept, swapped)
    odd = jnp.where(core == 0, swapped, kept)
    return jnp.concatenate([even[0], odd[0], even[1], odd[1]], axis=1)


def solution(mesh):
    wide = Mesh(mesh.devices.reshape(2, 8, 2, 4, 2), ("ylo", "z", "core", "x", "yhi"))
    ctx, ch = ("ylo", "z", "core"), ("x", "yhi")
    return jax.shard_map(
        shards,
        mesh=wide,
        in_specs=(P(ctx, ch), P(ctx, ch), P(ctx, ch), P(None, ch), P(None, ch), P(ch, ctx)),
        out_specs=P(ctx, ch),
        check_vma=False,
    )
```

time: 582 us -> 149 us (0.26)
  blocking collectives: 328 us -> 33.1 us
  waiting for transfers between devices: 181 us -> 28.2 us
  starting transfers between devices: 0.09 us -> 67.7 us
  other arithmetic: 34.1 us -> 1.72 us
  matrix products: 20.1 us -> 0 us
  between operations: 13.2 us -> 0.17 us
  Pallas kernels: 0 us -> 7.69 us
  local copies, waits for them, and re-layouts: 1.87 us -> 8.18 us
    psum x1 -> x0, blocking collectives: 328 us -> none  [shards(): summed = lax.psum(partial_value, 'ch')]
    all_gather x3 -> x0, waiting for transfers between devices: 180 us -> none  [the longest x2 130 us: entering(): everything = jax.tree.map(lambda part: lax.all_gather(part, axis), value)]
    ppermute x0 -> x20, starting transfers between devices: none -> 60.1 us  [the longest x6 28.9 us: gather_weight(): down[turn] = lax.ppermute(down[turn], 'z', ring(8, -1))]
    all_to_all x0 -> x1, blocking collectives: none -> 33.1 us  [shards(): own = lax.all_to_all(gated, ('x', 'yhi'), 0, 0)]
    select_n x32 -> x3, other arithmetic: 25.2 us -> 0.13 us  [the longest x1 0.06 us: shards(): even = jnp.where(core == 0, kept, swapped)]
    ppermute x0 -> x20, waiting for transfers between devices: none -> 23.3 us  [the longest x8 18 us: gather_weight(): up[turn] = lax.ppermute(up[turn], 'z', ring(8, 1))]
    dot_general x5 -> x0, matrix products: 20.1 us -> none  [the longest x1 8.94 us: shards(): jnp.dot(gated, lax.all_gather(out_weight, 'ctx', axis=1, tiled=True), pre...]
    pallas_call x0 -> x4, Pallas kernels: none -> 7.69 us  [call(): pl.pallas_call(body, out_shape=outs, in_specs=whole(len(args)), out_specs...]
  transfers between devices with their start and end apart: 3 -> 21, of which waited for: 3 -> 12; matrix products, arithmetic and copies ran while one was open for 8% -> 0% of each run, Pallas kernels for 0% -> 0%
where the time goes in v1:
time: 149 us; the launch traced here: 147 us
  starting transfers between devices  67.7 us (45%)
  blocking collectives  33.1 us (22%)
  waiting for transfers between devices  28.2 us (19%)
  local copies, waits for them, and re-layouts  8.18 us (5%)
  Pallas kernels  7.69 us (5%)
  other arithmetic  1.72 us (1%)
    all_to_all x1, blocking collectives, shards(): own = lax.all_to_all(gated, ('x', 'yhi'), 0, 0)  33.1 us
    ppermute x6, starting transfers between devices, gather_weight(): down[turn] = lax.ppermute(down[turn], 'z', ring(8, -1))  28.9 us
    ppermute x8, waiting for transfers between devices, gather_weight(): up[turn] = lax.ppermute(up[turn], 'z', ring(8, 1))  18 us
    ppermute x1, starting transfers between devices, gather_weight(): second = lax.ppermute(first, 'ylo', ring(2, 1))  13.3 us
    pallas_call x4, Pallas kernels, call(): pl.pallas_call(body, out_shape=outs, in_specs=whole(len(args)), out_specs...  7.69 us
    all_to_all x1, starting transfers between devices, shards(): lax.all_to_all(jnp.broadcast_to(chip[None], (16, MODES, HALF)), ('ylo', '...  7.57 us
    unnamed x26, local copies, waits for them, and re-layouts  7.41 us
    ppermute x8, starting transfers between devices, gather_weight(): up[turn] = lax.ppermute(up[turn], 'z', ring(8, 1))  6.62 us
  transfers between devices with their start and end apart: 21, of which 12 were waited for; matrix products, arithmetic and copies ran while one was open for 0% of the time, Pallas kernels for 0%

profile of v1, /device:TPU:1, one launch (start us, length us, event | category | flops | bytes accessed | tf_op | source)
XLA Modules:
  0.0 146.8 jit_solution(9465998664584221949)
XLA Ops:
  3.7 3.3 %collective-permute-start = (f32[16,256]{1,0:T(8,128)S(1)}, f32[16,256]{1,0:T(8,128)S(1)}, u32[]{:S(2)}, u32[]{:S(2)}) collective-permute-start(f32[16,256]{1,0:T(8,128)S(1)} %get-tuple-element.12), channel_id=1, source_target_pairs={{0,8},{8,0},{1,9},{9,1},{2,10},{10,2},{3,11},{11,3},{4,12},{12,4},... | collective-permute-start | bytes 49160 | tf_op jit(solution)/shard_map/ppermute | solution.py:174
  9.4 7.6 %all-to-all-start = ((f32[16,16,256]{2,1,0:T(8,128)}), f32[16,16,256]{2,1,0:T(8,128)S(1)}, u32[]{:S(2)}, u32[]{:S(2)}) async-start(f32[16,16,256]{2,1,0:T(8,128)} %broadcast_in_dim.10), calls=%async_computation | async-start | bytes 524288 | tf_op jit(solution)/shard_map/all_to_all | solution.py:179
  21.0 4.9 %all-to-all-done = f32[16,16,256]{2,1,0:T(8,128)S(1)} async-done(((f32[16,16,256]{2,1,0:T(8,128)}), f32[16,16,256]{2,1,0:T(8,128)S(1)}, u32[]{:S(2)}, u32[]{:S(2)}) %all-to-all-start) | async-done | bytes 262176 | tf_op jit(solution)/shard_map/all_to_all | solution.py:179
  26.0 2.2 %collective-permute-start.1 = (f32[16,256]{1,0:T(8,128)S(1)}, f32[16,256]{1,0:T(8,128)S(1)}, u32[]{:S(2)}, u32[]{:S(2)}) collective-permute-start(f32[16,256]{1,0:T(8,128)S(1)} %get-tuple-element.15), channel_id=1, source_target_pairs={{0,8},{8,0},{1,9},{9,1},{2,10},{10,2},{3,11},{11,3},{4,12},{12,4},... | collective-permute-start | bytes 49160 | tf_op jit(solution)/shard_map/ppermute | solution.py:190
  29.1 1.3 shard_map.66
  30.4 33.1 %all_to_all.10.refs_0_ = bf16[8,256,512]{2,1,0:T(8,128)(2,1)S(1)} all-to-all(bf16[8,256,512]{2,1,0:T(8,128)(2,1)S(1)} %shard_map.66), channel_id=1, replica_groups=mesh['ylo'=2,'z'=8,'core'=2,'x'=4,'yhi'=2] {'x','yhi'}, dimensions={0} | all-to-all | bytes 4194304 | tf_op jit(solution)/shard_map/all_to_all | solution.py:196
  63.6 2.2 %collective-permute-start.2 = (bf16[8,256,512]{2,1,0:T(8,128)(2,1)S(1)}, bf16[8,256,512]{2,1,0:T(8,128)(2,1)S(1)}, u32[]{:S(2)}, u32[]{:S(2)}) collective-permute-start(bf16[8,256,512]{2,1,0:T(8,128)(2,1)S(1)} %all_to_all.10.refs_0_), channel_id=1, source_target_pairs={{0,8},{8,0},{1,9},{9,1},{2,10},{10,2},{3,11},{11,3},{4,12},{12,4},... | collective-permute-start | bytes 6291464 | tf_op jit(solution)/shard_map/ppermute | solution.py:197
  66.4 13.3 %collective-permute-start.4 = (bf16[512,256]{1,0:T(8,128)(2,1)S(1)}, bf16[512,256]{1,0:T(8,128)(2,1)S(1)}, u32[]{:S(2)}, u32[]{:S(2)}) collective-permute-start(bf16[512,256]{1,0:T(8,128)(2,1)S(1)} %collective-permute-done.3.refs_2_), channel_id=1, source_target_pairs={{0,128},{128,0},{1,129},{129,1},{2,130},{130,2},{3,131},{131,3},{4... | collective-permute-start | bytes 786440 | tf_op jit(solution)/shard_map/ppermute | solution.py:149
  79.8 3.1 %collective-permute-start.5 = (bf16[512,256]{1,0:T(8,128)(2,1)S(1)}, bf16[512,256]{1,0:T(8,128)(2,1)S(1)}, u32[]{:S(2)}, u32[]{:S(2)}) collective-permute-start(bf16[512,256]{1,0:T(8,128)(2,1)S(1)} %collective-permute-done.3.refs_2_), channel_id=1, source_target_pairs={{0,16},{16,32},{32,48},{48,64},{64,80},{80,96},{96,112},{112,0},{1... | collective-permute-start | bytes 786440 | tf_op jit(solution)/shard_map/ppermute | solution.py:154
  82.9 2.5 %collective-permute-done.4.refs_3_ = bf16[512,256]{1,0:T(8,128)(2,1)S(1)} collective-permute-done((bf16[512,256]{1,0:T(8,128)(2,1)S(1)}, bf16[512,256]{1,0:T(8,128)(2,1)S(1)}, u32[]{:S(2)}, u32[]{:S(2)}) %collective-permute-start.4) | collective-permute-done | bytes 262176 | tf_op jit(solution)/shard_map/ppermute | solution.py:149
  85.4 3.5 %collective-permute-start.7 = (bf16[512,256]{1,0:T(8,128)(2,1)S(1)}, bf16[512,256]{1,0:T(8,128)(2,1)S(1)}, u32[]{:S(2)}, u32[]{:S(2)}) collective-permute-start(bf16[512,256]{1,0:T(8,128)(2,1)S(1)} %collective-permute-done.4.refs_3_), channel_id=1, source_target_pairs={{0,16},{16,32},{32,48},{48,64},{64,80},{80,96},{96,112},{112,0},{1... | collective-permute-start | bytes 786440 | tf_op jit(solution)/shard_map/ppermute | solution.py:154
  88.9 8.7 %collective-permute-start.6 = (bf16[512,256]{1,0:T(8,128)(2,1)S(1)}, bf16[512,256]{1,0:T(8,128)(2,1)S(1)}, u32[]{:S(2)}, u32[]{:S(2)}) collective-permute-start(bf16[512,256]{1,0:T(8,128)(2,1)S(1)} %collective-permute-done.3.refs_2_), channel_id=1, source_target_pairs={{0,112},{16,0},{32,16},{48,32},{64,48},{80,64},{96,80},{112,96},{1... | collective-permute-start | bytes 786440 | tf_op jit(solution)/shard_map/ppermute | solution.py:158
  97.6 4.0 %collective-permute-start.8 = (bf16[512,256]{1,0:T(8,128)(2,1)S(1)}, bf16[512,256]{1,0:T(8,128)(2,1)S(1)}, u32[]{:S(2)}, u32[]{:S(2)}) collective-permute-start(bf16[512,256]{1,0:T(8,128)(2,1)S(1)} %collective-permute-done.4.refs_3_), channel_id=1, source_target_pairs={{0,112},{16,0},{32,16},{48,32},{64,48},{80,64},{96,80},{112,96},{1... | collective-permute-start | bytes 786440 | tf_op jit(solution)/shard_map/ppermute | solution.py:158
  102.5 3.9 %collective-permute-start.10 = (bf16[512,256]{1,0:T(8,128)(2,1)S(1)}, bf16[512,256]{1,0:T(8,128)(2,1)S(1)}, u32[]{:S(2)}, u32[]{:S(2)}) collective-permute-start(bf16[512,256]{1,0:T(8,128)(2,1)S(1)} %collective-permute-done.6.refs_5_), channel_id=1, source_target_pairs={{0,112},{16,0},{32,16},{48,32},{64,48},{80,64},{96,80},{112,96},{1... | collective-permute-start | bytes 786440 | tf_op jit(solution)/shard_map/ppermute | solution.py:158
  106.5 2.1 %collective-permute-done.9.refs_8_ = bf16[512,256]{1,0:T(8,128)(2,1)S(1)} collective-permute-done((bf16[512,256]{1,0:T(8,128)(2,1)S(1)}, bf16[512,256]{1,0:T(8,128)(2,1)S(1)}, u32[]{:S(2)}, u32[]{:S(2)}) %collective-permute-start.9) | collective-permute-done | bytes 262176 | tf_op jit(solution)/shard_map/ppermute | solution.py:154
  108.6 3.5 %collective-permute-start.12 = (bf16[512,256]{1,0:T(8,128)(2,1)S(1)}, bf16[512,256]{1,0:T(8,128)(2,1)S(1)}, u32[]{:S(2)}, u32[]{:S(2)}) collective-permute-start(bf16[512,256]{1,0:T(8,128)(2,1)S(1)} %collective-permute-done.8.refs_7_), channel_id=1, source_target_pairs={{0,112},{16,0},{32,16},{48,32},{64,48},{80,64},{96,80},{112,96},{1... | collective-permute-start | bytes 786440 | tf_op jit(solution)/shard_map/ppermute | solution.py:158
  113.3 4.3 %collective-permute-start.14 = (bf16[512,256]{1,0:T(8,128)(2,1)S(1)}, bf16[512,256]{1,0:T(8,128)(2,1)S(1)}, u32[]{:S(2)}, u32[]{:S(2)}) collective-permute-start(bf16[512,256]{1,0:T(8,128)(2,1)S(1)} %collective-permute-done.10.refs_9_), channel_id=1, source_target_pairs={{0,112},{16,0},{32,16},{48,32},{64,48},{80,64},{96,80},{112,96},{1... | collective-permute-start | bytes 786440 | tf_op jit(solution)/shard_map/ppermute | solution.py:158
  119.0 4.3 %collective-permute-start.16 = (bf16[512,256]{1,0:T(8,128)(2,1)S(1)}, bf16[512,256]{1,0:T(8,128)(2,1)S(1)}, u32[]{:S(2)}, u32[]{:S(2)}) collective-permute-start(bf16[512,256]{1,0:T(8,128)(2,1)S(1)} %collective-permute-done.12.refs_11_), channel_id=1, source_target_pairs={{0,112},{16,0},{32,16},{48,32},{64,48},{80,64},{96,80},{112,96},{1... | collective-permute-start | bytes 786440 | tf_op jit(solution)/shard_map/ppermute | solution.py:158
  123.3 1.3 collective-permute-done.15.refs_14_
  124.6 5.6 %collective-permute-done.17.refs_16_ = bf16[512,256]{1,0:T(8,128)(2,1)S(1)} collective-permute-done((bf16[512,256]{1,0:T(8,128)(2,1)S(1)}, bf16[512,256]{1,0:T(8,128)(2,1)S(1)}, u32[]{:S(2)}, u32[]{:S(2)}) %collective-permute-start.17) | collective-permute-done | bytes 262176 | tf_op jit(solution)/shard_map/ppermute | solution.py:154
  130.2 5.6 %collective-permute-done.18.refs_17_ = bf16[512,256]{1,0:T(8,128)(2,1)S(1)} collective-permute-done((bf16[512,256]{1,0:T(8,128)(2,1)S(1)}, bf16[512,256]{1,0:T(8,128)(2,1)S(1)}, u32[]{:S(2)}, u32[]{:S(2)}) %collective-permute-start.18) | collective-permute-done | bytes 262176 | tf_op jit(solution)/shard_map/ppermute | solution.py:154
  135.8 1.3 copy-done.11
  137.1 4.7 %shard_map.67 = (bf16[2,256,256]{2,1,0:T(8,128)(2,1)S(1)}, bf16[2,256,256]{2,1,0:T(8,128)(2,1)S(1)}) custom-call(bf16[8,256,512]{2,1,0:T(8,128)(2,1)} %copy-done.10, bf16[8,256,512]{2,1,0:T(8,128)(2,1)} %copy-done.11, bf16[512,256]{1,0:T(8,128)(2,1)S(1)} %collective-permute-done.3.refs_2_, bf16[512,256]{1,0:T(8,128)(2,1)S(1)} %collective-permute-done.4.refs_3_, ...), custom_call_target="tpu_custom_call" | custom-call | flops 2147483648 | bytes 10485760 | tf_op jit(solution)/shard_map/pallas_call | solution.py:24
  141.9 2.8 %collective-permute-start.19 = (bf16[2,256,256]{2,1,0:T(8,128)(2,1)S(1)}, bf16[2,256,256]{2,1,0:T(8,128)(2,1)S(1)}, u32[]{:S(2)}, u32[]{:S(2)}) collective-permute-start(bf16[2,256,256]{2,1,0:T(8,128)(2,1)S(1)} %get-tuple-element.14), channel_id=1, source_target_pairs={{0,8},{8,0},{1,9},{9,1},{2,10},{10,2},{3,11},{11,3},{4,12},{12,4},... | collective-permute-start | bytes 786440 | tf_op jit(solution)/shard_map/ppermute | solution.py:206
  (56 shorter events, 17.1 us)
Async XLA Ops:
  2.7 26.4 %copy-start.9 = (f32[16,512]{1,0:T(8,128)S(1)}, f32[16,512]{1,0:T(8,128)}, u32[]{:S(2)}) copy-start(f32[16,512]{1,0:T(8,128)} %residues.3) | copy-start | bytes 98308
  3.7 4.2 %collective-permute-start = (f32[16,256]{1,0:T(8,128)S(1)}, f32[16,256]{1,0:T(8,128)S(1)}, u32[]{:S(2)}, u32[]{:S(2)}) collective-permute-start(f32[16,256]{1,0:T(8,128)S(1)} %get-tuple-element.12), channel_id=1, source_target_pairs={{0,8},{8,0},{1,9},{9,1},{2,10},{10,2},{3,11},{11,3},{4,12},{12,4},... | collective-permute-start | bytes 49160 | tf_op jit(solution)/shard_map/ppermute | solution.py:174
  9.4 16.5 %all-to-all-start = ((f32[16,16,256]{2,1,0:T(8,128)}), f32[16,16,256]{2,1,0:T(8,128)S(1)}, u32[]{:S(2)}, u32[]{:S(2)}) async-start(f32[16,16,256]{2,1,0:T(8,128)} %broadcast_in_dim.10), calls=%async_computation | async-start | bytes 524288 | tf_op jit(solution)/shard_map/all_to_all | solution.py:179
  26.0 3.1 %collective-permute-start.1 = (f32[16,256]{1,0:T(8,128)S(1)}, f32[16,256]{1,0:T(8,128)S(1)}, u32[]{:S(2)}, u32[]{:S(2)}) collective-permute-start(f32[16,256]{1,0:T(8,128)S(1)} %get-tuple-element.15), channel_id=1, source_target_pairs={{0,8},{8,0},{1,9},{9,1},{2,10},{10,2},{3,11},{11,3},{4,12},{12,4},... | collective-permute-start | bytes 49160 | tf_op jit(solution)/shard_map/ppermute | solution.py:190
  30.4 35.3 %copy-start.12 = (bf16[512,256]{1,0:T(8,128)(2,1)S(1)}, bf16[512,256]{1,0:T(8,128)(2,1)}, u32[]{:S(2)}) copy-start(bf16[512,256]{1,0:T(8,128)(2,1)} %param.11) | copy-start | bytes 786436
  63.6 72.3 %copy-start.10 = (bf16[8,256,512]{2,1,0:T(8,128)(2,1)}, bf16[8,256,512]{2,1,0:T(8,128)(2,1)S(1)}, u32[]{:S(2)}) copy-start(bf16[8,256,512]{2,1,0:T(8,128)(2,1)S(1)} %all_to_all.10.refs_0_) | copy-start | bytes 6291460
  63.6 72.2 %collective-permute-start.2 = (bf16[8,256,512]{2,1,0:T(8,128)(2,1)S(1)}, bf16[8,256,512]{2,1,0:T(8,128)(2,1)S(1)}, u32[]{:S(2)}, u32[]{:S(2)}) collective-permute-start(bf16[8,256,512]{2,1,0:T(8,128)(2,1)S(1)} %all_to_all.10.refs_0_), channel_id=1, source_target_pairs={{0,8},{8,0},{1,9},{9,1},{2,10},{10,2},{3,11},{11,3},{4,12},{12,4},... | collective-permute-start | bytes 6291464 | tf_op jit(solution)/shard_map/ppermute | solution.py:197
  65.8 0.7 collective-permute-start.3
  66.4 18.9 %collective-permute-start.4 = (bf16[512,256]{1,0:T(8,128)(2,1)S(1)}, bf16[512,256]{1,0:T(8,128)(2,1)S(1)}, u32[]{:S(2)}, u32[]{:S(2)}) collective-permute-start(bf16[512,256]{1,0:T(8,128)(2,1)S(1)} %collective-permute-done.3.refs_2_), channel_id=1, source_target_pairs={{0,128},{128,0},{1,129},{129,1},{2,130},{130,2},{3,131},{131,3},{4... | collective-permute-start | bytes 786440 | tf_op jit(solution)/shard_map/ppermute | solution.py:149
  79.8 17.8 %collective-permute-start.5 = (bf16[512,256]{1,0:T(8,128)(2,1)S(1)}, bf16[512,256]{1,0:T(8,128)(2,1)S(1)}, u32[]{:S(2)}, u32[]{:S(2)}) collective-permute-start(bf16[512,256]{1,0:T(8,128)(2,1)S(1)} %collective-permute-done.3.refs_2_), channel_id=1, source_target_pairs={{0,16},{16,32},{32,48},{48,64},{64,80},{80,96},{96,112},{112,0},{1... | collective-permute-start | bytes 786440 | tf_op jit(solution)/shard_map/ppermute | solution.py:154
  85.4 17.2 %collective-permute-start.7 = (bf16[512,256]{1,0:T(8,128)(2,1)S(1)}, bf16[512,256]{1,0:T(8,128)(2,1)S(1)}, u32[]{:S(2)}, u32[]{:S(2)}) collective-permute-start(bf16[512,256]{1,0:T(8,128)(2,1)S(1)} %collective-permute-done.4.refs_3_), channel_id=1, source_target_pairs={{0,16},{16,32},{32,48},{48,64},{64,80},{80,96},{96,112},{112,0},{1... | collective-permute-start | bytes 786440 | tf_op jit(solution)/shard_map/ppermute | solution.py:154
  88.9 13.7 %collective-permute-start.6 = (bf16[512,256]{1,0:T(8,128)(2,1)S(1)}, bf16[512,256]{1,0:T(8,128)(2,1)S(1)}, u32[]{:S(2)}, u32[]{:S(2)}) collective-permute-start(bf16[512,256]{1,0:T(8,128)(2,1)S(1)} %collective-permute-done.3.refs_2_), channel_id=1, source_target_pairs={{0,112},{16,0},{32,16},{48,32},{64,48},{80,64},{96,80},{112,96},{1... | collective-permute-start | bytes 786440 | tf_op jit(solution)/shard_map/ppermute | solution.py:158
  97.6 11.0 %collective-permute-start.9 = (bf16[512,256]{1,0:T(8,128)(2,1)S(1)}, bf16[512,256]{1,0:T(8,128)(2,1)S(1)}, u32[]{:S(2)}, u32[]{:S(2)}) collective-permute-start(bf16[512,256]{1,0:T(8,128)(2,1)S(1)} %collective-permute-done.5.refs_4_), channel_id=1, source_target_pairs={{0,16},{16,32},{32,48},{48,64},{64,80},{80,96},{96,112},{112,0},{1... | collective-permute-start | bytes 786440 | tf_op jit(solution)/shard_map/ppermute | solution.py:154
  97.6 11.0 %collective-permute-start.8 = (bf16[512,256]{1,0:T(8,128)(2,1)S(1)}, bf16[512,256]{1,0:T(8,128)(2,1)S(1)}, u32[]{:S(2)}, u32[]{:S(2)}) collective-permute-start(bf16[512,256]{1,0:T(8,128)(2,1)S(1)} %collective-permute-done.4.refs_3_), channel_id=1, source_target_pairs={{0,112},{16,0},{32,16},{48,32},{64,48},{80,64},{96,80},{112,96},{1... | collective-permute-start | bytes 786440 | tf_op jit(solution)/shard_map/ppermute | solution.py:158
  102.5 10.8 %collective-permute-start.11 = (bf16[512,256]{1,0:T(8,128)(2,1)S(1)}, bf16[512,256]{1,0:T(8,128)(2,1)S(1)}, u32[]{:S(2)}, u32[]{:S(2)}) collective-permute-start(bf16[512,256]{1,0:T(8,128)(2,1)S(1)} %collective-permute-done.7.refs_6_), channel_id=1, source_target_pairs={{0,16},{16,32},{32,48},{48,64},{64,80},{80,96},{96,112},{112,0},{1... | collective-permute-start | bytes 786440 | tf_op jit(solution)/shard_map/ppermute | solution.py:154
  102.5 10.8 %collective-permute-start.10 = (bf16[512,256]{1,0:T(8,128)(2,1)S(1)}, bf16[512,256]{1,0:T(8,128)(2,1)S(1)}, u32[]{:S(2)}, u32[]{:S(2)}) collective-permute-start(bf16[512,256]{1,0:T(8,128)(2,1)S(1)} %collective-permute-done.6.refs_5_), channel_id=1, source_target_pairs={{0,112},{16,0},{32,16},{48,32},{64,48},{80,64},{96,80},{112,96},{1... | collective-permute-start | bytes 786440 | tf_op jit(solution)/shard_map/ppermute | solution.py:158
  108.6 10.4 %collective-permute-start.13 = (bf16[512,256]{1,0:T(8,128)(2,1)S(1)}, bf16[512,256]{1,0:T(8,128)(2,1)S(1)}, u32[]{:S(2)}, u32[]{:S(2)}) collective-permute-start(bf16[512,256]{1,0:T(8,128)(2,1)S(1)} %collective-permute-done.9.refs_8_), channel_id=1, source_target_pairs={{0,16},{16,32},{32,48},{48,64},{64,80},{80,96},{96,112},{112,0},{1... | collective-permute-start | bytes 786440 | tf_op jit(solution)/shard_map/ppermute | solution.py:154
  108.6 10.4 %collective-permute-start.12 = (bf16[512,256]{1,0:T(8,128)(2,1)S(1)}, bf16[512,256]{1,0:T(8,128)(2,1)S(1)}, u32[]{:S(2)}, u32[]{:S(2)}) collective-permute-start(bf16[512,256]{1,0:T(8,128)(2,1)S(1)} %collective-permute-done.8.refs_7_), channel_id=1, source_target_pairs={{0,112},{16,0},{32,16},{48,32},{64,48},{80,64},{96,80},{112,96},{1... | collective-permute-start | bytes 786440 | tf_op jit(solution)/shard_map/ppermute | solution.py:158
  113.3 11.2 %collective-permute-start.15 = (bf16[512,256]{1,0:T(8,128)(2,1)S(1)}, bf16[512,256]{1,0:T(8,128)(2,1)S(1)}, u32[]{:S(2)}, u32[]{:S(2)}) collective-permute-start(bf16[512,256]{1,0:T(8,128)(2,1)S(1)} %collective-permute-done.11.refs_10_), channel_id=1, source_target_pairs={{0,16},{16,32},{32,48},{48,64},{64,80},{80,96},{96,112},{112,0},{1... | collective-permute-start | bytes 786440 | tf_op jit(solution)/shard_map/ppermute | solution.py:154
  113.3 11.2 %collective-permute-start.14 = (bf16[512,256]{1,0:T(8,128)(2,1)S(1)}, bf16[512,256]{1,0:T(8,128)(2,1)S(1)}, u32[]{:S(2)}, u32[]{:S(2)}) collective-permute-start(bf16[512,256]{1,0:T(8,128)(2,1)S(1)} %collective-permute-done.10.refs_9_), channel_id=1, source_target_pairs={{0,112},{16,0},{32,16},{48,32},{64,48},{80,64},{96,80},{112,96},{1... | collective-permute-start | bytes 786440 | tf_op jit(solution)/shard_map/ppermute | solution.py:158
  119.0 11.2 %collective-permute-start.17 = (bf16[512,256]{1,0:T(8,128)(2,1)S(1)}, bf16[512,256]{1,0:T(8,128)(2,1)S(1)}, u32[]{:S(2)}, u32[]{:S(2)}) collective-permute-start(bf16[512,256]{1,0:T(8,128)(2,1)S(1)} %collective-permute-done.13.refs_12_), channel_id=1, source_target_pairs={{0,16},{16,32},{32,48},{48,64},{64,80},{80,96},{96,112},{112,0},{1... | collective-permute-start | bytes 786440 | tf_op jit(solution)/shard_map/ppermute | solution.py:154
  119.0 11.2 %collective-permute-start.16 = (bf16[512,256]{1,0:T(8,128)(2,1)S(1)}, bf16[512,256]{1,0:T(8,128)(2,1)S(1)}, u32[]{:S(2)}, u32[]{:S(2)}) collective-permute-start(bf16[512,256]{1,0:T(8,128)(2,1)S(1)} %collective-permute-done.12.refs_11_), channel_id=1, source_target_pairs={{0,112},{16,0},{32,16},{48,32},{64,48},{80,64},{96,80},{112,96},{1... | collective-permute-start | bytes 786440 | tf_op jit(solution)/shard_map/ppermute | solution.py:158
  124.6 11.2 %collective-permute-start.18 = (bf16[512,256]{1,0:T(8,128)(2,1)S(1)}, bf16[512,256]{1,0:T(8,128)(2,1)S(1)}, u32[]{:S(2)}, u32[]{:S(2)}) collective-permute-start(bf16[512,256]{1,0:T(8,128)(2,1)S(1)} %collective-permute-done.15.refs_14_), channel_id=1, source_target_pairs={{0,16},{16,32},{32,48},{48,64},{64,80},{80,96},{96,112},{112,0},{1... | collective-permute-start | bytes 786440 | tf_op jit(solution)/shard_map/ppermute | solution.py:154
  141.9 4.0 %collective-permute-start.19 = (bf16[2,256,256]{2,1,0:T(8,128)(2,1)S(1)}, bf16[2,256,256]{2,1,0:T(8,128)(2,1)S(1)}, u32[]{:S(2)}, u32[]{:S(2)}) collective-permute-start(bf16[2,256,256]{2,1,0:T(8,128)(2,1)S(1)} %get-tuple-element.14), channel_id=1, source_target_pairs={{0,8},{8,0},{1,9},{9,1},{2,10},{10,2},{3,11},{11,3},{4,12},{12,4},... | collective-permute-start | bytes 786440 | tf_op jit(solution)/shard_map/ppermute | solution.py:206
  (10 other events, 57.1 us)

commit v2 on v1

--- a/solution.py
+++ b/solution.py
@@ -118,19 +118,31 @@
             gated[copy, :, cols] = result
 
 
-def project_body(places, *refs):
-    own, other = refs[0], refs[1]
-    blocks = refs[2 : 2 + len(places)]
-    mine, theirs, acc = refs[2 + len(places) :]
-    z, y = lax.axis_index("z"), lax.axis_index("ylo")
+def project_body(places, ranks, *refs):
+    pieces = refs[: len(ranks)]
+    blocks = refs[len(ranks) : len(ranks) + len(places)]
+    mine, theirs, gated, weight, acc, piece_sem, block_sem = refs[len(ranks) + len(places) :]
+    x, yhi = lax.axis_index("x"), lax.axis_index("yhi")
+    z, ylo = lax.axis_index("z"), lax.axis_index("ylo")
+    loads = []
+    for i, (piece, (rows, dx, dy)) in enumerate(zip(pieces, ranks)):
+        rank = lax.rem(x + dx, 4) * 2 + lax.rem(yhi + dy, 2)
+        loads.append(pltpu.make_async_copy(piece, gated.at[rows, rank], piece_sem.at[i]))
+    stores = [
+        pltpu.make_async_copy(block, weight.at[i], block_sem.at[i]) for i, block in enumerate(blocks)
+    ]
+    for copy in loads + stores:
+        copy.start()
     acc[...] = jnp.zeros_like(acc)
-    for block, (turn, shift) in zip(blocks, places):
+    for copy in loads:
+        copy.wait()
+    for i, (turn, shift) in enumerate(places):
         at = lax.rem(z + shift, 8)
-        rank = lax.rem(y + turn, 2) * 4 + at // 2
+        rank = lax.rem(ylo + turn, 2) * 4 + at // 2
         odd = lax.rem(at, 2)
-        weight = block[...]
-        acc[0, odd] += jnp.dot(own[rank], weight, preferred_element_type=F32)
-        acc[1, odd] += jnp.dot(other[rank], weight, preferred_element_type=F32)
+        stores[i].wait()
+        for rows in range(2):
+            acc[rows, odd] += jnp.dot(gated[rows, rank], weight[i], preferred_element_type=F32)
     mine[...] = acc[0].astype(BF16)
     theirs[...] = acc[1].astype(BF16)
 
@@ -139,30 +151,25 @@
     return [(i, (i + shift) % size) for i in range(size)]
 
 
-def gather_weight(block):
+def swap(block):
     pairs = []
     for a in range(8):
         for b in range(4):
             for c in range(8):
                 pairs.append(((a * 4 + b) * 8 + c, (c * 4 + b) * 8 + a))
-    first = lax.ppermute(block, ("ylo", "z", "core", "x", "yhi"), pairs)
-    second = lax.ppermute(first, "ylo", ring(2, 1))
-    blocks, places = [first, second], [(0, 0), (1, 0)]
-    up, down = [first, second], [first, second]
-    for step in range(1, 5):
-        for turn in range(2):
-            up[turn] = lax.ppermute(up[turn], "z", ring(8, 1))
-            blocks.append(up[turn])
-            places.append((turn, 8 - step))
-            if step < 4:
-                down[turn] = lax.ppermute(down[turn], "z", ring(8, -1))
-                blocks.append(down[turn])
-                places.append((turn, step))
-    return blocks, places
+    return lax.ppermute(block, ("ylo", "z", "core", "x", "yhi"), pairs)
+
+
+def move(value, axis, shift):
+    return lax.ppermute(value, axis, ring({"ylo": 2, "z": 8, "core": 2, "x": 4, "yhi": 2}[axis], shift))
+
+
+def together(*values):
+    return lax.optimization_barrier(values)
 
 
 def shards(outer_gate, inner_gate, values, residues, decays, out_weight):
-    blocks, places = gather_weight(out_weight)
+    first = swap(out_weight)
     tiled = jax.ShapeDtypeStruct((TILES, ROWS, LANES), F32)
     half = jax.ShapeDtypeStruct((MODES, HALF), F32)
     tile_scratch = pltpu.VMEM((TILES, ROWS, LANES), F32)
@@ -171,39 +178,90 @@
         sums_body, [tiled, half, half], [tile_scratch], work, 1 << 20, inner_gate, values, decays
     )
     core, z, y = lax.axis_index("core"), lax.axis_index("z"), lax.axis_index("ylo")
-    came = lax.ppermute(send, "core", ring(2, 1))
+    came = move(send, "core", 1)
     mine = lax.dynamic_slice_in_dim(decays, core * HALF, HALF, 1)
     fade = jnp.exp(-mine * ROWS)
-    first = jnp.where(core == 0, keep, came)
-    chip = fade * first + jnp.where(core == 0, came, keep)
+    before = jnp.where(core == 0, keep, came)
+    chip = fade * before + jnp.where(core == 0, came, keep)
     everyone = lax.all_to_all(jnp.broadcast_to(chip[None], (16, MODES, HALF)), ("ylo", "z"), 0, 0)
     local = call(
         taps_body, tiled, [tile_scratch], ROWS * CHANS * SUB, 1 << 20, inner_gate, values, residues, decays
     )
+    everyone, local, first = together(everyone, local, first)
+
+    second, up_a, down_a = move(first, "ylo", 1), move(first, "z", 1), move(first, "z", -1)
     place = y * 8 + z
     chip_fade = fade * fade
     state = jnp.zeros_like(chip)
     for k in range(15):
         state = jnp.where(k < place, state * chip_fade + everyone[k], state)
-    after = fade * state + first
+    after = fade * state + before
     near = jnp.where(core == 0, state, after)
-    far = lax.ppermute(jnp.where(core == 0, after, state), "core", ring(2, 1))
-    copies = jax.ShapeDtypeStruct((8, ROWS, CHANS), BF16)
+    far = move(jnp.where(core == 0, after, state), "core", 1)
     gated = call(
-        gate_body, copies, [tile_scratch, tile_scratch], work, 4 << 20,
+        gate_body, jax.ShapeDtypeStruct((1, ROWS, CHANS), BF16), [tile_scratch, tile_scratch], work, 2 << 20,
         outer_gate, sums, local, near, far, residues, decays,
     )
-    own = lax.all_to_all(gated, ("x", "yhi"), 0, 0)
-    other = lax.ppermute(own, "core", ring(2, 1))
+    blocks, places = [first, second, up_a, down_a], [(0, 0), (1, 0), (0, 7), (0, 1)]
+
+    def arrived(*new):
+        for block, at in new:
+            blocks.append(block)
+            places.append(at)
+
+    gated, second, up_a, down_a = together(gated, second, up_a, down_a)
+    side = move(gated, "yhi", 1)
+    up_a, down_a = move(up_a, "z", 1), move(down_a, "z", -1)
+    up_b, down_b = move(second, "z", 1), move(second, "z", -1)
+    arrived((up_a, (0, 6)), (down_a, (0, 2)), (up_b, (1, 7)), (down_b, (1, 1)))
+
+    side, up_a, down_a, up_b, down_b = together(side, up_a, down_a, up_b, down_b)
+    pair = jnp.concatenate([gated, side], axis=0)
+    pair_up, pair_down = move(pair, "x", 1), move(pair, "x", -1)
+    up_a, down_a = move(up_a, "z", 1), move(down_a, "z", -1)
+    up_b, down_b = move(up_b, "z", 1), move(down_b, "z", -1)
+    other = move(pair, "core", 1)
+    arrived((up_a, (0, 5)), (down_a, (0, 3)), (up_b, (1, 6)), (down_b, (1, 2)))
+
+    pair_up, pair_down, up_a, up_b, down_b, other = together(pair_up, pair_down, up_a, up_b, down_b, other)
+    far_same, far_cross = move(pair_up[0], "x", 1), move(pair_down[1], "x", -1)
+    up_a, up_b, down_b = move(up_a, "z", 1), move(up_b, "z", 1), move(down_b, "z", -1)
+    other_up, other_down = move(pair_up, "core", 1), move(pair_down, "core", 1)
+    arrived((up_a, (0, 4)), (up_b, (1, 5)), (down_b, (1, 3)))
+
+    far_same, far_cross, down_b, other_up, other_down = together(far_same, far_cross, down_b, other_up, other_down)
+    down_b = move(down_b, "z", -1)
+    other_same, other_cross = move(far_same, "core", 1), move(far_cross, "core", 1)
+    arrived((down_b, (1, 4)))
+
+    pieces, ranks = [], []
+    for rows, group in enumerate(
+        [(pair, pair_up, pair_down, far_same, far_cross), (other, other_up, other_down, other_same, other_cross)]
+    ):
+        for value, dx in zip(group[:3], (0, 3, 1)):
+            for dy in range(2):
+                pieces.append(value[dy])
+                ranks.append((rows, dx, dy))
+        for dy in range(2):
+            pieces.append(group[3 + dy])
+            ranks.append((rows, 2, dy))
     part = jax.ShapeDtypeStruct((2, ROWS, 256), BF16)
-    kept, sent = call(
-        lambda *refs: project_body(places, *refs),
-        [part, part],
-        [pltpu.VMEM((2, 2, ROWS, 256), F32)],
-        2 * 512 * 512 * 4096, 10 << 20,
-        own, other, *blocks,
-    )
-    swapped = lax.ppermute(sent, "core", ring(2, 1))
+    kept, sent = pl.pallas_call(
+        lambda *refs: project_body(places, ranks, *refs),
+        out_shape=[part, part],
+        in_specs=[pl.BlockSpec(memory_space=pl.ANY)] * (len(pieces) + len(blocks)),
+        out_specs=whole(2),
+        scratch_shapes=[
+            pltpu.VMEM((2, 8, ROWS, CHANS), BF16),
+            pltpu.VMEM((len(blocks), 512, 256), BF16),
+            pltpu.VMEM((2, 2, ROWS, 256), F32),
+            pltpu.SemaphoreType.DMA((len(pieces),)),
+            pltpu.SemaphoreType.DMA((len(blocks),)),
+        ],
+        compiler_params=pltpu.CompilerParams(vmem_limit_bytes=VMEM_LIMIT),
+        cost_estimate=pl.CostEstimate(flops=2 * 512 * 512 * 4096, bytes_accessed=10 << 20, transcendentals=0),
+    )(*pieces, *blocks)
+    swapped = move(sent, "core", 1)
     even = jnp.where(core == 0, kept, swapped)
     odd = jnp.where(core == 0, swapped, kept)
     return jnp.concatenate([even[0], odd[0], even[1], odd[1]], axis=1)

time: 149 us -> 126 us (0.85); the launches traced: 147 us -> 125 us
  blocking collectives: 33.1 us -> 0 us
  waiting for transfers between devices: 28.2 us -> 45 us
  local copies, waits for them, and re-layouts: 8.18 us -> 4.81 us
  starting transfers between devices: 67.7 us -> 65.9 us
    all_to_all x1 -> x0, blocking collectives: 33.1 us -> none  [shards(): own = lax.all_to_all(gated, ('x', 'yhi'), 0, 0)]
    ppermute x20 -> x29, waiting for transfers between devices: 23.3 us -> 37.4 us  [the longest x28 37.4 us: move(): lax.ppermute(value, axis, ring({'ylo': 2, 'z': 8, 'core': 2, 'x': 4, 'yhi...]
    pallas_call x0 -> x1, Pallas kernels: none -> 5.64 us  [shards(): pl.pallas_call(lambda *refs: project_body(places, ranks, *refs), out_shap...]
    pallas_call x4 -> x3, Pallas kernels: 7.69 us -> 2.76 us  [call(): pl.pallas_call(body, out_shape=outs, in_specs=whole(len(args)), out_specs...]
    unnamed x26 -> x41, local copies, waits for them, and re-layouts: 7.41 us -> 3.85 us
    all_to_all x1, waiting for transfers between devices: 4.93 us -> 7.59 us  [shards(): lax.all_to_all(jnp.broadcast_to(chip[None], (16, MODES, HALF)), ('ylo', '...]
    ppermute x20 -> x29, starting transfers between devices: 60.1 us -> 58.2 us  [the longest x28 57.5 us: move(): lax.ppermute(value, axis, ring({'ylo': 2, 'z': 8, 'core': 2, 'x': 4, 'yhi...]
  transfers between devices with their start and end apart: 21 -> 30, of which waited for: 12 -> 15; matrix products, arithmetic and copies ran while one was open for 0% -> 0% of each run, Pallas kernels for 0% -> 1%
where the time goes in v2:
time: 126 us; the launch traced here: 125 us
  starting transfers between devices  65.9 us (52%)
  waiting for transfers between devices  45 us (36%)
  Pallas kernels  8.41 us (7%)
  local copies, waits for them, and re-layouts  4.81 us (4%)
    ppermute x28, starting transfers between devices, move(): lax.ppermute(value, axis, ring({'ylo': 2, 'z': 8, 'core': 2, 'x': 4, 'yhi...  57.5 us
    ppermute x28, waiting for transfers between devices, move(): lax.ppermute(value, axis, ring({'ylo': 2, 'z': 8, 'core': 2, 'x': 4, 'yhi...  37.4 us
    all_to_all x1, starting transfers between devices, shards(): lax.all_to_all(jnp.broadcast_to(chip[None], (16, MODES, HALF)), ('ylo', '...  7.7 us
    all_to_all x1, waiting for transfers between devices, shards(): lax.all_to_all(jnp.broadcast_to(chip[None], (16, MODES, HALF)), ('ylo', '...  7.59 us
    pallas_call x1, Pallas kernels, shards(): pl.pallas_call(lambda *refs: project_body(places, ranks, *refs), out_shap...  5.64 us
    unnamed x41, local copies, waits for them, and re-layouts  3.85 us
    pallas_call x3, Pallas kernels, call(): pl.pallas_call(body, out_shape=outs, in_specs=whole(len(args)), out_specs...  2.76 us
  transfers between devices with their start and end apart: 30, of which 15 were waited for; matrix products, arithmetic and copies ran while one was open for 0% of the time, Pallas kernels for 1%

profile of v2, /device:TPU:1, one launch (start us, length us, event | category | flops | bytes accessed | tf_op | source)
XLA Modules:
  0.0 125.4 jit_solution(8104211947718577173)
XLA Ops:
  3.7 3.3 %collective-permute-start = (f32[16,256]{1,0:T(8,128)S(1)}, f32[16,256]{1,0:T(8,128)S(1)}, u32[]{:S(2)}, u32[]{:S(2)}) collective-permute-start(f32[16,256]{1,0:T(8,128)S(1)} %get-tuple-element.35), channel_id=1, source_target_pairs={{0,8},{8,0},{1,9},{9,1},{2,10},{10,2},{3,11},{11,3},{4,12},{12,4},... | collective-permute-start | bytes 49160 | tf_op jit(solution)/shard_map/ppermute | solution.py:164
  8.7 7.7 %all-to-all-start = ((f32[16,16,256]{2,1,0:T(8,128)}), f32[16,16,256]{2,1,0:T(8,128)S(1)}, u32[]{:S(2)}, u32[]{:S(2)}) async-start(f32[16,16,256]{2,1,0:T(8,128)} %broadcast_in_dim.4), calls=%async_computation | async-start | bytes 524288 | tf_op jit(solution)/shard_map/all_to_all | solution.py:186
  17.8 7.6 %all-to-all-done = f32[16,16,256]{2,1,0:T(8,128)S(1)} async-done(((f32[16,16,256]{2,1,0:T(8,128)}), f32[16,16,256]{2,1,0:T(8,128)S(1)}, u32[]{:S(2)}, u32[]{:S(2)}) %all-to-all-start) | async-done | bytes 262176 | tf_op jit(solution)/shard_map/all_to_all | solution.py:186
  25.3 17.1 %collective-permute-start.5 = (bf16[512,256]{1,0:T(8,128)(2,1)S(1)}, bf16[512,256]{1,0:T(8,128)(2,1)S(1)}, u32[]{:S(2)}, u32[]{:S(2)}) collective-permute-start(bf16[512,256]{1,0:T(8,128)(2,1)S(1)} %collective-permute-done.1.refs_16_), channel_id=1, source_target_pairs={{0,112},{16,0},{32,16},{48,32},{64,48},{80,64},{96,80},{112,96},{1... | collective-permute-start | bytes 786440 | tf_op jit(solution)/shard_map/ppermute | solution.py:164
  46.8 6.0 %collective-permute-done.4.refs_18_ = bf16[512,256]{1,0:T(8,128)(2,1)S(1)} collective-permute-done((bf16[512,256]{1,0:T(8,128)(2,1)S(1)}, bf16[512,256]{1,0:T(8,128)(2,1)S(1)}, u32[]{:S(2)}, u32[]{:S(2)}) %collective-permute-start.4) | collective-permute-done | bytes 262176 | tf_op jit(solution)/shard_map/ppermute | solution.py:164
  52.8 2.7 %collective-permute-start.8 = (bf16[512,256]{1,0:T(8,128)(2,1)S(1)}, bf16[512,256]{1,0:T(8,128)(2,1)S(1)}, u32[]{:S(2)}, u32[]{:S(2)}) collective-permute-start(bf16[512,256]{1,0:T(8,128)(2,1)S(1)} %collective-permute-done.5.refs_19_), channel_id=1, source_target_pairs={{0,112},{16,0},{32,16},{48,32},{64,48},{80,64},{96,80},{112,96},{1... | collective-permute-start | bytes 786440 | tf_op jit(solution)/shard_map/ppermute | solution.py:164
  57.0 1.7 %collective-permute-start.6 = (bf16[1,256,512]{2,1,0:T(8,128)(2,1)S(1)}, bf16[1,256,512]{2,1,0:T(8,128)(2,1)S(1)}, u32[]{:S(2)}, u32[]{:S(2)}) collective-permute-start(bf16[1,256,512]{2,1,0:T(8,128)(2,1)S(1)} %shard_map.66), channel_id=1, source_target_pairs={{0,1},{1,0},{2,3},{3,2},{4,5},{5,4},{6,7},{7,6},{8,9},{9,8},{10,11... | collective-permute-start | bytes 786440 | tf_op jit(solution)/shard_map/ppermute | solution.py:164
  60.0 4.6 %collective-permute-done.10.refs_23_ = bf16[512,256]{1,0:T(8,128)(2,1)S(1)} collective-permute-done((bf16[512,256]{1,0:T(8,128)(2,1)S(1)}, bf16[512,256]{1,0:T(8,128)(2,1)S(1)}, u32[]{:S(2)}, u32[]{:S(2)}) %collective-permute-start.10) | collective-permute-done | bytes 262176 | tf_op jit(solution)/shard_map/ppermute | solution.py:164
  66.2 3.2 %collective-permute-start.16 = (bf16[2,256,512]{2,1,0:T(8,128)(2,1)S(1)}, bf16[2,256,512]{2,1,0:T(8,128)(2,1)S(1)}, u32[]{:S(2)}, u32[]{:S(2)}) collective-permute-start(bf16[2,256,512]{2,1,0:T(8,128)(2,1)S(1)} %constant_dynamic-update-slice_fusion), channel_id=1, source_target_pairs={{0,8},{8,0},{1,9},{9,1},{2,10},{10,2},{3,11},{11,3},{4,12},{12,4},... | collective-permute-start | bytes 1572872 | tf_op jit(solution)/shard_map/ppermute | solution.py:164
  69.5 4.2 %collective-permute-start.12 = (bf16[2,256,512]{2,1,0:T(8,128)(2,1)S(1)}, bf16[2,256,512]{2,1,0:T(8,128)(2,1)S(1)}, u32[]{:S(2)}, u32[]{:S(2)}) collective-permute-start(bf16[2,256,512]{2,1,0:T(8,128)(2,1)S(1)} %constant_dynamic-update-slice_fusion), channel_id=1, source_target_pairs={{0,6},{2,0},{4,2},{6,4},{1,7},{3,1},{5,3},{7,5},{8,14},{10,8},{12,... | collective-permute-start | bytes 1572872 | tf_op jit(solution)/shard_map/ppermute | solution.py:164
  73.8 3.0 %collective-permute-start.15 = (bf16[512,256]{1,0:T(8,128)(2,1)S(1)}, bf16[512,256]{1,0:T(8,128)(2,1)S(1)}, u32[]{:S(2)}, u32[]{:S(2)}) collective-permute-start(bf16[512,256]{1,0:T(8,128)(2,1)S(1)} %collective-permute-done.10.refs_23_), channel_id=1, source_target_pairs={{0,112},{16,0},{32,16},{48,32},{64,48},{80,64},{96,80},{112,96},{1... | collective-permute-start | bytes 786440 | tf_op jit(solution)/shard_map/ppermute | solution.py:164
  76.8 6.1 %collective-permute-done.14.refs_26_ = bf16[512,256]{1,0:T(8,128)(2,1)S(1)} collective-permute-done((bf16[512,256]{1,0:T(8,128)(2,1)S(1)}, bf16[512,256]{1,0:T(8,128)(2,1)S(1)}, u32[]{:S(2)}, u32[]{:S(2)}) %collective-permute-start.14) | collective-permute-done | bytes 262176 | tf_op jit(solution)/shard_map/ppermute | solution.py:164
  82.9 1.9 %collective-permute-done.12 = bf16[2,256,512]{2,1,0:T(8,128)(2,1)S(1)} collective-permute-done((bf16[2,256,512]{2,1,0:T(8,128)(2,1)S(1)}, bf16[2,256,512]{2,1,0:T(8,128)(2,1)S(1)}, u32[]{:S(2)}, u32[]{:S(2)}) %collective-permute-start.12) | collective-permute-done | bytes 524320 | tf_op jit(solution)/shard_map/ppermute | solution.py:164
  84.8 3.1 %collective-permute-done.11 = bf16[2,256,512]{2,1,0:T(8,128)(2,1)S(1)} collective-permute-done((bf16[2,256,512]{2,1,0:T(8,128)(2,1)S(1)}, bf16[2,256,512]{2,1,0:T(8,128)(2,1)S(1)}, u32[]{:S(2)}, u32[]{:S(2)}) %collective-permute-start.11) | collective-permute-done | bytes 524320 | tf_op jit(solution)/shard_map/ppermute | solution.py:164
  87.9 2.9 %collective-permute-start.19 = (bf16[512,256]{1,0:T(8,128)(2,1)S(1)}, bf16[512,256]{1,0:T(8,128)(2,1)S(1)}, u32[]{:S(2)}, u32[]{:S(2)}) collective-permute-start(bf16[512,256]{1,0:T(8,128)(2,1)S(1)} %collective-permute-done.15.refs_27_), channel_id=1, source_target_pairs={{0,112},{16,0},{32,16},{48,32},{64,48},{80,64},{96,80},{112,96},{1... | collective-permute-start | bytes 786440 | tf_op jit(solution)/shard_map/ppermute | solution.py:164
  92.7 2.7 %collective-permute-start.18 = (bf16[256,512]{1,0:T(8,128)(2,1)S(1)}, bf16[256,512]{1,0:T(8,128)(2,1)S(1)}, u32[]{:S(2)}, u32[]{:S(2)}) collective-permute-start(bf16[256,512]{1,0:T(8,128)(2,1)S(1)} %get-tuple-element.71.refs_5_), channel_id=1, source_target_pairs={{0,6},{2,0},{4,2},{6,4},{1,7},{3,1},{5,3},{7,5},{8,14},{10,8},{12,... | collective-permute-start | bytes 786440 | tf_op jit(solution)/shard_map/ppermute | solution.py:164
  95.4 3.0 %collective-permute-start.24 = (bf16[512,256]{1,0:T(8,128)(2,1)S(1)}, bf16[512,256]{1,0:T(8,128)(2,1)S(1)}, u32[]{:S(2)}, u32[]{:S(2)}) collective-permute-start(bf16[512,256]{1,0:T(8,128)(2,1)S(1)} %collective-permute-done.8.refs_21_), channel_id=1, source_target_pairs={{0,112},{16,0},{32,16},{48,32},{64,48},{80,64},{96,80},{112,96},{1... | collective-permute-start | bytes 786440 | tf_op jit(solution)/shard_map/ppermute | solution.py:164
  98.5 2.8 %collective-permute-done.17.refs_6_ = bf16[256,512]{1,0:T(8,128)(2,1)S(1)} collective-permute-done((bf16[256,512]{1,0:T(8,128)(2,1)S(1)}, bf16[256,512]{1,0:T(8,128)(2,1)S(1)}, u32[]{:S(2)}, u32[]{:S(2)}) %collective-permute-start.17) | collective-permute-done | bytes 262176 | tf_op jit(solution)/shard_map/ppermute | solution.py:164
  101.4 2.7 %collective-permute-start.27 = (bf16[512,256]{1,0:T(8,128)(2,1)S(1)}, bf16[512,256]{1,0:T(8,128)(2,1)S(1)}, u32[]{:S(2)}, u32[]{:S(2)}) collective-permute-start(bf16[512,256]{1,0:T(8,128)(2,1)S(1)} %collective-permute-done.19.refs_30_), channel_id=1, source_target_pairs={{0,112},{16,0},{32,16},{48,32},{64,48},{80,64},{96,80},{112,96},{1... | collective-permute-start | bytes 786440 | tf_op jit(solution)/shard_map/ppermute | solution.py:164
  104.1 1.9 %collective-permute-start.22 = (bf16[256,512]{1,0:T(8,128)(2,1)S(1)}, bf16[256,512]{1,0:T(8,128)(2,1)S(1)}, u32[]{:S(2)}, u32[]{:S(2)}) collective-permute-start(bf16[256,512]{1,0:T(8,128)(2,1)S(1)} %collective-permute-done.17.refs_6_), channel_id=1, source_target_pairs={{0,8},{8,0},{1,9},{9,1},{2,10},{10,2},{3,11},{11,3},{4,12},{12,4},... | collective-permute-start | bytes 786440 | tf_op jit(solution)/shard_map/ppermute | solution.py:164
  106.7 2.2 %collective-permute-done.25.refs_28_ = bf16[512,256]{1,0:T(8,128)(2,1)S(1)} collective-permute-done((bf16[512,256]{1,0:T(8,128)(2,1)S(1)}, bf16[512,256]{1,0:T(8,128)(2,1)S(1)}, u32[]{:S(2)}, u32[]{:S(2)}) %collective-permute-start.25) | collective-permute-done | bytes 262176 | tf_op jit(solution)/shard_map/ppermute | solution.py:164
  108.9 5.6 %collective-permute-done.26.refs_29_ = bf16[512,256]{1,0:T(8,128)(2,1)S(1)} collective-permute-done((bf16[512,256]{1,0:T(8,128)(2,1)S(1)}, bf16[512,256]{1,0:T(8,128)(2,1)S(1)}, u32[]{:S(2)}, u32[]{:S(2)}) %collective-permute-start.26) | collective-permute-done | bytes 262176 | tf_op jit(solution)/shard_map/ppermute | solution.py:164
  115.3 5.6 %shard_map.67 = (bf16[2,256,256]{2,1,0:T(8,128)(2,1)S(1)}, bf16[2,256,256]{2,1,0:T(8,128)(2,1)S(1)}) custom-call(bf16[256,512]{1,0:T(8,128)(2,1)S(1)} %bitcast.133, bf16[256,512]{1,0:T(8,128)(2,1)S(1)} %bitcast.134, bf16[256,512]{1,0:T(8,128)(2,1)S(1)} %get-tuple-element.74.refs_2_, bf16[256,512]{1,0:T(8,128)(2,1)S(1)} %get-tuple-element.73.refs_3_, ...), custom_call_target="tpu_custom_call" | custom-call | flops 2147483648 | bytes 10485760 | tf_op jit(solution)/shard_map/pallas_call | solution.py:249
  121.0 2.4 %collective-permute-start.28 = (bf16[2,256,256]{2,1,0:T(8,128)(2,1)S(1)}, bf16[2,256,256]{2,1,0:T(8,128)(2,1)S(1)}, u32[]{:S(2)}, u32[]{:S(2)}) collective-permute-start(bf16[2,256,256]{2,1,0:T(8,128)(2,1)S(1)} %get-tuple-element.60), channel_id=1, source_target_pairs={{0,8},{8,0},{1,9},{9,1},{2,10},{10,2},{3,11},{11,3},{4,12},{12,4},... | collective-permute-start | bytes 786440 | tf_op jit(solution)/shard_map/ppermute | solution.py:164
  (94 shorter events, 20.9 us)
Async XLA Ops:
  8.7 16.7 %all-to-all-start = ((f32[16,16,256]{2,1,0:T(8,128)}), f32[16,16,256]{2,1,0:T(8,128)S(1)}, u32[]{:S(2)}, u32[]{:S(2)}) async-start(f32[16,16,256]{2,1,0:T(8,128)} %broadcast_in_dim.4), calls=%async_computation | async-start | bytes 524288 | tf_op jit(solution)/shard_map/all_to_all | solution.py:186
  25.3 21.5 %collective-permute-start.5 = (bf16[512,256]{1,0:T(8,128)(2,1)S(1)}, bf16[512,256]{1,0:T(8,128)(2,1)S(1)}, u32[]{:S(2)}, u32[]{:S(2)}) collective-permute-start(bf16[512,256]{1,0:T(8,128)(2,1)S(1)} %collective-permute-done.1.refs_16_), channel_id=1, source_target_pairs={{0,112},{16,0},{32,16},{48,32},{64,48},{80,64},{96,80},{112,96},{1... | collective-permute-start | bytes 786440 | tf_op jit(solution)/shard_map/ppermute | solution.py:164
  42.5 10.4 %collective-permute-start.4 = (bf16[512,256]{1,0:T(8,128)(2,1)S(1)}, bf16[512,256]{1,0:T(8,128)(2,1)S(1)}, u32[]{:S(2)}, u32[]{:S(2)}) collective-permute-start(bf16[512,256]{1,0:T(8,128)(2,1)S(1)} %collective-permute-done.1.refs_16_), channel_id=1, source_target_pairs={{0,16},{16,32},{32,48},{48,64},{64,80},{80,96},{96,112},{112,0},{1... | collective-permute-start | bytes 786440 | tf_op jit(solution)/shard_map/ppermute | solution.py:164
  42.5 10.4 %collective-permute-start.3 = (bf16[512,256]{1,0:T(8,128)(2,1)S(1)}, bf16[512,256]{1,0:T(8,128)(2,1)S(1)}, u32[]{:S(2)}, u32[]{:S(2)}) collective-permute-start(bf16[512,256]{1,0:T(8,128)(2,1)S(1)} %collective-permute-done.1.refs_16_), channel_id=1, source_target_pairs={{0,128},{128,0},{1,129},{129,1},{2,130},{130,2},{3,131},{131,3},{4... | collective-permute-start | bytes 786440 | tf_op jit(solution)/shard_map/ppermute | solution.py:164
  55.5 9.1 %collective-permute-start.10 = (bf16[512,256]{1,0:T(8,128)(2,1)S(1)}, bf16[512,256]{1,0:T(8,128)(2,1)S(1)}, u32[]{:S(2)}, u32[]{:S(2)}) collective-permute-start(bf16[512,256]{1,0:T(8,128)(2,1)S(1)} %collective-permute-done.3.refs_17_), channel_id=1, source_target_pairs={{0,112},{16,0},{32,16},{48,32},{64,48},{80,64},{96,80},{112,96},{1... | collective-permute-start | bytes 786440 | tf_op jit(solution)/shard_map/ppermute | solution.py:164
  55.6 10.1 %collective-permute-start.9 = (bf16[512,256]{1,0:T(8,128)(2,1)S(1)}, bf16[512,256]{1,0:T(8,128)(2,1)S(1)}, u32[]{:S(2)}, u32[]{:S(2)}) collective-permute-start(bf16[512,256]{1,0:T(8,128)(2,1)S(1)} %collective-permute-done.3.refs_17_), channel_id=1, source_target_pairs={{0,16},{16,32},{32,48},{48,64},{64,80},{80,96},{96,112},{112,0},{1... | collective-permute-start | bytes 786440 | tf_op jit(solution)/shard_map/ppermute | solution.py:164
  57.0 8.7 %collective-permute-start.6 = (bf16[1,256,512]{2,1,0:T(8,128)(2,1)S(1)}, bf16[1,256,512]{2,1,0:T(8,128)(2,1)S(1)}, u32[]{:S(2)}, u32[]{:S(2)}) collective-permute-start(bf16[1,256,512]{2,1,0:T(8,128)(2,1)S(1)} %shard_map.66), channel_id=1, source_target_pairs={{0,1},{1,0},{2,3},{3,2},{4,5},{5,4},{6,7},{7,6},{8,9},{9,8},{10,11... | collective-permute-start | bytes 786440 | tf_op jit(solution)/shard_map/ppermute | solution.py:164
  65.6 8.1 %collective-permute-start.13 = (bf16[512,256]{1,0:T(8,128)(2,1)S(1)}, bf16[512,256]{1,0:T(8,128)(2,1)S(1)}, u32[]{:S(2)}, u32[]{:S(2)}) collective-permute-start(bf16[512,256]{1,0:T(8,128)(2,1)S(1)} %collective-permute-done.7.refs_20_), channel_id=1, source_target_pairs={{0,16},{16,32},{32,48},{48,64},{64,80},{80,96},{96,112},{112,0},{1... | collective-permute-start | bytes 786440 | tf_op jit(solution)/shard_map/ppermute | solution.py:164
  66.2 16.6 %collective-permute-start.16 = (bf16[2,256,512]{2,1,0:T(8,128)(2,1)S(1)}, bf16[2,256,512]{2,1,0:T(8,128)(2,1)S(1)}, u32[]{:S(2)}, u32[]{:S(2)}) collective-permute-start(bf16[2,256,512]{2,1,0:T(8,128)(2,1)S(1)} %constant_dynamic-update-slice_fusion), channel_id=1, source_target_pairs={{0,8},{8,0},{1,9},{9,1},{2,10},{10,2},{3,11},{11,3},{4,12},{12,4},... | collective-permute-start | bytes 1572872 | tf_op jit(solution)/shard_map/ppermute | solution.py:164
  69.5 15.3 %collective-permute-start.12 = (bf16[2,256,512]{2,1,0:T(8,128)(2,1)S(1)}, bf16[2,256,512]{2,1,0:T(8,128)(2,1)S(1)}, u32[]{:S(2)}, u32[]{:S(2)}) collective-permute-start(bf16[2,256,512]{2,1,0:T(8,128)(2,1)S(1)} %constant_dynamic-update-slice_fusion), channel_id=1, source_target_pairs={{0,6},{2,0},{4,2},{6,4},{1,7},{3,1},{5,3},{7,5},{8,14},{10,8},{12,... | collective-permute-start | bytes 1572872 | tf_op jit(solution)/shard_map/ppermute | solution.py:164
  73.7 14.1 %collective-permute-start.11 = (bf16[2,256,512]{2,1,0:T(8,128)(2,1)S(1)}, bf16[2,256,512]{2,1,0:T(8,128)(2,1)S(1)}, u32[]{:S(2)}, u32[]{:S(2)}) collective-permute-start(bf16[2,256,512]{2,1,0:T(8,128)(2,1)S(1)} %constant_dynamic-update-slice_fusion), channel_id=1, source_target_pairs={{0,2},{2,4},{4,6},{6,0},{1,3},{3,5},{5,7},{7,1},{8,10},{10,12},{12... | collective-permute-start | bytes 1572872 | tf_op jit(solution)/shard_map/ppermute | solution.py:164
  73.7 9.1 %collective-permute-start.14 = (bf16[512,256]{1,0:T(8,128)(2,1)S(1)}, bf16[512,256]{1,0:T(8,128)(2,1)S(1)}, u32[]{:S(2)}, u32[]{:S(2)}) collective-permute-start(bf16[512,256]{1,0:T(8,128)(2,1)S(1)} %collective-permute-done.9.refs_22_), channel_id=1, source_target_pairs={{0,16},{16,32},{32,48},{48,64},{64,80},{80,96},{96,112},{112,0},{1... | collective-permute-start | bytes 786440 | tf_op jit(solution)/shard_map/ppermute | solution.py:164
  73.8 9.1 %collective-permute-start.15 = (bf16[512,256]{1,0:T(8,128)(2,1)S(1)}, bf16[512,256]{1,0:T(8,128)(2,1)S(1)}, u32[]{:S(2)}, u32[]{:S(2)}) collective-permute-start(bf16[512,256]{1,0:T(8,128)(2,1)S(1)} %collective-permute-done.10.refs_23_), channel_id=1, source_target_pairs={{0,112},{16,0},{32,16},{48,32},{64,48},{80,64},{96,80},{112,96},{1... | collective-permute-start | bytes 786440 | tf_op jit(solution)/shard_map/ppermute | solution.py:164
  87.9 7.6 %collective-permute-start.19 = (bf16[512,256]{1,0:T(8,128)(2,1)S(1)}, bf16[512,256]{1,0:T(8,128)(2,1)S(1)}, u32[]{:S(2)}, u32[]{:S(2)}) collective-permute-start(bf16[512,256]{1,0:T(8,128)(2,1)S(1)} %collective-permute-done.15.refs_27_), channel_id=1, source_target_pairs={{0,112},{16,0},{32,16},{48,32},{64,48},{80,64},{96,80},{112,96},{1... | collective-permute-start | bytes 786440 | tf_op jit(solution)/shard_map/ppermute | solution.py:164
  90.8 10.5 %collective-permute-start.20 = (bf16[2,256,512]{2,1,0:T(8,128)(2,1)S(1)}, bf16[2,256,512]{2,1,0:T(8,128)(2,1)S(1)}, u32[]{:S(2)}, u32[]{:S(2)}) collective-permute-start(bf16[2,256,512]{2,1,0:T(8,128)(2,1)S(1)} %collective-permute-done.11), channel_id=1, source_target_pairs={{0,8},{8,0},{1,9},{9,1},{2,10},{10,2},{3,11},{11,3},{4,12},{12,4},... | collective-permute-start | bytes 1572872 | tf_op jit(solution)/shard_map/ppermute | solution.py:164
  92.5 8.8 %collective-permute-start.21 = (bf16[2,256,512]{2,1,0:T(8,128)(2,1)S(1)}, bf16[2,256,512]{2,1,0:T(8,128)(2,1)S(1)}, u32[]{:S(2)}, u32[]{:S(2)}) collective-permute-start(bf16[2,256,512]{2,1,0:T(8,128)(2,1)S(1)} %collective-permute-done.12), channel_id=1, source_target_pairs={{0,8},{8,0},{1,9},{9,1},{2,10},{10,2},{3,11},{11,3},{4,12},{12,4},... | collective-permute-start | bytes 1572872 | tf_op jit(solution)/shard_map/ppermute | solution.py:164
  92.6 8.6 %collective-permute-start.17 = (bf16[256,512]{1,0:T(8,128)(2,1)S(1)}, bf16[256,512]{1,0:T(8,128)(2,1)S(1)}, u32[]{:S(2)}, u32[]{:S(2)}) collective-permute-start(bf16[256,512]{1,0:T(8,128)(2,1)S(1)} %get-tuple-element.74.refs_2_), channel_id=1, source_target_pairs={{0,2},{2,4},{4,6},{6,0},{1,3},{3,5},{5,7},{7,1},{8,10},{10,12},{12... | collective-permute-start | bytes 786440 | tf_op jit(solution)/shard_map/ppermute | solution.py:164
  92.7 8.5 %collective-permute-start.18 = (bf16[256,512]{1,0:T(8,128)(2,1)S(1)}, bf16[256,512]{1,0:T(8,128)(2,1)S(1)}, u32[]{:S(2)}, u32[]{:S(2)}) collective-permute-start(bf16[256,512]{1,0:T(8,128)(2,1)S(1)} %get-tuple-element.71.refs_5_), channel_id=1, source_target_pairs={{0,6},{2,0},{4,2},{6,4},{1,7},{3,1},{5,3},{7,5},{8,14},{10,8},{12,... | collective-permute-start | bytes 786440 | tf_op jit(solution)/shard_map/ppermute | solution.py:164
  95.4 10.6 %collective-permute-start.24 = (bf16[512,256]{1,0:T(8,128)(2,1)S(1)}, bf16[512,256]{1,0:T(8,128)(2,1)S(1)}, u32[]{:S(2)}, u32[]{:S(2)}) collective-permute-start(bf16[512,256]{1,0:T(8,128)(2,1)S(1)} %collective-permute-done.8.refs_21_), channel_id=1, source_target_pairs={{0,112},{16,0},{32,16},{48,32},{64,48},{80,64},{96,80},{112,96},{1... | collective-permute-start | bytes 786440 | tf_op jit(solution)/shard_map/ppermute | solution.py:164
  101.2 7.7 %collective-permute-start.25 = (bf16[512,256]{1,0:T(8,128)(2,1)S(1)}, bf16[512,256]{1,0:T(8,128)(2,1)S(1)}, u32[]{:S(2)}, u32[]{:S(2)}) collective-permute-start(bf16[512,256]{1,0:T(8,128)(2,1)S(1)} %collective-permute-done.13.refs_24_), channel_id=1, source_target_pairs={{0,16},{16,32},{32,48},{48,64},{64,80},{80,96},{96,112},{112,0},{1... | collective-permute-start | bytes 786440 | tf_op jit(solution)/shard_map/ppermute | solution.py:164
  101.2 13.2 %collective-permute-start.26 = (bf16[512,256]{1,0:T(8,128)(2,1)S(1)}, bf16[512,256]{1,0:T(8,128)(2,1)S(1)}, u32[]{:S(2)}, u32[]{:S(2)}) collective-permute-start(bf16[512,256]{1,0:T(8,128)(2,1)S(1)} %collective-permute-done.14.refs_26_), channel_id=1, source_target_pairs={{0,16},{16,32},{32,48},{48,64},{64,80},{80,96},{96,112},{112,0},{1... | collective-permute-start | bytes 786440 | tf_op jit(solution)/shard_map/ppermute | solution.py:164
  101.4 13.1 %collective-permute-start.27 = (bf16[512,256]{1,0:T(8,128)(2,1)S(1)}, bf16[512,256]{1,0:T(8,128)(2,1)S(1)}, u32[]{:S(2)}, u32[]{:S(2)}) collective-permute-start(bf16[512,256]{1,0:T(8,128)(2,1)S(1)} %collective-permute-done.19.refs_30_), channel_id=1, source_target_pairs={{0,112},{16,0},{32,16},{48,32},{64,48},{80,64},{96,80},{112,96},{1... | collective-permute-start | bytes 786440 | tf_op jit(solution)/shard_map/ppermute | solution.py:164
  104.1 10.4 %collective-permute-start.22 = (bf16[256,512]{1,0:T(8,128)(2,1)S(1)}, bf16[256,512]{1,0:T(8,128)(2,1)S(1)}, u32[]{:S(2)}, u32[]{:S(2)}) collective-permute-start(bf16[256,512]{1,0:T(8,128)(2,1)S(1)} %collective-permute-done.17.refs_6_), channel_id=1, source_target_pairs={{0,8},{8,0},{1,9},{9,1},{2,10},{10,2},{3,11},{11,3},{4,12},{12,4},... | collective-permute-start | bytes 786440 | tf_op jit(solution)/shard_map/ppermute | solution.py:164
  106.0 8.5 %collective-permute-start.23 = (bf16[256,512]{1,0:T(8,128)(2,1)S(1)}, bf16[256,512]{1,0:T(8,128)(2,1)S(1)}, u32[]{:S(2)}, u32[]{:S(2)}) collective-permute-start(bf16[256,512]{1,0:T(8,128)(2,1)S(1)} %collective-permute-done.18.refs_7_), channel_id=1, source_target_pairs={{0,8},{8,0},{1,9},{9,1},{2,10},{10,2},{3,11},{11,3},{4,12},{12,4},... | collective-permute-start | bytes 786440 | tf_op jit(solution)/shard_map/ppermute | solution.py:164
  (26 other events, 228.4 us)

commit v3 on v1

--- a/solution.py
+++ b/solution.py
@@ -1,5 +1,6 @@
 import jax
 import jax.numpy as jnp
+import numpy as np
 from jax import lax
 from jax.experimental import pallas as pl
 from jax.experimental.pallas import tpu as pltpu
@@ -14,6 +15,7 @@
 HALF = CHANS // 2
 F32, BF16 = jnp.float32, jnp.bfloat16
 VMEM_LIMIT = 48 * 1024 * 1024
+AHEAD = 10**11
 
 
 def whole(n):
@@ -39,7 +41,13 @@
         sig[lt] = product.astype(BF16).astype(F32)
 
 
-def sums_body(inner, values, decays, sums, keep, send, sig):
+def sums_body(inner_hbm, values_hbm, decays_hbm, sums, keep, send, sig, inner, values, decays, sems):
+    pairs = ((decays_hbm, decays), (inner_hbm, inner), (values_hbm, values))
+    copies = [pltpu.make_async_copy(a, b, sems.at[i]) for i, (a, b) in enumerate(pairs)]
+    for copy in copies:
+        copy.start()
+    for copy in copies:
+        copy.wait()
     signal_into(inner, values, sig)
     for lt in range(TILES):
         cols = slice(lt * LANES, (lt + 1) * LANES)
@@ -118,95 +126,180 @@
             gated[copy, :, cols] = result
 
 
-def project_body(places, *refs):
-    own, other = refs[0], refs[1]
-    blocks = refs[2 : 2 + len(places)]
-    mine, theirs, acc = refs[2 + len(places) :]
-    z, y = lax.axis_index("z"), lax.axis_index("ylo")
-    acc[...] = jnp.zeros_like(acc)
-    for block, (turn, shift) in zip(blocks, places):
-        at = lax.rem(z + shift, 8)
-        rank = lax.rem(y + turn, 2) * 4 + at // 2
-        odd = lax.rem(at, 2)
-        weight = block[...]
-        acc[0, odd] += jnp.dot(own[rank], weight, preferred_element_type=F32)
-        acc[1, odd] += jnp.dot(other[rank], weight, preferred_element_type=F32)
-    mine[...] = acc[0].astype(BF16)
-    theirs[...] = acc[1].astype(BF16)
+def source_of(turn, shift):
+    x, yhi = lax.axis_index("x"), lax.axis_index("yhi")
+    z, ylo = lax.axis_index("z"), lax.axis_index("ylo")
+    ahead = lax.rem(z + shift + 8 - 2 * (lax.rem(x, 2) * 2 + yhi), 8)
+    odd = jnp.where((ahead >= 1) & (ahead <= 4), 1, 0)
+    far = jnp.where(odd == 1, ahead - 1, lax.rem(8 - ahead, 8))
+    turned = jnp.where(far == 0, 2, jnp.where(far == 1, 3, jnp.where(far == 2, 1, 0)))
+    group = lax.rem(x + turned, 4) * 2 + lax.rem(ylo + turn + yhi, 2)
+    return group, odd
+
+
+def bundle_body(*refs):
+    stacks, (out, sems) = refs[:-2], refs[-2:]
+    copies, at = [], 0
+    for i, stack in enumerate(stacks):
+        count = stack.shape[0]
+        copies.append(pltpu.make_async_copy(stack, out.at[at : at + count], sems.at[i]))
+        at += count
+    for copy in copies:
+        copy.start()
+    for copy in copies:
+        copy.wait()
+
+
+def bundle(stacks):
+    count = sum(stack.shape[0] for stack in stacks)
+    return pl.pallas_call(
+        bundle_body,
+        out_shape=jax.ShapeDtypeStruct((count, 512, 256), BF16),
+        in_specs=[pl.BlockSpec(memory_space=pl.ANY)] * len(stacks),
+        out_specs=pl.BlockSpec(memory_space=pl.ANY),
+        scratch_shapes=[pltpu.SemaphoreType.DMA((len(stacks),))],
+        compiler_params=pltpu.CompilerParams(vmem_limit_bytes=VMEM_LIMIT),
+        cost_estimate=pl.CostEstimate(flops=0, bytes_accessed=count << 19, transcendentals=0),
+    )(*stacks)
+
+
+RANKS = [(dx, dy) for dx in (0, 3, 1, 2) for dy in range(2)]
+
+
+def project_body(places, counts, *refs):
+    pieces, stacks = refs[:8], refs[8 : 8 + len(counts)]
+    result, gated, weight, row_sem, block_sem = refs[8 + len(counts) :]
+    x, yhi, core = lax.axis_index("x"), lax.axis_index("yhi"), lax.axis_index("core")
+    copies = []
+    for i, (piece, (dx, dy)) in enumerate(zip(pieces, RANKS)):
+        rank = lax.rem(x + dx, 4) * 2 + lax.rem(yhi + dy, 2)
+        columns = pl.ds(pl.multiple_of(rank * CHANS, CHANS), CHANS)
+        copies.append(pltpu.make_async_copy(piece, gated.at[:, columns], row_sem.at[i]))
+    at = 0
+    for stack, count in zip(stacks, counts):
+        for i in range(count):
+            side, (group, odd) = at // 16, source_of(*places[at % 16])
+            columns = slice(side * 256, side * 256 + 256)
+            copies.append(pltpu.make_async_copy(stack.at[i], weight.at[odd, group, :, columns], block_sem.at[at]))
+            at += 1
+    for copy in copies:
+        copy.start()
+    for copy in copies:
+        copy.wait()
+    for odd in range(2):
+        total = jnp.dot(gated[...], weight[odd].reshape(8 * 512, 512), preferred_element_type=F32).astype(BF16)
+        own, other = total[:, :256], total[:, 256:]
+        result[:, odd * 512 : odd * 512 + 256] = jnp.where(core == 0, own, other)
+        result[:, odd * 512 + 256 : odd * 512 + 512] = jnp.where(core == 0, other, own)
+
+
+def project(places, pieces, stacks):
+    counts = [stack.shape[0] for stack in stacks]
+    return pl.pallas_call(
+        lambda *refs: project_body(places, counts, *refs),
+        out_shape=jax.ShapeDtypeStruct((ROWS, 1024), BF16),
+        in_specs=[pl.BlockSpec(memory_space=pl.ANY)] * (8 + len(stacks)),
+        out_specs=whole(1)[0],
+        scratch_shapes=[
+            pltpu.VMEM((ROWS, 8 * CHANS), BF16),
+            pltpu.VMEM((2, 8, 512, 512), BF16),
+            pltpu.SemaphoreType.DMA((8,)),
+            pltpu.SemaphoreType.DMA((32,)),
+        ],
+        compiler_params=pltpu.CompilerParams(vmem_limit_bytes=VMEM_LIMIT),
+        cost_estimate=pl.CostEstimate(flops=1 << 31, bytes_accessed=10 << 20, transcendentals=0),
+    )(*pieces, *stacks)
 
 
 def ring(size, shift):
     return [(i, (i + shift) % size) for i in range(size)]
 
 
-def gather_weight(block):
+def swap(block):
+    def number(x, yhi, ylo, z, core):
+        return ((ylo * 8 + z) * 2 + core) * 8 + x * 2 + yhi
+
     pairs = []
-    for a in range(8):
-        for b in range(4):
-            for c in range(8):
-                pairs.append(((a * 4 + b) * 8 + c, (c * 4 + b) * 8 + a))
-    first = lax.ppermute(block, ("ylo", "z", "core", "x", "yhi"), pairs)
-    second = lax.ppermute(first, "ylo", ring(2, 1))
-    blocks, places = [first, second], [(0, 0), (1, 0)]
-    up, down = [first, second], [first, second]
-    for step in range(1, 5):
-        for turn in range(2):
-            up[turn] = lax.ppermute(up[turn], "z", ring(8, 1))
-            blocks.append(up[turn])
-            places.append((turn, 8 - step))
-            if step < 4:
-                down[turn] = lax.ppermute(down[turn], "z", ring(8, -1))
-                blocks.append(down[turn])
-                places.append((turn, step))
-    return blocks, places
+    for x, yhi, ylo, z, core in np.ndindex(4, 2, 2, 8, 2):
+        to_x, to_yhi = ylo * 2 + z // 4, z // 2 % 2
+        far = (3, 2, 0, 1)[(x - to_x) % 4]
+        to_z = (z + far if z % 2 else z - far) % 8
+        pairs.append((number(x, yhi, ylo, z, core), number(to_x, to_yhi, yhi ^ to_yhi, to_z, core)))
+    return lax.ppermute(block, ("ylo", "z", "core", "x", "yhi"), pairs)
+
+
+def move(value, axis, shift):
+    return lax.ppermute(value, axis, ring({"ylo": 2, "z": 8, "core": 2, "x": 4, "yhi": 2}[axis], shift))
+
+
+def together(*values):
+    return lax.optimization_barrier(values)
 
 
 def shards(outer_gate, inner_gate, values, residues, decays, out_weight):
-    blocks, places = gather_weight(out_weight)
+    first = swap(out_weight)
     tiled = jax.ShapeDtypeStruct((TILES, ROWS, LANES), F32)
     half = jax.ShapeDtypeStruct((MODES, HALF), F32)
     tile_scratch = pltpu.VMEM((TILES, ROWS, LANES), F32)
     work = ROWS * CHANS * MODES * 2
-    sums, keep, send = call(
-        sums_body, [tiled, half, half], [tile_scratch], work, 1 << 20, inner_gate, values, decays
-    )
+    shard = pltpu.VMEM((ROWS, CHANS), BF16)
+    sums, keep, send = pl.pallas_call(
+        sums_body,
+        out_shape=[tiled, half, half],
+        in_specs=[pl.BlockSpec(memory_space=pl.ANY)] * 3,
+        out_specs=whole(3),
+        scratch_shapes=[tile_scratch, shard, shard, pltpu.VMEM((MODES, CHANS), F32), pltpu.SemaphoreType.DMA((3,))],
+        compiler_params=pltpu.CompilerParams(vmem_limit_bytes=60 * 1024 * 1024),
+        cost_estimate=pl.CostEstimate(flops=work, bytes_accessed=1 << 20, transcendentals=0),
+    )(inner_gate, values, decays)
     core, z, y = lax.axis_index("core"), lax.axis_index("z"), lax.axis_index("ylo")
-    came = lax.ppermute(send, "core", ring(2, 1))
+    came = move(send, "core", 1)
     mine = lax.dynamic_slice_in_dim(decays, core * HALF, HALF, 1)
     fade = jnp.exp(-mine * ROWS)
-    first = jnp.where(core == 0, keep, came)
-    chip = fade * first + jnp.where(core == 0, came, keep)
+    before = jnp.where(core == 0, keep, came)
+    chip = fade * before + jnp.where(core == 0, came, keep)
     everyone = lax.all_to_all(jnp.broadcast_to(chip[None], (16, MODES, HALF)), ("ylo", "z"), 0, 0)
+    first, late_inner, late_values = together(first, inner_gate, values)
     local = call(
-        taps_body, tiled, [tile_scratch], ROWS * CHANS * SUB, 1 << 20, inner_gate, values, residues, decays
+        taps_body, tiled, [tile_scratch], AHEAD, 1 << 20, late_inner, late_values, residues, decays
     )
+
+    first = first[None]
+    second, up, down = move(first, "ylo", 1), move(first, "z", 1), move(first, "z", -1)
+    everyone, second, up, down = together(everyone, second, up, down)
+    early, places = [first, second, up, down], [(0, 0), (1, 0), (0, 7), (0, 1)]
     place = y * 8 + z
     chip_fade = fade * fade
     state = jnp.zeros_like(chip)
     for k in range(15):
         state = jnp.where(k < place, state * chip_fade + everyone[k], state)
-    after = fade * state + first
+    after = fade * state + before
     near = jnp.where(core == 0, state, after)
-    far = lax.ppermute(jnp.where(core == 0, after, state), "core", ring(2, 1))
-    copies = jax.ShapeDtypeStruct((8, ROWS, CHANS), BF16)
+    far = move(jnp.where(core == 0, after, state), "core", 1)
     gated = call(
-        gate_body, copies, [tile_scratch, tile_scratch], work, 4 << 20,
+        gate_body, jax.ShapeDtypeStruct((1, ROWS, CHANS), BF16), [tile_scratch, tile_scratch], work, 2 << 20,
         outer_gate, sums, local, near, far, residues, decays,
     )
-    own = lax.all_to_all(gated, ("x", "yhi"), 0, 0)
-    other = lax.ppermute(own, "core", ring(2, 1))
-    part = jax.ShapeDtypeStruct((2, ROWS, 256), BF16)
-    kept, sent = call(
-        lambda *refs: project_body(places, *refs),
-        [part, part],
-        [pltpu.VMEM((2, 2, ROWS, 256), F32)],
-        2 * 512 * 512 * 4096, 10 << 20,
-        own, other, *blocks,
-    )
-    swapped = lax.ppermute(sent, "core", ring(2, 1))
-    even = jnp.where(core == 0, kept, swapped)
-    odd = jnp.where(core == 0, swapped, kept)
-    return jnp.concatenate([even[0], odd[0], even[1], odd[1]], axis=1)
+    side = move(gated, "yhi", 1)
+    up = move(jnp.concatenate([up, second], axis=0), "z", 1)
+    down = move(jnp.concatenate([down, second], axis=0), "z", -1)
+    side, up, down = together(side, up, down)
+    early, places = early + [up, down], places + [(0, 6), (1, 7), (0, 2), (1, 1)]
+
+    pair = jnp.concatenate([gated, side], axis=0)
+    pair_up, pair_down = move(pair, "x", 1), move(pair, "x", -1)
+    up, down = move(up, "z", 1), move(down, "z", -1)
+    pair_up, pair_down, up, down = together(pair_up, pair_down, up, down)
+    early, places = early + [up, down], places + [(0, 5), (1, 6), (0, 3), (1, 2)]
+
+    far_same, far_cross = move(pair_up[0], "x", 1), move(pair_down[1], "x", -1)
+    up, down = move(up, "z", 1), move(down[1:], "z", -1)
+    far_same, far_cross, up, down, *early = together(far_same, far_cross, up, down, *early)
+    last = move(up[:1], "ylo", 1)
+    early = bundle(early)
+    stacks, places = [early, up, down, last], places + [(0, 4), (1, 5), (1, 3), (1, 4)]
+    pieces = [v[dy] for v in (pair, pair_up, pair_down) for dy in range(2)] + [far_same, far_cross]
+    return project(places, pieces, stacks + [move(stack, "core", 1) for stack in stacks])
 
 
 def solution(mesh):

time: 149 us -> 100 us (0.67); the launches traced: 147 us -> 99.6 us
  blocking collectives: 33.1 us -> 0 us
  starting transfers between devices: 67.7 us -> 41.4 us
  waiting for transfers between devices: 28.2 us -> 38.3 us
  Pallas kernels: 7.69 us -> 12.8 us
  local copies, waits for them, and re-layouts: 8.18 us -> 5.96 us
    all_to_all x1 -> x0, blocking collectives: 33.1 us -> none  [shards(): own = lax.all_to_all(gated, ('x', 'yhi'), 0, 0)]
    ppermute x20 -> x22, starting transfers between devices: 60.1 us -> 34.3 us  [the longest x21 27 us: move(): lax.ppermute(value, axis, ring({'ylo': 2, 'z': 8, 'core': 2, 'x': 4, 'yhi...]
    ppermute x20 -> x22, waiting for transfers between devices: 23.3 us -> 37.3 us  [the longest x21 37.3 us: move(): lax.ppermute(value, axis, ring({'ylo': 2, 'z': 8, 'core': 2, 'x': 4, 'yhi...]
    pallas_call x0 -> x3, Pallas kernels: none -> 11.1 us  [the longest x1 6.43 us: project(): pl.pallas_call(lambda *refs: project_body(places, counts, *refs), out_sha...]
    pallas_call x4 -> x2, Pallas kernels: 7.69 us -> 1.7 us  [call(): pl.pallas_call(body, out_shape=outs, in_specs=whole(len(args)), out_specs...]
    all_to_all x1, waiting for transfers between devices: 4.93 us -> 1.03 us  [shards(): lax.all_to_all(jnp.broadcast_to(chip[None], (16, MODES, HALF)), ('ylo', '...]
    unnamed x26 -> x20, local copies, waits for them, and re-layouts: 7.41 us -> 5.12 us
  transfers between devices with their start and end apart: 21 -> 23, of which waited for: 12 -> 14; matrix products, arithmetic and copies ran while one was open for 0% -> 2% of each run, Pallas kernels for 0% -> 5%
where the time goes in v3:
time: 100 us; the launch traced here: 99.6 us
  starting transfers between devices  41.4 us (41%)
  waiting for transfers between devices  38.3 us (38%)
  Pallas kernels  12.8 us (13%)
  local copies, waits for them, and re-layouts  5.96 us (6%)
    ppermute x21, waiting for transfers between devices, move(): lax.ppermute(value, axis, ring({'ylo': 2, 'z': 8, 'core': 2, 'x': 4, 'yhi...  37.3 us
    ppermute x21, starting transfers between devices, move(): lax.ppermute(value, axis, ring({'ylo': 2, 'z': 8, 'core': 2, 'x': 4, 'yhi...  27 us
    ppermute x1, starting transfers between devices, swap(): return lax.ppermute(block, ('ylo', 'z', 'core', 'x', 'yhi'), pairs)  7.29 us
    all_to_all x1, starting transfers between devices, shards(): lax.all_to_all(jnp.broadcast_to(chip[None], (16, MODES, HALF)), ('ylo', '...  7.05 us
    pallas_call x1, Pallas kernels, project(): pl.pallas_call(lambda *refs: project_body(places, counts, *refs), out_sha...  6.43 us
    unnamed x20, local copies, waits for them, and re-layouts  5.12 us
    pallas_call x1, Pallas kernels, shards(): pl.pallas_call(sums_body, out_shape=[tiled, half, half], in_specs=[pl.Blo...  2.93 us
  transfers between devices with their start and end apart: 23, of which 14 were waited for; matrix products, arithmetic and copies ran while one was open for 2% of the time, Pallas kernels for 5%

profile of v3, /device:TPU:1, one launch (start us, length us, event | category | flops | bytes accessed | tf_op | source)
XLA Modules:
  0.0 99.6 jit_solution(4963894350998749301)
XLA Ops:
  0.0 7.3 %collective-permute-start = (bf16[512,256]{1,0:T(8,128)(2,1)}, bf16[512,256]{1,0:T(8,128)(2,1)S(1)}, u32[]{:S(2)}, u32[]{:S(2)}) collective-permute-start(bf16[512,256]{1,0:T(8,128)(2,1)} %param.11), channel_id=1, source_target_pairs={{0,80},{8,88},{16,64},{24,72},{32,241},{40,249},{48,225},{56,233},... | collective-permute-start | bytes 786440 | tf_op jit(solution)/shard_map/ppermute | solution.py:228
  7.3 2.9 %shard_map.64 = (f32[4,256,128]{2,1,0:T(8,128)}, f32[16,256]{1,0:T(8,128)}, f32[16,256]{1,0:T(8,128)}) custom-call(bf16[256,512]{1,0:T(8,128)(2,1)} %inner, bf16[256,512]{1,0:T(8,128)(2,1)} %values, f32[16,512]{1,0:T(8,128)} %decays.3), custom_call_target="tpu_custom_call" | custom-call | flops 4194304 | bytes 1048576 | tf_op jit(solution)/shard_map/pallas_call | solution.py:246
  13.8 7.0 %all-to-all-start = ((f32[16,16,256]{2,1,0:T(8,128)}), f32[16,16,256]{2,1,0:T(8,128)S(1)}, u32[]{:S(2)}, u32[]{:S(2)}) async-start(f32[16,16,256]{2,1,0:T(8,128)} %broadcast_in_dim.13), calls=%async_computation | async-start | bytes 524288 | tf_op jit(solution)/shard_map/all_to_all | solution.py:261
  20.9 2.7 %collective-permute-start.4 = (bf16[1,512,256]{2,1,0:T(8,128)(2,1)S(1)}, bf16[1,512,256]{2,1,0:T(8,128)(2,1)S(1)}, u32[]{:S(2)}, u32[]{:S(2)}) collective-permute-start(bf16[1,512,256]{2,1,0:T(8,128)(2,1)S(1)} %bitcast.116), channel_id=1, source_target_pairs={{0,112},{16,0},{32,16},{48,32},{64,48},{80,64},{96,80},{112,96},{1... | collective-permute-start | bytes 786440 | tf_op jit(solution)/shard_map/ppermute | solution.py:232
  23.5 1.2 %collective-permute-start.2 = (bf16[1,512,256]{2,1,0:T(8,128)(2,1)S(1)}, bf16[1,512,256]{2,1,0:T(8,128)(2,1)S(1)}, u32[]{:S(2)}, u32[]{:S(2)}) collective-permute-start(bf16[1,512,256]{2,1,0:T(8,128)(2,1)S(1)} %bitcast.118), channel_id=1, source_target_pairs={{0,128},{128,0},{1,129},{129,1},{2,130},{130,2},{3,131},{131,3},{4... | collective-permute-start | bytes 786440 | tf_op jit(solution)/shard_map/ppermute | solution.py:232
  29.8 4.1 %collective-permute-done.4.refs_3_ = bf16[1,512,256]{2,1,0:T(8,128)(2,1)S(1)} collective-permute-done((bf16[1,512,256]{2,1,0:T(8,128)(2,1)S(1)}, bf16[1,512,256]{2,1,0:T(8,128)(2,1)S(1)}, u32[]{:S(2)}, u32[]{:S(2)}) %collective-permute-start.4) | collective-permute-done | bytes 262176 | tf_op jit(solution)/shard_map/ppermute | solution.py:232
  33.9 1.6 %collective-permute-done.3.refs_2_ = bf16[1,512,256]{2,1,0:T(8,128)(2,1)S(1)} collective-permute-done((bf16[1,512,256]{2,1,0:T(8,128)(2,1)S(1)}, bf16[1,512,256]{2,1,0:T(8,128)(2,1)S(1)}, u32[]{:S(2)}, u32[]{:S(2)}) %collective-permute-start.3) | collective-permute-done | bytes 262176 | tf_op jit(solution)/shard_map/ppermute | solution.py:232
  37.2 1.7 %collective-permute-start.5 = (f32[16,256]{1,0:T(8,128)S(1)}, f32[16,256]{1,0:T(8,128)S(1)}, u32[]{:S(2)}, u32[]{:S(2)}) collective-permute-start(f32[16,256]{1,0:T(8,128)S(1)} %get-tuple-element.63), channel_id=1, source_target_pairs={{0,8},{8,0},{1,9},{9,1},{2,10},{10,2},{3,11},{11,3},{4,12},{12,4},... | collective-permute-start | bytes 49160 | tf_op jit(solution)/shard_map/ppermute | solution.py:232
  40.8 2.1 %collective-permute-start.6 = (bf16[1,256,512]{2,1,0:T(8,128)(2,1)S(1)}, bf16[1,256,512]{2,1,0:T(8,128)(2,1)S(1)}, u32[]{:S(2)}, u32[]{:S(2)}) collective-permute-start(bf16[1,256,512]{2,1,0:T(8,128)(2,1)S(1)} %shard_map.66), channel_id=1, source_target_pairs={{0,1},{1,0},{2,3},{3,2},{4,5},{5,4},{6,7},{7,6},{8,9},{9,8},{10,11... | collective-permute-start | bytes 786440 | tf_op jit(solution)/shard_map/ppermute | solution.py:232
  42.9 7.0 %collective-permute-done.6 = bf16[1,256,512]{2,1,0:T(8,128)(2,1)S(1)} collective-permute-done((bf16[1,256,512]{2,1,0:T(8,128)(2,1)S(1)}, bf16[1,256,512]{2,1,0:T(8,128)(2,1)S(1)}, u32[]{:S(2)}, u32[]{:S(2)}) %collective-permute-start.6) | collective-permute-done | bytes 262176 | tf_op jit(solution)/shard_map/ppermute | solution.py:232
  51.6 2.7 %collective-permute-start.12 = (bf16[2,512,256]{2,1,0:T(8,128)(2,1)S(1)}, bf16[2,512,256]{2,1,0:T(8,128)(2,1)S(1)}, u32[]{:S(2)}, u32[]{:S(2)}) collective-permute-start(bf16[2,512,256]{2,1,0:T(8,128)(2,1)S(1)} %collective-permute-done.8.refs_5_), channel_id=1, source_target_pairs={{0,112},{16,0},{32,16},{48,32},{64,48},{80,64},{96,80},{112,96},{1... | collective-permute-start | bytes 1572872 | tf_op jit(solution)/shard_map/ppermute | solution.py:232
  54.3 7.2 %collective-permute-done.10 = bf16[2,256,512]{2,1,0:T(8,128)(2,1)S(1)} collective-permute-done((bf16[2,256,512]{2,1,0:T(8,128)(2,1)S(1)}, bf16[2,256,512]{2,1,0:T(8,128)(2,1)S(1)}, u32[]{:S(2)}, u32[]{:S(2)}) %collective-permute-start.10) | collective-permute-done | bytes 524320 | tf_op jit(solution)/shard_map/ppermute | solution.py:232
  61.5 1.9 %collective-permute-done.9 = bf16[2,256,512]{2,1,0:T(8,128)(2,1)S(1)} collective-permute-done((bf16[2,256,512]{2,1,0:T(8,128)(2,1)S(1)}, bf16[2,256,512]{2,1,0:T(8,128)(2,1)S(1)}, u32[]{:S(2)}, u32[]{:S(2)}) %collective-permute-start.9) | collective-permute-done | bytes 524320 | tf_op jit(solution)/shard_map/ppermute | solution.py:232
  63.6 2.9 %collective-permute-start.15 = (bf16[2,512,256]{2,1,0:T(8,128)(2,1)S(1)}, bf16[2,512,256]{2,1,0:T(8,128)(2,1)S(1)}, u32[]{:S(2)}, u32[]{:S(2)}) collective-permute-start(bf16[2,512,256]{2,1,0:T(8,128)(2,1)S(1)} %collective-permute-done.11.refs_6_), channel_id=1, source_target_pairs={{0,16},{16,32},{32,48},{48,64},{64,80},{80,96},{96,112},{112,0},{1... | collective-permute-start | bytes 1572872 | tf_op jit(solution)/shard_map/ppermute | solution.py:232
  66.9 2.7 %collective-permute-start.14 = (bf16[256,512]{1,0:T(8,128)(2,1)S(1)}, bf16[256,512]{1,0:T(8,128)(2,1)S(1)}, u32[]{:S(2)}, u32[]{:S(2)}) collective-permute-start(bf16[256,512]{1,0:T(8,128)(2,1)S(1)} %get-tuple-element.65.refs_5_), channel_id=1, source_target_pairs={{0,6},{2,0},{4,2},{6,4},{1,7},{3,1},{5,3},{7,5},{8,14},{10,8},{12,... | collective-permute-start | bytes 786440 | tf_op jit(solution)/shard_map/ppermute | solution.py:232
  69.6 2.6 %collective-permute-done.16.refs_10_ = bf16[1,512,256]{2,1,0:T(8,128)(2,1)S(1)} collective-permute-done((bf16[1,512,256]{2,1,0:T(8,128)(2,1)S(1)}, bf16[1,512,256]{2,1,0:T(8,128)(2,1)S(1)}, u32[]{:S(2)}, u32[]{:S(2)}) %collective-permute-start.16) | collective-permute-done | bytes 262176 | tf_op jit(solution)/shard_map/ppermute | solution.py:232
  72.2 1.4 %collective-permute-done.13.refs_6_ = bf16[256,512]{1,0:T(8,128)(2,1)S(1)} collective-permute-done((bf16[256,512]{1,0:T(8,128)(2,1)S(1)}, bf16[256,512]{1,0:T(8,128)(2,1)S(1)}, u32[]{:S(2)}, u32[]{:S(2)}) %collective-permute-start.13) | collective-permute-done | bytes 262176 | tf_op jit(solution)/shard_map/ppermute | solution.py:232
  73.6 1.9 %collective-permute-done.15.refs_9_ = bf16[2,512,256]{2,1,0:T(8,128)(2,1)S(1)} collective-permute-done((bf16[2,512,256]{2,1,0:T(8,128)(2,1)S(1)}, bf16[2,512,256]{2,1,0:T(8,128)(2,1)S(1)}, u32[]{:S(2)}, u32[]{:S(2)}) %collective-permute-start.15) | collective-permute-done | bytes 524320 | tf_op jit(solution)/shard_map/ppermute | solution.py:232
  75.5 1.7 %shard_map.67.refs_8_ = bf16[12,512,256]{2,1,0:T(8,128)(2,1)} custom-call(bf16[1,512,256]{2,1,0:T(8,128)(2,1)S(1)} %bitcast.119, bf16[1,512,256]{2,1,0:T(8,128)(2,1)S(1)} %collective-permute-done.2.refs_1_, bf16[1,512,256]{2,1,0:T(8,128)(2,1)S(1)} %collective-permute-done.3.refs_2_, bf16[1,512,256]{2,1,0:T(8,128)(2,1)S(1)} %collective-permute-done.4.refs_3_, ...), custom_call_target="tpu_custom_call" | custom-call | bytes 6291456 | tf_op jit(solution)/shard_map/pallas_call | solution.py:155
  77.2 4.1 %collective-permute-start.18 = (bf16[12,512,256]{2,1,0:T(8,128)(2,1)}, bf16[12,512,256]{2,1,0:T(8,128)(2,1)S(1)}, u32[]{:S(2)}, u32[]{:S(2)}) collective-permute-start(bf16[12,512,256]{2,1,0:T(8,128)(2,1)} %shard_map.67.refs_8_), channel_id=1, source_target_pairs={{0,8},{8,0},{1,9},{9,1},{2,10},{10,2},{3,11},{11,3},{4,12},{12,4},... | collective-permute-start | bytes 9437192 | tf_op jit(solution)/shard_map/ppermute | solution.py:232
  81.4 1.3 %collective-permute-start.17 = (bf16[1,512,256]{2,1,0:T(8,128)(2,1)S(1)}, bf16[1,512,256]{2,1,0:T(8,128)(2,1)S(1)}, u32[]{:S(2)}, u32[]{:S(2)}) collective-permute-start(bf16[1,512,256]{2,1,0:T(8,128)(2,1)S(1)} %slice.85), channel_id=1, source_target_pairs={{0,128},{128,0},{1,129},{129,1},{2,130},{130,2},{3,131},{131,3},{4... | collective-permute-start | bytes 786440 | tf_op jit(solution)/shard_map/ppermute | solution.py:232
  83.2 6.2 %collective-permute-done.17.refs_11_ = bf16[1,512,256]{2,1,0:T(8,128)(2,1)S(1)} collective-permute-done((bf16[1,512,256]{2,1,0:T(8,128)(2,1)S(1)}, bf16[1,512,256]{2,1,0:T(8,128)(2,1)S(1)}, u32[]{:S(2)}, u32[]{:S(2)}) %collective-permute-start.17) | collective-permute-done | bytes 262176 | tf_op jit(solution)/shard_map/ppermute | solution.py:232
  91.4 1.7 %copy-done.8 = bf16[12,512,256]{2,1,0:T(8,128)(2,1)} copy-done((bf16[12,512,256]{2,1,0:T(8,128)(2,1)}, bf16[12,512,256]{2,1,0:T(8,128)(2,1)S(1)}, u32[]{:S(2)}) %copy-start.8) | copy-done | bytes 3145752
  93.0 6.4 %shard_map.68 = bf16[256,1024]{1,0:T(8,128)(2,1)} custom-call(bf16[256,512]{1,0:T(8,128)(2,1)S(1)} %bitcast.114, bf16[256,512]{1,0:T(8,128)(2,1)S(1)} %bitcast.115, bf16[256,512]{1,0:T(8,128)(2,1)S(1)} %get-tuple-element.68.refs_2_, bf16[256,512]{1,0:T(8,128)(2,1)S(1)} %get-tuple-element.67.refs_3_, bf16[256,512]{1,0:T(8,128)(2,1)S(1)} %get-tuple-element.66.refs_4_, ...), custom_call_target="tpu_custom_call" | custom-call | flops 2147483648 | bytes 10485760 | tf_op jit(solution)/shard_map/pallas_call | solution.py:198
  (57 shorter events, 16.8 us)
Async XLA Ops:
  0.0 20.9 %collective-permute-start = (bf16[512,256]{1,0:T(8,128)(2,1)}, bf16[512,256]{1,0:T(8,128)(2,1)S(1)}, u32[]{:S(2)}, u32[]{:S(2)}) collective-permute-start(bf16[512,256]{1,0:T(8,128)(2,1)} %param.11), channel_id=1, source_target_pairs={{0,80},{8,88},{16,64},{24,72},{32,241},{40,249},{48,225},{56,233},... | collective-permute-start | bytes 786440 | tf_op jit(solution)/shard_map/ppermute | solution.py:228
  10.2 2.1 %collective-permute-start.1 = (f32[16,256]{1,0:T(8,128)}, f32[16,256]{1,0:T(8,128)S(1)}, u32[]{:S(2)}, u32[]{:S(2)}) collective-permute-start(f32[16,256]{1,0:T(8,128)} %get-tuple-element.38), channel_id=1, source_target_pairs={{0,8},{8,0},{1,9},{9,1},{2,10},{10,2},{3,11},{11,3},{4,12},{12,4},... | collective-permute-start | bytes 49160 | tf_op jit(solution)/shard_map/ppermute | solution.py:232
  13.8 16.0 %all-to-all-start = ((f32[16,16,256]{2,1,0:T(8,128)}), f32[16,16,256]{2,1,0:T(8,128)S(1)}, u32[]{:S(2)}, u32[]{:S(2)}) async-start(f32[16,16,256]{2,1,0:T(8,128)} %broadcast_in_dim.13), calls=%async_computation | async-start | bytes 524288 | tf_op jit(solution)/shard_map/all_to_all | solution.py:261
  20.9 18.8 %copy-start = (f32[4,256,128]{2,1,0:T(8,128)S(1)}, f32[4,256,128]{2,1,0:T(8,128)}, u32[]{:S(2)}) copy-start(f32[4,256,128]{2,1,0:T(8,128)} %get-tuple-element.34.sums) | copy-start | bytes 1572868
  20.9 13.0 %collective-permute-start.4 = (bf16[1,512,256]{2,1,0:T(8,128)(2,1)S(1)}, bf16[1,512,256]{2,1,0:T(8,128)(2,1)S(1)}, u32[]{:S(2)}, u32[]{:S(2)}) collective-permute-start(bf16[1,512,256]{2,1,0:T(8,128)(2,1)S(1)} %bitcast.116), channel_id=1, source_target_pairs={{0,112},{16,0},{32,16},{48,32},{64,48},{80,64},{96,80},{112,96},{1... | collective-permute-start | bytes 786440 | tf_op jit(solution)/shard_map/ppermute | solution.py:232
  23.5 12.0 %collective-permute-start.3 = (bf16[1,512,256]{2,1,0:T(8,128)(2,1)S(1)}, bf16[1,512,256]{2,1,0:T(8,128)(2,1)S(1)}, u32[]{:S(2)}, u32[]{:S(2)}) collective-permute-start(bf16[1,512,256]{2,1,0:T(8,128)(2,1)S(1)} %bitcast.117), channel_id=1, source_target_pairs={{0,16},{16,32},{32,48},{48,64},{64,80},{80,96},{96,112},{112,0},{1... | collective-permute-start | bytes 786440 | tf_op jit(solution)/shard_map/ppermute | solution.py:232
  23.5 12.0 %collective-permute-start.2 = (bf16[1,512,256]{2,1,0:T(8,128)(2,1)S(1)}, bf16[1,512,256]{2,1,0:T(8,128)(2,1)S(1)}, u32[]{:S(2)}, u32[]{:S(2)}) collective-permute-start(bf16[1,512,256]{2,1,0:T(8,128)(2,1)S(1)} %bitcast.118), channel_id=1, source_target_pairs={{0,128},{128,0},{1,129},{129,1},{2,130},{130,2},{3,131},{131,3},{4... | collective-permute-start | bytes 786440 | tf_op jit(solution)/shard_map/ppermute | solution.py:232
  35.6 14.4 %collective-permute-start.8 = (bf16[2,512,256]{2,1,0:T(8,128)(2,1)S(1)}, bf16[2,512,256]{2,1,0:T(8,128)(2,1)S(1)}, u32[]{:S(2)}, u32[]{:S(2)}) collective-permute-start(bf16[2,512,256]{2,1,0:T(8,128)(2,1)S(1)} %get-tuple-element.69), channel_id=1, source_target_pairs={{0,112},{16,0},{32,16},{48,32},{64,48},{80,64},{96,80},{112,96},{1... | collective-permute-start | bytes 1572872 | tf_op jit(solution)/shard_map/ppermute | solution.py:232
  36.4 13.5 %collective-permute-start.7 = (bf16[2,512,256]{2,1,0:T(8,128)(2,1)S(1)}, bf16[2,512,256]{2,1,0:T(8,128)(2,1)S(1)}, u32[]{:S(2)}, u32[]{:S(2)}) collective-permute-start(bf16[2,512,256]{2,1,0:T(8,128)(2,1)S(1)} %get-tuple-element.70), channel_id=1, source_target_pairs={{0,16},{16,32},{32,48},{48,64},{64,80},{80,96},{96,112},{112,0},{1... | collective-permute-start | bytes 1572872 | tf_op jit(solution)/shard_map/ppermute | solution.py:232
  37.2 2.5 %collective-permute-start.5 = (f32[16,256]{1,0:T(8,128)S(1)}, f32[16,256]{1,0:T(8,128)S(1)}, u32[]{:S(2)}, u32[]{:S(2)}) collective-permute-start(f32[16,256]{1,0:T(8,128)S(1)} %get-tuple-element.63), channel_id=1, source_target_pairs={{0,8},{8,0},{1,9},{9,1},{2,10},{10,2},{3,11},{11,3},{4,12},{12,4},... | collective-permute-start | bytes 49160 | tf_op jit(solution)/shard_map/ppermute | solution.py:232
  40.8 9.1 %collective-permute-start.6 = (bf16[1,256,512]{2,1,0:T(8,128)(2,1)S(1)}, bf16[1,256,512]{2,1,0:T(8,128)(2,1)S(1)}, u32[]{:S(2)}, u32[]{:S(2)}) collective-permute-start(bf16[1,256,512]{2,1,0:T(8,128)(2,1)S(1)} %shard_map.66), channel_id=1, source_target_pairs={{0,1},{1,0},{2,3},{3,2},{4,5},{5,4},{6,7},{7,6},{8,9},{9,8},{10,11... | collective-permute-start | bytes 786440 | tf_op jit(solution)/shard_map/ppermute | solution.py:232
  50.0 11.5 %collective-permute-start.10 = (bf16[2,256,512]{2,1,0:T(8,128)(2,1)S(1)}, bf16[2,256,512]{2,1,0:T(8,128)(2,1)S(1)}, u32[]{:S(2)}, u32[]{:S(2)}) collective-permute-start(bf16[2,256,512]{2,1,0:T(8,128)(2,1)S(1)} %pad_maximum_fusion.2), channel_id=1, source_target_pairs={{0,6},{2,0},{4,2},{6,4},{1,7},{3,1},{5,3},{7,5},{8,14},{10,8},{12,... | collective-permute-start | bytes 1572872 | tf_op jit(solution)/shard_map/ppermute | solution.py:232
  51.1 12.3 %collective-permute-start.9 = (bf16[2,256,512]{2,1,0:T(8,128)(2,1)S(1)}, bf16[2,256,512]{2,1,0:T(8,128)(2,1)S(1)}, u32[]{:S(2)}, u32[]{:S(2)}) collective-permute-start(bf16[2,256,512]{2,1,0:T(8,128)(2,1)S(1)} %pad_maximum_fusion.2), channel_id=1, source_target_pairs={{0,2},{2,4},{4,6},{6,0},{1,3},{3,5},{5,7},{7,1},{8,10},{10,12},{12... | collective-permute-start | bytes 1572872 | tf_op jit(solution)/shard_map/ppermute | solution.py:232
  51.6 12.0 %collective-permute-start.11 = (bf16[2,512,256]{2,1,0:T(8,128)(2,1)S(1)}, bf16[2,512,256]{2,1,0:T(8,128)(2,1)S(1)}, u32[]{:S(2)}, u32[]{:S(2)}) collective-permute-start(bf16[2,512,256]{2,1,0:T(8,128)(2,1)S(1)} %collective-permute-done.7.refs_4_), channel_id=1, source_target_pairs={{0,16},{16,32},{32,48},{48,64},{64,80},{80,96},{96,112},{112,0},{1... | collective-permute-start | bytes 1572872 | tf_op jit(solution)/shard_map/ppermute | solution.py:232
  51.6 12.0 %collective-permute-start.12 = (bf16[2,512,256]{2,1,0:T(8,128)(2,1)S(1)}, bf16[2,512,256]{2,1,0:T(8,128)(2,1)S(1)}, u32[]{:S(2)}, u32[]{:S(2)}) collective-permute-start(bf16[2,512,256]{2,1,0:T(8,128)(2,1)S(1)} %collective-permute-done.8.refs_5_), channel_id=1, source_target_pairs={{0,112},{16,0},{32,16},{48,32},{64,48},{80,64},{96,80},{112,96},{1... | collective-permute-start | bytes 1572872 | tf_op jit(solution)/shard_map/ppermute | solution.py:232
  63.6 11.9 %collective-permute-start.15 = (bf16[2,512,256]{2,1,0:T(8,128)(2,1)S(1)}, bf16[2,512,256]{2,1,0:T(8,128)(2,1)S(1)}, u32[]{:S(2)}, u32[]{:S(2)}) collective-permute-start(bf16[2,512,256]{2,1,0:T(8,128)(2,1)S(1)} %collective-permute-done.11.refs_6_), channel_id=1, source_target_pairs={{0,16},{16,32},{32,48},{48,64},{64,80},{80,96},{96,112},{112,0},{1... | collective-permute-start | bytes 1572872 | tf_op jit(solution)/shard_map/ppermute | solution.py:232
  66.6 5.6 %collective-permute-start.16 = (bf16[1,512,256]{2,1,0:T(8,128)(2,1)S(1)}, bf16[1,512,256]{2,1,0:T(8,128)(2,1)S(1)}, u32[]{:S(2)}, u32[]{:S(2)}) collective-permute-start(bf16[1,512,256]{2,1,0:T(8,128)(2,1)S(1)} %slice.84), channel_id=1, source_target_pairs={{0,112},{16,0},{32,16},{48,32},{64,48},{80,64},{96,80},{112,96},{1... | collective-permute-start | bytes 786440 | tf_op jit(solution)/shard_map/ppermute | solution.py:232
  66.8 6.7 %collective-permute-start.13 = (bf16[256,512]{1,0:T(8,128)(2,1)S(1)}, bf16[256,512]{1,0:T(8,128)(2,1)S(1)}, u32[]{:S(2)}, u32[]{:S(2)}) collective-permute-start(bf16[256,512]{1,0:T(8,128)(2,1)S(1)} %get-tuple-element.68.refs_2_), channel_id=1, source_target_pairs={{0,2},{2,4},{4,6},{6,0},{1,3},{3,5},{5,7},{7,1},{8,10},{10,12},{12... | collective-permute-start | bytes 786440 | tf_op jit(solution)/shard_map/ppermute | solution.py:232
  66.9 6.7 %collective-permute-start.14 = (bf16[256,512]{1,0:T(8,128)(2,1)S(1)}, bf16[256,512]{1,0:T(8,128)(2,1)S(1)}, u32[]{:S(2)}, u32[]{:S(2)}) collective-permute-start(bf16[256,512]{1,0:T(8,128)(2,1)S(1)} %get-tuple-element.65.refs_5_), channel_id=1, source_target_pairs={{0,6},{2,0},{4,2},{6,4},{1,7},{3,1},{5,3},{7,5},{8,14},{10,8},{12,... | collective-permute-start | bytes 786440 | tf_op jit(solution)/shard_map/ppermute | solution.py:232
  77.2 14.1 %collective-permute-start.18 = (bf16[12,512,256]{2,1,0:T(8,128)(2,1)}, bf16[12,512,256]{2,1,0:T(8,128)(2,1)S(1)}, u32[]{:S(2)}, u32[]{:S(2)}) collective-permute-start(bf16[12,512,256]{2,1,0:T(8,128)(2,1)} %shard_map.67.refs_8_), channel_id=1, source_target_pairs={{0,8},{8,0},{1,9},{9,1},{2,10},{10,2},{3,11},{11,3},{4,12},{12,4},... | collective-permute-start | bytes 9437192 | tf_op jit(solution)/shard_map/ppermute | solution.py:232
  81.4 8.0 %collective-permute-start.17 = (bf16[1,512,256]{2,1,0:T(8,128)(2,1)S(1)}, bf16[1,512,256]{2,1,0:T(8,128)(2,1)S(1)}, u32[]{:S(2)}, u32[]{:S(2)}) collective-permute-start(bf16[1,512,256]{2,1,0:T(8,128)(2,1)S(1)} %slice.85), channel_id=1, source_target_pairs={{0,128},{128,0},{1,129},{129,1},{2,130},{130,2},{3,131},{131,3},{4... | collective-permute-start | bytes 786440 | tf_op jit(solution)/shard_map/ppermute | solution.py:232
  82.6 8.7 %collective-permute-start.19 = (bf16[2,512,256]{2,1,0:T(8,128)(2,1)S(1)}, bf16[2,512,256]{2,1,0:T(8,128)(2,1)S(1)}, u32[]{:S(2)}, u32[]{:S(2)}) collective-permute-start(bf16[2,512,256]{2,1,0:T(8,128)(2,1)S(1)} %collective-permute-done.15.refs_9_), channel_id=1, source_target_pairs={{0,8},{8,0},{1,9},{9,1},{2,10},{10,2},{3,11},{11,3},{4,12},{12,4},... | collective-permute-start | bytes 1572872 | tf_op jit(solution)/shard_map/ppermute | solution.py:232
  82.9 7.2 %collective-permute-start.20 = (bf16[1,512,256]{2,1,0:T(8,128)(2,1)S(1)}, bf16[1,512,256]{2,1,0:T(8,128)(2,1)S(1)}, u32[]{:S(2)}, u32[]{:S(2)}) collective-permute-start(bf16[1,512,256]{2,1,0:T(8,128)(2,1)S(1)} %collective-permute-done.16.refs_10_), channel_id=1, source_target_pairs={{0,8},{8,0},{1,9},{9,1},{2,10},{10,2},{3,11},{11,3},{4,12},{12,4},... | collective-permute-start | bytes 786440 | tf_op jit(solution)/shard_map/ppermute | solution.py:232
  89.4 2.0 %collective-permute-start.21 = (bf16[1,512,256]{2,1,0:T(8,128)(2,1)S(1)}, bf16[1,512,256]{2,1,0:T(8,128)(2,1)S(1)}, u32[]{:S(2)}, u32[]{:S(2)}) collective-permute-start(bf16[1,512,256]{2,1,0:T(8,128)(2,1)S(1)} %collective-permute-done.17.refs_11_), channel_id=1, source_target_pairs={{0,8},{8,0},{1,9},{9,1},{2,10},{10,2},{3,11},{11,3},{4,12},{12,4},... | collective-permute-start | bytes 786440 | tf_op jit(solution)/shard_map/ppermute | solution.py:232
  (9 other events, 46.2 us)

commit v4 on v3

--- a/solution.py
+++ b/solution.py
@@ -14,7 +14,7 @@
 TILES = CHANS // LANES
 HALF = CHANS // 2
 F32, BF16 = jnp.float32, jnp.bfloat16
-VMEM_LIMIT = 48 * 1024 * 1024
+VMEM_LIMIT = 24 * 1024 * 1024
 AHEAD = 10**11
 
 
@@ -41,13 +41,16 @@
         sig[lt] = product.astype(BF16).astype(F32)
 
 
+def load(sems, *pairs):
+    copies = [pltpu.make_async_copy(a, b, sems.at[i]) for i, (a, b) in enumerate(pairs)]
+    for copy in copies:
+        copy.start()
+    for copy in copies:
+        copy.wait()
+
+
 def sums_body(inner_hbm, values_hbm, decays_hbm, sums, keep, send, sig, inner, values, decays, sems):
-    pairs = ((decays_hbm, decays), (inner_hbm, inner), (values_hbm, values))
-    copies = [pltpu.make_async_copy(a, b, sems.at[i]) for i, (a, b) in enumerate(pairs)]
-    for copy in copies:
-        copy.start()
-    for copy in copies:
-        copy.wait()
+    load(sems, (decays_hbm, decays), (inner_hbm, inner), (values_hbm, values))
     signal_into(inner, values, sig)
     for lt in range(TILES):
         cols = slice(lt * LANES, (lt + 1) * LANES)
@@ -78,7 +81,8 @@
             send[:, place] = state
 
 
-def taps_body(inner, values, residues, decays, local, sig):
+def taps_body(inner_hbm, values_hbm, residues_hbm, decays_hbm, local, sig, inner, values, residues, decays, sems):
+    load(sems, (inner_hbm, inner), (values_hbm, values), (residues_hbm, residues), (decays_hbm, decays))
     signal_into(inner, values, sig)
     for lt in range(TILES):
         cols = slice(lt * LANES, (lt + 1) * LANES)
@@ -150,7 +154,7 @@
         copy.wait()
 
 
-def bundle(stacks):
+def bundle(stacks, cost=0):
     count = sum(stack.shape[0] for stack in stacks)
     return pl.pallas_call(
         bundle_body,
@@ -159,17 +163,20 @@
         out_specs=pl.BlockSpec(memory_space=pl.ANY),
         scratch_shapes=[pltpu.SemaphoreType.DMA((len(stacks),))],
         compiler_params=pltpu.CompilerParams(vmem_limit_bytes=VMEM_LIMIT),
-        cost_estimate=pl.CostEstimate(flops=0, bytes_accessed=count << 19, transcendentals=0),
+        cost_estimate=pl.CostEstimate(flops=cost, bytes_accessed=count << 19, transcendentals=0),
     )(*stacks)
 
 
 RANKS = [(dx, dy) for dx in (0, 3, 1, 2) for dy in range(2)]
+
+
+LAST = (1, 4)
 
 
 def project_body(places, counts, *refs):
     pieces, stacks = refs[:8], refs[8 : 8 + len(counts)]
-    result, gated, weight, row_sem, block_sem = refs[8 + len(counts) :]
-    x, yhi, core = lax.axis_index("x"), lax.axis_index("yhi"), lax.axis_index("core")
+    total, rows, gated, weight, row_sem, block_sem = refs[8 + len(counts) :]
+    x, yhi = lax.axis_index("x"), lax.axis_index("yhi")
     copies = []
     for i, (piece, (dx, dy)) in enumerate(zip(pieces, RANKS)):
         rank = lax.rem(x + dx, 4) * 2 + lax.rem(yhi + dy, 2)
@@ -178,37 +185,50 @@
     at = 0
     for stack, count in zip(stacks, counts):
         for i in range(count):
-            side, (group, odd) = at // 16, source_of(*places[at % 16])
+            side, (group, odd) = at // 15, source_of(*places[at % 15])
             columns = slice(side * 256, side * 256 + 256)
             copies.append(pltpu.make_async_copy(stack.at[i], weight.at[odd, group, :, columns], block_sem.at[at]))
             at += 1
     for copy in copies:
         copy.start()
+    group, odd = source_of(*LAST)
+    weight[odd, group] = jnp.zeros((512, 512), BF16)
     for copy in copies:
         copy.wait()
+    rows[...] = gated[:, pl.ds(pl.multiple_of(group * CHANS, CHANS), CHANS)]
     for odd in range(2):
-        total = jnp.dot(gated[...], weight[odd].reshape(8 * 512, 512), preferred_element_type=F32).astype(BF16)
-        own, other = total[:, :256], total[:, 256:]
-        result[:, odd * 512 : odd * 512 + 256] = jnp.where(core == 0, own, other)
-        result[:, odd * 512 + 256 : odd * 512 + 512] = jnp.where(core == 0, other, own)
+        total[odd] = jnp.dot(gated[...], weight[odd].reshape(8 * 512, 512), preferred_element_type=F32)
 
 
 def project(places, pieces, stacks):
     counts = [stack.shape[0] for stack in stacks]
     return pl.pallas_call(
         lambda *refs: project_body(places, counts, *refs),
-        out_shape=jax.ShapeDtypeStruct((ROWS, 1024), BF16),
+        out_shape=[jax.ShapeDtypeStruct((2, ROWS, 512), F32), jax.ShapeDtypeStruct((ROWS, CHANS), BF16)],
         in_specs=[pl.BlockSpec(memory_space=pl.ANY)] * (8 + len(stacks)),
-        out_specs=whole(1)[0],
+        out_specs=whole(2),
         scratch_shapes=[
             pltpu.VMEM((ROWS, 8 * CHANS), BF16),
             pltpu.VMEM((2, 8, 512, 512), BF16),
             pltpu.SemaphoreType.DMA((8,)),
-            pltpu.SemaphoreType.DMA((32,)),
+            pltpu.SemaphoreType.DMA((30,)),
         ],
         compiler_params=pltpu.CompilerParams(vmem_limit_bytes=VMEM_LIMIT),
         cost_estimate=pl.CostEstimate(flops=1 << 31, bytes_accessed=10 << 20, transcendentals=0),
     )(*pieces, *stacks)
+
+
+def finish_body(total, rows, own, other, result):
+    core = lax.axis_index("core")
+    _, odd = source_of(*LAST)
+    parts = [jnp.dot(rows[...], side[0], preferred_element_type=F32) for side in (own, other)]
+    for half in range(2):
+        mine, theirs = (
+            (total[half, :, i * 256 : i * 256 + 256] + jnp.where(odd == half, parts[i], 0.0)).astype(BF16)
+            for i in range(2)
+        )
+        result[:, half * 512 : half * 512 + 256] = jnp.where(core == 0, mine, theirs)
+        result[:, half * 512 + 256 : half * 512 + 512] = jnp.where(core == 0, theirs, mine)
 
 
 def ring(size, shift):
@@ -242,15 +262,16 @@
     half = jax.ShapeDtypeStruct((MODES, HALF), F32)
     tile_scratch = pltpu.VMEM((TILES, ROWS, LANES), F32)
     work = ROWS * CHANS * MODES * 2
-    shard = pltpu.VMEM((ROWS, CHANS), BF16)
+    shard, modes = pltpu.VMEM((ROWS, CHANS), BF16), pltpu.VMEM((MODES, CHANS), F32)
+    full = pltpu.CompilerParams(vmem_limit_bytes=60 * 1024 * 1024)
     sums, keep, send = pl.pallas_call(
         sums_body,
         out_shape=[tiled, half, half],
         in_specs=[pl.BlockSpec(memory_space=pl.ANY)] * 3,
         out_specs=whole(3),
-        scratch_shapes=[tile_scratch, shard, shard, pltpu.VMEM((MODES, CHANS), F32), pltpu.SemaphoreType.DMA((3,))],
-        compiler_params=pltpu.CompilerParams(vmem_limit_bytes=60 * 1024 * 1024),
-        cost_estimate=pl.CostEstimate(flops=work, bytes_accessed=1 << 20, transcendentals=0),
+        scratch_shapes=[tile_scratch, shard, shard, modes, pltpu.SemaphoreType.DMA((3,))],
+        compiler_params=full,
+        cost_estimate=pl.CostEstimate(flops=work, bytes_accessed=2 << 20, transcendentals=0),
     )(inner_gate, values, decays)
     core, z, y = lax.axis_index("core"), lax.axis_index("z"), lax.axis_index("ylo")
     came = move(send, "core", 1)
@@ -259,17 +280,21 @@
     before = jnp.where(core == 0, keep, came)
     chip = fade * before + jnp.where(core == 0, came, keep)
     everyone = lax.all_to_all(jnp.broadcast_to(chip[None], (16, MODES, HALF)), ("ylo", "z"), 0, 0)
-    first, late_inner, late_values = together(first, inner_gate, values)
-    local = call(
-        taps_body, tiled, [tile_scratch], AHEAD, 1 << 20, late_inner, late_values, residues, decays
-    )
-
+    first, late_inner = together(first, inner_gate)
+    local = pl.pallas_call(
+        taps_body,
+        out_shape=tiled,
+        in_specs=[pl.BlockSpec(memory_space=pl.ANY)] * 4,
+        out_specs=whole(1)[0],
+        scratch_shapes=[tile_scratch, shard, shard, modes, modes, pltpu.SemaphoreType.DMA((4,))],
+        compiler_params=full,
+        cost_estimate=pl.CostEstimate(flops=AHEAD, bytes_accessed=1 << 20, transcendentals=0),
+    )(late_inner, values, residues, decays)
+    chip_fade = fade * fade
     first = first[None]
-    second, up, down = move(first, "ylo", 1), move(first, "z", 1), move(first, "z", -1)
-    everyone, second, up, down = together(everyone, second, up, down)
-    early, places = [first, second, up, down], [(0, 0), (1, 0), (0, 7), (0, 1)]
+    second, up_a, down_a = move(first, "ylo", 1), move(first, "z", 1), move(first, "z", -1)
+    early, places = [first, second, up_a, down_a], [(0, 0), (1, 0), (0, 7), (0, 1)]
     place = y * 8 + z
-    chip_fade = fade * fade
     state = jnp.zeros_like(chip)
     for k in range(15):
         state = jnp.where(k < place, state * chip_fade + everyone[k], state)
@@ -280,26 +305,34 @@
         gate_body, jax.ShapeDtypeStruct((1, ROWS, CHANS), BF16), [tile_scratch, tile_scratch], work, 2 << 20,
         outer_gate, sums, local, near, far, residues, decays,
     )
+    gated, second, up_a, down_a = together(gated, second, up_a, down_a)
+    early = [first, second, up_a, down_a]
+    up_b, down_b = move(second, "z", 1), move(second, "z", -1)
+    up_a, down_a = move(up_a, "z", 1), move(down_a, "z", -1)
+    early, places = early + [up_a, up_b, down_a, down_b], places + [(0, 6), (1, 7), (0, 2), (1, 1)]
     side = move(gated, "yhi", 1)
-    up = move(jnp.concatenate([up, second], axis=0), "z", 1)
-    down = move(jnp.concatenate([down, second], axis=0), "z", -1)
-    side, up, down = together(side, up, down)
-    early, places = early + [up, down], places + [(0, 6), (1, 7), (0, 2), (1, 1)]
-
+    side, *early = together(side, *early)
+    early = bundle(early)
+
+    up_a, down_a = move(up_a, "z", 1), move(down_a, "z", -1)
+    up_b, down_b = move(up_b, "z", 1), move(down_b, "z", -1)
+    late, places = [up_a, down_a, up_b, down_b], places + [(0, 5), (0, 3), (1, 6), (1, 2)]
     pair = jnp.concatenate([gated, side], axis=0)
     pair_up, pair_down = move(pair, "x", 1), move(pair, "x", -1)
-    up, down = move(up, "z", 1), move(down, "z", -1)
-    pair_up, pair_down, up, down = together(pair_up, pair_down, up, down)
-    early, places = early + [up, down], places + [(0, 5), (1, 6), (0, 3), (1, 2)]
+    pair_up, pair_down, _, _, _, _, early = together(pair_up, pair_down, up_a, down_a, up_b, down_b, early)
 
     far_same, far_cross = move(pair_up[0], "x", 1), move(pair_down[1], "x", -1)
-    up, down = move(up, "z", 1), move(down[1:], "z", -1)
-    far_same, far_cross, up, down, *early = together(far_same, far_cross, up, down, *early)
-    last = move(up[:1], "ylo", 1)
-    early = bundle(early)
-    stacks, places = [early, up, down, last], places + [(0, 4), (1, 5), (1, 3), (1, 4)]
+    side_a, up_a, down_b = move(up_a, "ylo", 1), move(up_a, "z", 1), move(down_b, "z", -1)
+    last = move(up_a, "ylo", 1)
+    far_same, far_cross, up_a, side_a, down_b = together(far_same, far_cross, up_a, side_a, down_b)
+    late, places = bundle(late + [up_a, side_a, down_b], AHEAD), places + [(0, 4), (1, 5), (1, 3)]
     pieces = [v[dy] for v in (pair, pair_up, pair_down) for dy in range(2)] + [far_same, far_cross]
-    return project(places, pieces, stacks + [move(stack, "core", 1) for stack in stacks])
+    total, rows = project(places, pieces, [early, late, move(early, "core", 1), move(late, "core", 1)])
+    last, total = together(last, total)
+    return call(
+        finish_body, jax.ShapeDtypeStruct((ROWS, 1024), BF16), [], 1 << 27, 2 << 20,
+        total, rows, last, move(last, "core", 1),
+    )
 
 
 def solution(mesh):

time: 100 us -> 90 us (0.900)
  waiting for transfers between devices: 38.3 us -> 21.7 us
  starting transfers between devices: 41.4 us -> 53.4 us
  local copies, waits for them, and re-layouts: 5.96 us -> 1.91 us
  Pallas kernels: 12.8 us -> 11.7 us
    ppermute x21 -> x25, waiting for transfers between devices: 37.3 us -> 19.1 us  [move(): lax.ppermute(value, axis, ring({'ylo': 2, 'z': 8, 'core': 2, 'x': 4, 'yhi...]
    ppermute x21 -> x25, starting transfers between devices: 27 us -> 39.1 us  [move(): lax.ppermute(value, axis, ring({'ylo': 2, 'z': 8, 'core': 2, 'x': 4, 'yhi...]
    unnamed x20 -> x13, local copies, waits for them, and re-layouts: 5.12 us -> 1.09 us
    pallas_call x1, Pallas kernels: 6.43 us -> 3.61 us  [project(): pl.pallas_call(lambda *refs: project_body(places, counts, *refs), out_sha...]
    pallas_call x0 -> x1, Pallas kernels: none -> 2.44 us  [shards(): pl.pallas_call(taps_body, out_shape=tiled, in_specs=[pl.BlockSpec(memory_...]
    all_to_all x1, waiting for transfers between devices: 1.03 us -> 2.55 us  [shards(): lax.all_to_all(jnp.broadcast_to(chip[None], (16, MODES, HALF)), ('ylo', '...]
    pallas_call x1 -> x2, Pallas kernels: 1.7 us -> 0.43 us  [bundle(): pl.pallas_call(bundle_body, out_shape=jax.ShapeDtypeStruct((count, 512, 2...]
  transfers between devices with their start and end apart: 23 -> 27, of which waited for: 14 -> 12; matrix products, arithmetic and copies ran while one was open for 2% -> 2% of each run, Pallas kernels for 5% -> 12%
where the time goes in v4:
time: 90 us; the launch traced here: 89.7 us
  starting transfers between devices  53.4 us (59%)
  waiting for transfers between devices  21.7 us (24%)
  Pallas kernels  11.7 us (13%)
  local copies, waits for them, and re-layouts  1.91 us (2%)
    ppermute x25, starting transfers between devices, move(): lax.ppermute(value, axis, ring({'ylo': 2, 'z': 8, 'core': 2, 'x': 4, 'yhi...  39.1 us
    ppermute x25, waiting for transfers between devices, move(): lax.ppermute(value, axis, ring({'ylo': 2, 'z': 8, 'core': 2, 'x': 4, 'yhi...  19.1 us
    ppermute x1, starting transfers between devices, swap(): return lax.ppermute(block, ('ylo', 'z', 'core', 'x', 'yhi'), pairs)  7.29 us
    all_to_all x1, starting transfers between devices, shards(): lax.all_to_all(jnp.broadcast_to(chip[None], (16, MODES, HALF)), ('ylo', '...  7.05 us
    pallas_call x1, Pallas kernels, project(): pl.pallas_call(lambda *refs: project_body(places, counts, *refs), out_sha...  3.61 us
    pallas_call x1, Pallas kernels, shards(): pl.pallas_call(sums_body, out_shape=[tiled, half, half], in_specs=[pl.Blo...  2.93 us
    all_to_all x1, waiting for transfers between devices, shards(): lax.all_to_all(jnp.broadcast_to(chip[None], (16, MODES, HALF)), ('ylo', '...  2.55 us
    pallas_call x1, Pallas kernels, shards(): pl.pallas_call(taps_body, out_shape=tiled, in_specs=[pl.BlockSpec(memory_...  2.44 us
  transfers between devices with their start and end apart: 27, of which 12 were waited for; matrix products, arithmetic and copies ran while one was open for 2% of the time, Pallas kernels for 12%

profile of v4, /device:TPU:1, one launch (start us, length us, event | category | flops | bytes accessed | tf_op | source)
XLA Modules:
  0.0 89.7 jit_solution(10653289216115883739)
XLA Ops:
  0.0 7.3 %collective-permute-start = (bf16[512,256]{1,0:T(8,128)(2,1)}, bf16[512,256]{1,0:T(8,128)(2,1)S(1)}, u32[]{:S(2)}, u32[]{:S(2)}) collective-permute-start(bf16[512,256]{1,0:T(8,128)(2,1)} %param.11), channel_id=1, source_target_pairs={{0,80},{8,88},{16,64},{24,72},{32,241},{40,249},{48,225},{56,233},... | collective-permute-start | bytes 786440 | tf_op jit(solution)/shard_map/ppermute | solution.py:248
  7.3 2.9 %shard_map.64 = (f32[4,256,128]{2,1,0:T(8,128)}, f32[16,256]{1,0:T(8,128)}, f32[16,256]{1,0:T(8,128)}) custom-call(bf16[256,512]{1,0:T(8,128)(2,1)} %inner_hbm.2, bf16[256,512]{1,0:T(8,128)(2,1)} %values_hbm.3, f32[16,512]{1,0:T(8,128)} %decays.1), custom_call_target="tpu_custom_call" | custom-call | flops 4194304 | bytes 2097152 | tf_op jit(solution)/shard_map/pallas_call | solution.py:267
  13.8 7.0 %all-to-all-start = ((f32[16,16,256]{2,1,0:T(8,128)}), f32[16,16,256]{2,1,0:T(8,128)S(1)}, u32[]{:S(2)}, u32[]{:S(2)}) async-start(f32[16,16,256]{2,1,0:T(8,128)} %broadcast_in_dim.13), calls=%async_computation | async-start | bytes 524288 | tf_op jit(solution)/shard_map/all_to_all | solution.py:282
  20.9 2.7 %collective-permute-start.5 = (bf16[1,512,256]{2,1,0:T(8,128)(2,1)S(1)}, bf16[1,512,256]{2,1,0:T(8,128)(2,1)S(1)}, u32[]{:S(2)}, u32[]{:S(2)}) collective-permute-start(bf16[1,512,256]{2,1,0:T(8,128)(2,1)S(1)} %bitcast.146), channel_id=1, source_target_pairs={{0,112},{16,0},{32,16},{48,32},{64,48},{80,64},{96,80},{112,96},{1... | collective-permute-start | bytes 786440 | tf_op jit(solution)/shard_map/ppermute | solution.py:252
  24.8 2.4 %shard_map.65.local = f32[4,256,128]{2,1,0:T(8,128)} custom-call(bf16[256,512]{1,0:T(8,128)(2,1)} %inner_hbm.2, bf16[256,512]{1,0:T(8,128)(2,1)} %values_hbm.3, f32[16,512]{1,0:T(8,128)} %residues.1, f32[16,512]{1,0:T(8,128)} %decays.1), custom_call_target="tpu_custom_call" | custom-call | flops 99999997952 | bytes 1048576 | tf_op jit(solution)/shard_map/pallas_call | solution.py:284
  27.2 2.5 %all-to-all-done = f32[16,16,256]{2,1,0:T(8,128)S(1)} async-done(((f32[16,16,256]{2,1,0:T(8,128)}), f32[16,16,256]{2,1,0:T(8,128)S(1)}, u32[]{:S(2)}, u32[]{:S(2)}) %all-to-all-start) | async-done | bytes 262176 | tf_op jit(solution)/shard_map/all_to_all | solution.py:282
  29.8 3.4 %collective-permute-start.2 = (f32[16,256]{1,0:T(8,128)S(1)}, f32[16,256]{1,0:T(8,128)S(1)}, u32[]{:S(2)}, u32[]{:S(2)}) collective-permute-start(f32[16,256]{1,0:T(8,128)S(1)} %get-tuple-element.65), channel_id=1, source_target_pairs={{0,8},{8,0},{1,9},{9,1},{2,10},{10,2},{3,11},{11,3},{4,12},{12,4},... | collective-permute-start | bytes 49160 | tf_op jit(solution)/shard_map/ppermute | solution.py:252
  36.8 2.2 %collective-permute-start.12 = (bf16[1,512,256]{2,1,0:T(8,128)(2,1)S(1)}, bf16[1,512,256]{2,1,0:T(8,128)(2,1)S(1)}, u32[]{:S(2)}, u32[]{:S(2)}) collective-permute-start(bf16[1,512,256]{2,1,0:T(8,128)(2,1)S(1)} %collective-permute-done.5.refs_3_), channel_id=1, source_target_pairs={{0,112},{16,0},{32,16},{48,32},{64,48},{80,64},{96,80},{112,96},{1... | collective-permute-start | bytes 786440 | tf_op jit(solution)/shard_map/ppermute | solution.py:252
  39.0 2.0 %collective-permute-start.10 = (bf16[1,256,512]{2,1,0:T(8,128)(2,1)S(1)}, bf16[1,256,512]{2,1,0:T(8,128)(2,1)S(1)}, u32[]{:S(2)}, u32[]{:S(2)}) collective-permute-start(bf16[1,256,512]{2,1,0:T(8,128)(2,1)S(1)} %shard_map.66), channel_id=1, source_target_pairs={{0,1},{1,0},{2,3},{3,2},{4,5},{5,4},{6,7},{7,6},{8,9},{9,8},{10,11... | collective-permute-start | bytes 786440 | tf_op jit(solution)/shard_map/ppermute | solution.py:252
  42.5 2.6 %collective-permute-done.6.refs_4_ = bf16[1,512,256]{2,1,0:T(8,128)(2,1)S(1)} collective-permute-done((bf16[1,512,256]{2,1,0:T(8,128)(2,1)S(1)}, bf16[1,512,256]{2,1,0:T(8,128)(2,1)S(1)}, u32[]{:S(2)}, u32[]{:S(2)}) %collective-permute-start.6) | collective-permute-done | bytes 262176 | tf_op jit(solution)/shard_map/ppermute | solution.py:252
  45.1 2.3 %collective-permute-done.10 = bf16[1,256,512]{2,1,0:T(8,128)(2,1)S(1)} collective-permute-done((bf16[1,256,512]{2,1,0:T(8,128)(2,1)S(1)}, bf16[1,256,512]{2,1,0:T(8,128)(2,1)S(1)}, u32[]{:S(2)}, u32[]{:S(2)}) %collective-permute-start.10) | collective-permute-done | bytes 262176 | tf_op jit(solution)/shard_map/ppermute | solution.py:252
  47.4 2.3 %collective-permute-done.13.refs_7_ = bf16[1,512,256]{2,1,0:T(8,128)(2,1)S(1)} collective-permute-done((bf16[1,512,256]{2,1,0:T(8,128)(2,1)S(1)}, bf16[1,512,256]{2,1,0:T(8,128)(2,1)S(1)}, u32[]{:S(2)}, u32[]{:S(2)}) %collective-permute-start.13) | collective-permute-done | bytes 262176 | tf_op jit(solution)/shard_map/ppermute | solution.py:252
  52.4 2.4 %collective-permute-start.16 = (bf16[1,512,256]{2,1,0:T(8,128)(2,1)S(1)}, bf16[1,512,256]{2,1,0:T(8,128)(2,1)S(1)}, u32[]{:S(2)}, u32[]{:S(2)}) collective-permute-start(bf16[1,512,256]{2,1,0:T(8,128)(2,1)S(1)} %collective-permute-done.12.refs_6_), channel_id=1, source_target_pairs={{0,112},{16,0},{32,16},{48,32},{64,48},{80,64},{96,80},{112,96},{1... | collective-permute-start | bytes 786440 | tf_op jit(solution)/shard_map/ppermute | solution.py:252
  54.8 1.5 %collective-permute-start.18 = (bf16[1,512,256]{2,1,0:T(8,128)(2,1)S(1)}, bf16[1,512,256]{2,1,0:T(8,128)(2,1)S(1)}, u32[]{:S(2)}, u32[]{:S(2)}) collective-permute-start(bf16[1,512,256]{2,1,0:T(8,128)(2,1)S(1)} %collective-permute-done.13.refs_7_), channel_id=1, source_target_pairs={{0,112},{16,0},{32,16},{48,32},{64,48},{80,64},{96,80},{112,96},{1... | collective-permute-start | bytes 786440 | tf_op jit(solution)/shard_map/ppermute | solution.py:252
  56.3 1.6 %collective-permute-done.7.refs_0_ = bf16[1,512,256]{2,1,0:T(8,128)(2,1)S(1)} collective-permute-done((bf16[1,512,256]{2,1,0:T(8,128)(2,1)S(1)}, bf16[1,512,256]{2,1,0:T(8,128)(2,1)S(1)}, u32[]{:S(2)}, u32[]{:S(2)}) %collective-permute-start.7) | collective-permute-done | bytes 262176 | tf_op jit(solution)/shard_map/ppermute | solution.py:252
  58.1 1.6 %collective-permute-start.21 = (bf16[1,512,256]{2,1,0:T(8,128)(2,1)S(1)}, bf16[1,512,256]{2,1,0:T(8,128)(2,1)S(1)}, u32[]{:S(2)}, u32[]{:S(2)}) collective-permute-start(bf16[1,512,256]{2,1,0:T(8,128)(2,1)S(1)} %collective-permute-done.7.refs_0_), channel_id=1, source_target_pairs={{0,128},{128,0},{1,129},{129,1},{2,130},{130,2},{3,131},{131,3},{4... | collective-permute-start | bytes 786440 | tf_op jit(solution)/shard_map/ppermute | solution.py:252
  59.8 3.9 %collective-permute-done.18.refs_3_ = bf16[1,512,256]{2,1,0:T(8,128)(2,1)S(1)} collective-permute-done((bf16[1,512,256]{2,1,0:T(8,128)(2,1)S(1)}, bf16[1,512,256]{2,1,0:T(8,128)(2,1)S(1)}, u32[]{:S(2)}, u32[]{:S(2)}) %collective-permute-start.18) | collective-permute-done | bytes 262176 | tf_op jit(solution)/shard_map/ppermute | solution.py:252
  64.6 2.5 %collective-permute-start.22 = (bf16[1,512,256]{2,1,0:T(8,128)(2,1)S(1)}, bf16[1,512,256]{2,1,0:T(8,128)(2,1)S(1)}, u32[]{:S(2)}, u32[]{:S(2)}) collective-permute-start(bf16[1,512,256]{2,1,0:T(8,128)(2,1)S(1)} %collective-permute-done.18.refs_3_), channel_id=1, source_target_pairs={{0,112},{16,0},{32,16},{48,32},{64,48},{80,64},{96,80},{112,96},{1... | collective-permute-start | bytes 786440 | tf_op jit(solution)/shard_map/ppermute | solution.py:252
  67.3 2.7 %collective-permute-start.20 = (bf16[256,512]{1,0:T(8,128)(2,1)S(1)}, bf16[256,512]{1,0:T(8,128)(2,1)S(1)}, u32[]{:S(2)}, u32[]{:S(2)}) collective-permute-start(bf16[256,512]{1,0:T(8,128)(2,1)S(1)} %get-tuple-element.67.refs_5_), channel_id=1, source_target_pairs={{0,6},{2,0},{4,2},{6,4},{1,7},{3,1},{5,3},{7,5},{8,14},{10,8},{12,... | collective-permute-start | bytes 786440 | tf_op jit(solution)/shard_map/ppermute | solution.py:252
  70.0 4.1 %collective-permute-start.23 = (bf16[8,512,256]{2,1,0:T(8,128)(2,1)S(1)}, bf16[8,512,256]{2,1,0:T(8,128)(2,1)S(1)}, u32[]{:S(2)}, u32[]{:S(2)}) collective-permute-start(bf16[8,512,256]{2,1,0:T(8,128)(2,1)S(1)} %shard_map.67.refs_8_), channel_id=1, source_target_pairs={{0,8},{8,0},{1,9},{9,1},{2,10},{10,2},{3,11},{11,3},{4,12},{12,4},... | collective-permute-start | bytes 6291464 | tf_op jit(solution)/shard_map/ppermute | solution.py:252
  74.4 4.3 %collective-permute-start.24 = (bf16[7,512,256]{2,1,0:T(8,128)(2,1)S(1)}, bf16[7,512,256]{2,1,0:T(8,128)(2,1)S(1)}, u32[]{:S(2)}, u32[]{:S(2)}) collective-permute-start(bf16[7,512,256]{2,1,0:T(8,128)(2,1)S(1)} %shard_map.68.refs_9_), channel_id=1, source_target_pairs={{0,8},{8,0},{1,9},{9,1},{2,10},{10,2},{3,11},{11,3},{4,12},{12,4},... | collective-permute-start | bytes 5505032 | tf_op jit(solution)/shard_map/ppermute | solution.py:252
  78.6 1.3 %collective-permute-start.9 = (bf16[1,512,256]{2,1,0:T(8,128)(2,1)S(1)}, bf16[1,512,256]{2,1,0:T(8,128)(2,1)S(1)}, u32[]{:S(2)}, u32[]{:S(2)}) collective-permute-start(bf16[1,512,256]{2,1,0:T(8,128)(2,1)S(1)} %collective-permute-done.8.refs_4_), channel_id=1, source_target_pairs={{0,128},{128,0},{1,129},{129,1},{2,130},{130,2},{3,131},{131,3},{4... | collective-permute-start | bytes 786440 | tf_op jit(solution)/shard_map/ppermute | solution.py:252
  79.9 2.1 %collective-permute-done.24.refs_11_ = bf16[7,512,256]{2,1,0:T(8,128)(2,1)S(1)} collective-permute-done((bf16[7,512,256]{2,1,0:T(8,128)(2,1)S(1)}, bf16[7,512,256]{2,1,0:T(8,128)(2,1)S(1)}, u32[]{:S(2)}, u32[]{:S(2)}) %collective-permute-start.24) | collective-permute-done | bytes 1835040 | tf_op jit(solution)/shard_map/ppermute | solution.py:252
  82.1 3.6 %shard_map.69 = (f32[2,256,512]{2,1,0:T(8,128)S(1)}, bf16[256,512]{1,0:T(8,128)(2,1)S(1)}) custom-call(bf16[256,512]{1,0:T(8,128)(2,1)S(1)} %bitcast.144, bf16[256,512]{1,0:T(8,128)(2,1)S(1)} %bitcast.145, bf16[256,512]{1,0:T(8,128)(2,1)S(1)} %get-tuple-element.70.refs_2_, bf16[256,512]{1,0:T(8,128)(2,1)S(1)} %get-tuple-element.69.refs_3_, ...), custom_call_target="tpu_custom_call" | custom-call | flops 2147483648 | bytes 10485760 | tf_op jit(solution)/shard_map/pallas_call | solution.py:205
  (57 shorter events, 18.2 us)
Async XLA Ops:
  0.0 20.9 %collective-permute-start = (bf16[512,256]{1,0:T(8,128)(2,1)}, bf16[512,256]{1,0:T(8,128)(2,1)S(1)}, u32[]{:S(2)}, u32[]{:S(2)}) collective-permute-start(bf16[512,256]{1,0:T(8,128)(2,1)} %param.11), channel_id=1, source_target_pairs={{0,80},{8,88},{16,64},{24,72},{32,241},{40,249},{48,225},{56,233},... | collective-permute-start | bytes 786440 | tf_op jit(solution)/shard_map/ppermute | solution.py:248
  13.8 16.0 %all-to-all-start = ((f32[16,16,256]{2,1,0:T(8,128)}), f32[16,16,256]{2,1,0:T(8,128)S(1)}, u32[]{:S(2)}, u32[]{:S(2)}) async-start(f32[16,16,256]{2,1,0:T(8,128)} %broadcast_in_dim.13), calls=%async_computation | async-start | bytes 524288 | tf_op jit(solution)/shard_map/all_to_all | solution.py:282
  20.9 15.3 %collective-permute-start.5 = (bf16[1,512,256]{2,1,0:T(8,128)(2,1)S(1)}, bf16[1,512,256]{2,1,0:T(8,128)(2,1)S(1)}, u32[]{:S(2)}, u32[]{:S(2)}) collective-permute-start(bf16[1,512,256]{2,1,0:T(8,128)(2,1)S(1)} %bitcast.146), channel_id=1, source_target_pairs={{0,112},{16,0},{32,16},{48,32},{64,48},{80,64},{96,80},{112,96},{1... | collective-permute-start | bytes 786440 | tf_op jit(solution)/shard_map/ppermute | solution.py:252
  23.6 12.6 %collective-permute-start.4 = (bf16[1,512,256]{2,1,0:T(8,128)(2,1)S(1)}, bf16[1,512,256]{2,1,0:T(8,128)(2,1)S(1)}, u32[]{:S(2)}, u32[]{:S(2)}) collective-permute-start(bf16[1,512,256]{2,1,0:T(8,128)(2,1)S(1)} %bitcast.147), channel_id=1, source_target_pairs={{0,16},{16,32},{32,48},{48,64},{64,80},{80,96},{96,112},{112,0},{1... | collective-permute-start | bytes 786440 | tf_op jit(solution)/shard_map/ppermute | solution.py:252
  23.6 12.6 %collective-permute-start.3 = (bf16[1,512,256]{2,1,0:T(8,128)(2,1)S(1)}, bf16[1,512,256]{2,1,0:T(8,128)(2,1)S(1)}, u32[]{:S(2)}, u32[]{:S(2)}) collective-permute-start(bf16[1,512,256]{2,1,0:T(8,128)(2,1)S(1)} %bitcast.148), channel_id=1, source_target_pairs={{0,128},{128,0},{1,129},{129,1},{2,130},{130,2},{3,131},{131,3},{4... | collective-permute-start | bytes 786440 | tf_op jit(solution)/shard_map/ppermute | solution.py:252
  36.2 8.8 %collective-permute-start.6 = (bf16[1,512,256]{2,1,0:T(8,128)(2,1)S(1)}, bf16[1,512,256]{2,1,0:T(8,128)(2,1)S(1)}, u32[]{:S(2)}, u32[]{:S(2)}) collective-permute-start(bf16[1,512,256]{2,1,0:T(8,128)(2,1)S(1)} %collective-permute-done.4.refs_2_), channel_id=1, source_target_pairs={{0,16},{16,32},{32,48},{48,64},{64,80},{80,96},{96,112},{112,0},{1... | collective-permute-start | bytes 786440 | tf_op jit(solution)/shard_map/ppermute | solution.py:252
  36.8 8.2 %collective-permute-start.12 = (bf16[1,512,256]{2,1,0:T(8,128)(2,1)S(1)}, bf16[1,512,256]{2,1,0:T(8,128)(2,1)S(1)}, u32[]{:S(2)}, u32[]{:S(2)}) collective-permute-start(bf16[1,512,256]{2,1,0:T(8,128)(2,1)S(1)} %collective-permute-done.5.refs_3_), channel_id=1, source_target_pairs={{0,112},{16,0},{32,16},{48,32},{64,48},{80,64},{96,80},{112,96},{1... | collective-permute-start | bytes 786440 | tf_op jit(solution)/shard_map/ppermute | solution.py:252
  39.0 8.4 %collective-permute-start.10 = (bf16[1,256,512]{2,1,0:T(8,128)(2,1)S(1)}, bf16[1,256,512]{2,1,0:T(8,128)(2,1)S(1)}, u32[]{:S(2)}, u32[]{:S(2)}) collective-permute-start(bf16[1,256,512]{2,1,0:T(8,128)(2,1)S(1)} %shard_map.66), channel_id=1, source_target_pairs={{0,1},{1,0},{2,3},{3,2},{4,5},{5,4},{6,7},{7,6},{8,9},{9,8},{10,11... | collective-permute-start | bytes 786440 | tf_op jit(solution)/shard_map/ppermute | solution.py:252
  41.0 8.6 %collective-permute-start.13 = (bf16[1,512,256]{2,1,0:T(8,128)(2,1)S(1)}, bf16[1,512,256]{2,1,0:T(8,128)(2,1)S(1)}, u32[]{:S(2)}, u32[]{:S(2)}) collective-permute-start(bf16[1,512,256]{2,1,0:T(8,128)(2,1)S(1)} %collective-permute-done.3.refs_1_), channel_id=1, source_target_pairs={{0,112},{16,0},{32,16},{48,32},{64,48},{80,64},{96,80},{112,96},{1... | collective-permute-start | bytes 786440 | tf_op jit(solution)/shard_map/ppermute | solution.py:252
  41.9 7.8 %collective-permute-start.11 = (bf16[1,512,256]{2,1,0:T(8,128)(2,1)S(1)}, bf16[1,512,256]{2,1,0:T(8,128)(2,1)S(1)}, u32[]{:S(2)}, u32[]{:S(2)}) collective-permute-start(bf16[1,512,256]{2,1,0:T(8,128)(2,1)S(1)} %collective-permute-done.3.refs_1_), channel_id=1, source_target_pairs={{0,16},{16,32},{32,48},{48,64},{64,80},{80,96},{96,112},{112,0},{1... | collective-permute-start | bytes 786440 | tf_op jit(solution)/shard_map/ppermute | solution.py:252
  49.7 8.2 %collective-permute-start.7 = (bf16[1,512,256]{2,1,0:T(8,128)(2,1)S(1)}, bf16[1,512,256]{2,1,0:T(8,128)(2,1)S(1)}, u32[]{:S(2)}, u32[]{:S(2)}) collective-permute-start(bf16[1,512,256]{2,1,0:T(8,128)(2,1)S(1)} %collective-permute-done.6.refs_4_), channel_id=1, source_target_pairs={{0,16},{16,32},{32,48},{48,64},{64,80},{80,96},{96,112},{112,0},{1... | collective-permute-start | bytes 786440 | tf_op jit(solution)/shard_map/ppermute | solution.py:252
  50.7 16.4 %collective-permute-start.15 = (bf16[2,256,512]{2,1,0:T(8,128)(2,1)S(1)}, bf16[2,256,512]{2,1,0:T(8,128)(2,1)S(1)}, u32[]{:S(2)}, u32[]{:S(2)}) collective-permute-start(bf16[2,256,512]{2,1,0:T(8,128)(2,1)S(1)} %constant_dynamic-update-slice_fusion), channel_id=1, source_target_pairs={{0,6},{2,0},{4,2},{6,4},{1,7},{3,1},{5,3},{7,5},{8,14},{10,8},{12,... | collective-permute-start | bytes 1572872 | tf_op jit(solution)/shard_map/ppermute | solution.py:252
  51.9 15.2 %collective-permute-start.14 = (bf16[2,256,512]{2,1,0:T(8,128)(2,1)S(1)}, bf16[2,256,512]{2,1,0:T(8,128)(2,1)S(1)}, u32[]{:S(2)}, u32[]{:S(2)}) collective-permute-start(bf16[2,256,512]{2,1,0:T(8,128)(2,1)S(1)} %constant_dynamic-update-slice_fusion), channel_id=1, source_target_pairs={{0,2},{2,4},{4,6},{6,0},{1,3},{3,5},{5,7},{7,1},{8,10},{10,12},{12... | collective-permute-start | bytes 1572872 | tf_op jit(solution)/shard_map/ppermute | solution.py:252
  52.4 5.8 %collective-permute-start.16 = (bf16[1,512,256]{2,1,0:T(8,128)(2,1)S(1)}, bf16[1,512,256]{2,1,0:T(8,128)(2,1)S(1)}, u32[]{:S(2)}, u32[]{:S(2)}) collective-permute-start(bf16[1,512,256]{2,1,0:T(8,128)(2,1)S(1)} %collective-permute-done.12.refs_6_), channel_id=1, source_target_pairs={{0,112},{16,0},{32,16},{48,32},{64,48},{80,64},{96,80},{112,96},{1... | collective-permute-start | bytes 786440 | tf_op jit(solution)/shard_map/ppermute | solution.py:252
  54.8 8.9 %collective-permute-start.18 = (bf16[1,512,256]{2,1,0:T(8,128)(2,1)S(1)}, bf16[1,512,256]{2,1,0:T(8,128)(2,1)S(1)}, u32[]{:S(2)}, u32[]{:S(2)}) collective-permute-start(bf16[1,512,256]{2,1,0:T(8,128)(2,1)S(1)} %collective-permute-done.13.refs_7_), channel_id=1, source_target_pairs={{0,112},{16,0},{32,16},{48,32},{64,48},{80,64},{96,80},{112,96},{1... | collective-permute-start | bytes 786440 | tf_op jit(solution)/shard_map/ppermute | solution.py:252
  57.9 6.7 %collective-permute-start.17 = (bf16[1,512,256]{2,1,0:T(8,128)(2,1)S(1)}, bf16[1,512,256]{2,1,0:T(8,128)(2,1)S(1)}, u32[]{:S(2)}, u32[]{:S(2)}) collective-permute-start(bf16[1,512,256]{2,1,0:T(8,128)(2,1)S(1)} %collective-permute-done.11.refs_5_), channel_id=1, source_target_pairs={{0,16},{16,32},{32,48},{48,64},{64,80},{80,96},{96,112},{112,0},{1... | collective-permute-start | bytes 786440 | tf_op jit(solution)/shard_map/ppermute | solution.py:252
  58.1 11.9 %collective-permute-start.21 = (bf16[1,512,256]{2,1,0:T(8,128)(2,1)S(1)}, bf16[1,512,256]{2,1,0:T(8,128)(2,1)S(1)}, u32[]{:S(2)}, u32[]{:S(2)}) collective-permute-start(bf16[1,512,256]{2,1,0:T(8,128)(2,1)S(1)} %collective-permute-done.7.refs_0_), channel_id=1, source_target_pairs={{0,128},{128,0},{1,129},{129,1},{2,130},{130,2},{3,131},{131,3},{4... | collective-permute-start | bytes 786440 | tf_op jit(solution)/shard_map/ppermute | solution.py:252
  63.7 10.4 %collective-permute-start.8 = (bf16[1,512,256]{2,1,0:T(8,128)(2,1)S(1)}, bf16[1,512,256]{2,1,0:T(8,128)(2,1)S(1)}, u32[]{:S(2)}, u32[]{:S(2)}) collective-permute-start(bf16[1,512,256]{2,1,0:T(8,128)(2,1)S(1)} %collective-permute-done.7.refs_0_), channel_id=1, source_target_pairs={{0,16},{16,32},{32,48},{48,64},{64,80},{80,96},{96,112},{112,0},{1... | collective-permute-start | bytes 786440 | tf_op jit(solution)/shard_map/ppermute | solution.py:252
  64.6 9.5 %collective-permute-start.22 = (bf16[1,512,256]{2,1,0:T(8,128)(2,1)S(1)}, bf16[1,512,256]{2,1,0:T(8,128)(2,1)S(1)}, u32[]{:S(2)}, u32[]{:S(2)}) collective-permute-start(bf16[1,512,256]{2,1,0:T(8,128)(2,1)S(1)} %collective-permute-done.18.refs_3_), channel_id=1, source_target_pairs={{0,112},{16,0},{32,16},{48,32},{64,48},{80,64},{96,80},{112,96},{1... | collective-permute-start | bytes 786440 | tf_op jit(solution)/shard_map/ppermute | solution.py:252
  67.2 7.0 %collective-permute-start.19 = (bf16[256,512]{1,0:T(8,128)(2,1)S(1)}, bf16[256,512]{1,0:T(8,128)(2,1)S(1)}, u32[]{:S(2)}, u32[]{:S(2)}) collective-permute-start(bf16[256,512]{1,0:T(8,128)(2,1)S(1)} %get-tuple-element.70.refs_2_), channel_id=1, source_target_pairs={{0,2},{2,4},{4,6},{6,0},{1,3},{3,5},{5,7},{7,1},{8,10},{10,12},{12... | collective-permute-start | bytes 786440 | tf_op jit(solution)/shard_map/ppermute | solution.py:252
  67.3 6.8 %collective-permute-start.20 = (bf16[256,512]{1,0:T(8,128)(2,1)S(1)}, bf16[256,512]{1,0:T(8,128)(2,1)S(1)}, u32[]{:S(2)}, u32[]{:S(2)}) collective-permute-start(bf16[256,512]{1,0:T(8,128)(2,1)S(1)} %get-tuple-element.67.refs_5_), channel_id=1, source_target_pairs={{0,6},{2,0},{4,2},{6,4},{1,7},{3,1},{5,3},{7,5},{8,14},{10,8},{12,... | collective-permute-start | bytes 786440 | tf_op jit(solution)/shard_map/ppermute | solution.py:252
  70.0 12.0 %collective-permute-start.23 = (bf16[8,512,256]{2,1,0:T(8,128)(2,1)S(1)}, bf16[8,512,256]{2,1,0:T(8,128)(2,1)S(1)}, u32[]{:S(2)}, u32[]{:S(2)}) collective-permute-start(bf16[8,512,256]{2,1,0:T(8,128)(2,1)S(1)} %shard_map.67.refs_8_), channel_id=1, source_target_pairs={{0,8},{8,0},{1,9},{9,1},{2,10},{10,2},{3,11},{11,3},{4,12},{12,4},... | collective-permute-start | bytes 6291464 | tf_op jit(solution)/shard_map/ppermute | solution.py:252
  74.4 7.7 %collective-permute-start.24 = (bf16[7,512,256]{2,1,0:T(8,128)(2,1)S(1)}, bf16[7,512,256]{2,1,0:T(8,128)(2,1)S(1)}, u32[]{:S(2)}, u32[]{:S(2)}) collective-permute-start(bf16[7,512,256]{2,1,0:T(8,128)(2,1)S(1)} %shard_map.68.refs_9_), channel_id=1, source_target_pairs={{0,8},{8,0},{1,9},{9,1},{2,10},{10,2},{3,11},{11,3},{4,12},{12,4},... | collective-permute-start | bytes 5505032 | tf_op jit(solution)/shard_map/ppermute | solution.py:252
  78.6 7.9 %collective-permute-start.9 = (bf16[1,512,256]{2,1,0:T(8,128)(2,1)S(1)}, bf16[1,512,256]{2,1,0:T(8,128)(2,1)S(1)}, u32[]{:S(2)}, u32[]{:S(2)}) collective-permute-start(bf16[1,512,256]{2,1,0:T(8,128)(2,1)S(1)} %collective-permute-done.8.refs_4_), channel_id=1, source_target_pairs={{0,128},{128,0},{1,129},{129,1},{2,130},{130,2},{3,131},{131,3},{4... | collective-permute-start | bytes 786440 | tf_op jit(solution)/shard_map/ppermute | solution.py:252
  (9 other events, 66.5 us)

commit v5 on v4

--- a/solution.py
+++ b/solution.py
@@ -170,65 +170,69 @@
 RANKS = [(dx, dy) for dx in (0, 3, 1, 2) for dy in range(2)]
 
 
-LAST = (1, 4)
-
-
-def project_body(places, counts, *refs):
-    pieces, stacks = refs[:8], refs[8 : 8 + len(counts)]
-    total, rows, gated, weight, row_sem, block_sem = refs[8 + len(counts) :]
+def column_sums(places, stacks, gated, weight, sems):
+    copies = []
+    for stack in stacks:
+        for i in range(stack.shape[0]):
+            at = len(copies)
+            group, odd = source_of(*places[at])
+            copies.append(pltpu.make_async_copy(stack.at[i], weight.at[odd, group], sems.at[at]))
+    for copy in copies:
+        copy.start()
+    for copy in copies:
+        copy.wait()
+    return [jnp.dot(gated[...], weight[odd].reshape(8 * 512, 256), preferred_element_type=F32) for odd in range(2)]
+
+
+def own_body(places, count, *refs):
+    pieces, stacks = refs[:8], refs[8 : 8 + count]
+    total, gated, weight, row_sem, block_sem = refs[8 + count :]
     x, yhi = lax.axis_index("x"), lax.axis_index("yhi")
     copies = []
     for i, (piece, (dx, dy)) in enumerate(zip(pieces, RANKS)):
         rank = lax.rem(x + dx, 4) * 2 + lax.rem(yhi + dy, 2)
         columns = pl.ds(pl.multiple_of(rank * CHANS, CHANS), CHANS)
         copies.append(pltpu.make_async_copy(piece, gated.at[:, columns], row_sem.at[i]))
-    at = 0
-    for stack, count in zip(stacks, counts):
-        for i in range(count):
-            side, (group, odd) = at // 15, source_of(*places[at % 15])
-            columns = slice(side * 256, side * 256 + 256)
-            copies.append(pltpu.make_async_copy(stack.at[i], weight.at[odd, group, :, columns], block_sem.at[at]))
-            at += 1
     for copy in copies:
         copy.start()
-    group, odd = source_of(*LAST)
-    weight[odd, group] = jnp.zeros((512, 512), BF16)
     for copy in copies:
         copy.wait()
-    rows[...] = gated[:, pl.ds(pl.multiple_of(group * CHANS, CHANS), CHANS)]
-    for odd in range(2):
-        total[odd] = jnp.dot(gated[...], weight[odd].reshape(8 * 512, 512), preferred_element_type=F32)
-
-
-def project(places, pieces, stacks):
-    counts = [stack.shape[0] for stack in stacks]
+    total[0], total[1] = column_sums(places, stacks, gated, weight, block_sem)
+
+
+def other_body(places, count, *refs):
+    total, gated, stacks = refs[0], refs[1], refs[2 : 2 + count]
+    result, weight, block_sem = refs[2 + count :]
+    core = lax.axis_index("core")
+    for odd, theirs in enumerate(column_sums(places, stacks, gated, weight, block_sem)):
+        mine, theirs = total[odd].astype(BF16), theirs.astype(BF16)
+        result[:, odd * 512 : odd * 512 + 256] = jnp.where(core == 0, mine, theirs)
+        result[:, odd * 512 + 256 : odd * 512 + 512] = jnp.where(core == 0, theirs, mine)
+
+
+def project(places, pieces, own, other):
+    blocks = [pltpu.VMEM((2, 8, 512, 256), BF16)]
+    sems = [pltpu.SemaphoreType.DMA((16,))]
+    params = pltpu.CompilerParams(vmem_limit_bytes=VMEM_LIMIT)
+    cost = pl.CostEstimate(flops=1 << 30, bytes_accessed=6 << 20, transcendentals=0)
+    total, gated = pl.pallas_call(
+        lambda *refs: own_body(places, len(own), *refs),
+        out_shape=[jax.ShapeDtypeStruct((2, ROWS, 256), F32), jax.ShapeDtypeStruct((ROWS, 8 * CHANS), BF16)],
+        in_specs=[pl.BlockSpec(memory_space=pl.ANY)] * (8 + len(own)),
+        out_specs=whole(2),
+        scratch_shapes=blocks + [pltpu.SemaphoreType.DMA((8,))] + sems,
+        compiler_params=params,
+        cost_estimate=cost,
+    )(*pieces, *own)
     return pl.pallas_call(
-        lambda *refs: project_body(places, counts, *refs),
-        out_shape=[jax.ShapeDtypeStruct((2, ROWS, 512), F32), jax.ShapeDtypeStruct((ROWS, CHANS), BF16)],
-        in_specs=[pl.BlockSpec(memory_space=pl.ANY)] * (8 + len(stacks)),
-        out_specs=whole(2),
-        scratch_shapes=[
-            pltpu.VMEM((ROWS, 8 * CHANS), BF16),
-            pltpu.VMEM((2, 8, 512, 512), BF16),
-            pltpu.SemaphoreType.DMA((8,)),
-            pltpu.SemaphoreType.DMA((30,)),
-        ],
-        compiler_params=pltpu.CompilerParams(vmem_limit_bytes=VMEM_LIMIT),
-        cost_estimate=pl.CostEstimate(flops=1 << 31, bytes_accessed=10 << 20, transcendentals=0),
-    )(*pieces, *stacks)
-
-
-def finish_body(total, rows, own, other, result):
-    core = lax.axis_index("core")
-    _, odd = source_of(*LAST)
-    parts = [jnp.dot(rows[...], side[0], preferred_element_type=F32) for side in (own, other)]
-    for half in range(2):
-        mine, theirs = (
-            (total[half, :, i * 256 : i * 256 + 256] + jnp.where(odd == half, parts[i], 0.0)).astype(BF16)
-            for i in range(2)
-        )
-        result[:, half * 512 : half * 512 + 256] = jnp.where(core == 0, mine, theirs)
-        result[:, half * 512 + 256 : half * 512 + 512] = jnp.where(core == 0, theirs, mine)
+        lambda *refs: other_body(places, len(other), *refs),
+        out_shape=jax.ShapeDtypeStruct((ROWS, 1024), BF16),
+        in_specs=whole(2) + [pl.BlockSpec(memory_space=pl.ANY)] * len(other),
+        out_specs=whole(1)[0],
+        scratch_shapes=blocks + sems,
+        compiler_params=params,
+        cost_estimate=cost,
+    )(total, gated, *other)
 
 
 def ring(size, shift):
@@ -287,7 +291,7 @@
         in_specs=[pl.BlockSpec(memory_space=pl.ANY)] * 4,
         out_specs=whole(1)[0],
         scratch_shapes=[tile_scratch, shard, shard, modes, modes, pltpu.SemaphoreType.DMA((4,))],
-        compiler_params=full,
+        compiler_params=pltpu.CompilerParams(vmem_limit_bytes=VMEM_LIMIT),
         cost_estimate=pl.CostEstimate(flops=AHEAD, bytes_accessed=1 << 20, transcendentals=0),
     )(late_inner, values, residues, decays)
     chip_fade = fade * fade
@@ -302,37 +306,34 @@
     near = jnp.where(core == 0, state, after)
     far = move(jnp.where(core == 0, after, state), "core", 1)
     gated = call(
-        gate_body, jax.ShapeDtypeStruct((1, ROWS, CHANS), BF16), [tile_scratch, tile_scratch], work, 2 << 20,
+        gate_body, jax.ShapeDtypeStruct((1, ROWS, CHANS), BF16), [tile_scratch, tile_scratch], 0, 0,
         outer_gate, sums, local, near, far, residues, decays,
     )
     gated, second, up_a, down_a = together(gated, second, up_a, down_a)
     early = [first, second, up_a, down_a]
-    up_b, down_b = move(second, "z", 1), move(second, "z", -1)
+    near_b = [move(second, "z", 1), move(second, "z", -1)]
     up_a, down_a = move(up_a, "z", 1), move(down_a, "z", -1)
-    early, places = early + [up_a, up_b, down_a, down_b], places + [(0, 6), (1, 7), (0, 2), (1, 1)]
+    early, places = early + [up_a, down_a], places + [(0, 6), (0, 2)]
     side = move(gated, "yhi", 1)
     side, *early = together(side, *early)
     early = bundle(early)
 
+    up_b, down_b = move(up_a, "ylo", 1), move(down_a, "ylo", 1)
     up_a, down_a = move(up_a, "z", 1), move(down_a, "z", -1)
-    up_b, down_b = move(up_b, "z", 1), move(down_b, "z", -1)
-    late, places = [up_a, down_a, up_b, down_b], places + [(0, 5), (0, 3), (1, 6), (1, 2)]
+    opposite = move(up_a, "z", 1)
+    middle, places = [up_a, down_a, up_b, down_b, opposite], places + [(0, 5), (0, 3), (1, 6), (1, 2), (0, 4)]
+    middle, places = middle + near_b, places + [(1, 7), (1, 1)]
     pair = jnp.concatenate([gated, side], axis=0)
     pair_up, pair_down = move(pair, "x", 1), move(pair, "x", -1)
-    pair_up, pair_down, _, _, _, _, early = together(pair_up, pair_down, up_a, down_a, up_b, down_b, early)
+    pair_up, pair_down, early, *middle = together(pair_up, pair_down, early, *middle)
 
     far_same, far_cross = move(pair_up[0], "x", 1), move(pair_down[1], "x", -1)
-    side_a, up_a, down_b = move(up_a, "ylo", 1), move(up_a, "z", 1), move(down_b, "z", -1)
-    last = move(up_a, "ylo", 1)
-    far_same, far_cross, up_a, side_a, down_b = together(far_same, far_cross, up_a, side_a, down_b)
-    late, places = bundle(late + [up_a, side_a, down_b], AHEAD), places + [(0, 4), (1, 5), (1, 3)]
+    late = [move(up_b, "z", 1), move(down_b, "z", -1), move(opposite, "ylo", 1)]
+    places += [(1, 5), (1, 3), (1, 4)]
+    far_same, far_cross, *late = together(far_same, far_cross, *late)
     pieces = [v[dy] for v in (pair, pair_up, pair_down) for dy in range(2)] + [far_same, far_cross]
-    total, rows = project(places, pieces, [early, late, move(early, "core", 1), move(late, "core", 1)])
-    last, total = together(last, total)
-    return call(
-        finish_body, jax.ShapeDtypeStruct((ROWS, 1024), BF16), [], 1 << 27, 2 << 20,
-        total, rows, last, move(last, "core", 1),
-    )
+    stacks = [early, bundle(middle + late)]
+    return project(places, pieces, stacks, [move(stack, "core", 1) for stack in stacks])
 
 
 def solution(mesh):

time: 90 us -> 86.7 us (0.963)
  starting transfers between devices: 53.4 us -> 48.7 us
  local copies, waits for them, and re-layouts: 1.91 us -> 4.28 us
  Pallas kernels: 11.7 us -> 9.88 us
    ppermute x25 -> x24, starting transfers between devices: 39.1 us -> 34.3 us  [move(): lax.ppermute(value, axis, ring({'ylo': 2, 'z': 8, 'core': 2, 'x': 4, 'yhi...]
    unnamed x13 -> x19, local copies, waits for them, and re-layouts: 1.09 us -> 3.45 us
    ppermute x25 -> x24, waiting for transfers between devices: 19.1 us -> 21.4 us  [move(): lax.ppermute(value, axis, ring({'ylo': 2, 'z': 8, 'core': 2, 'x': 4, 'yhi...]
    pallas_call x1, Pallas kernels: 2.44 us -> 0.74 us  [shards(): pl.pallas_call(taps_body, out_shape=tiled, in_specs=[pl.BlockSpec(memory_...]
    all_to_all x1, waiting for transfers between devices: 2.55 us -> 0.86 us  [shards(): lax.all_to_all(jnp.broadcast_to(chip[None], (16, MODES, HALF)), ('ylo', '...]
    pallas_call x2 -> x1, Pallas kernels: 2.27 us -> 1.12 us  [call(): pl.pallas_call(body, out_shape=outs, in_specs=whole(len(args)), out_specs...]
    pallas_call x1 -> x2, Pallas kernels: 3.61 us -> 4.64 us  [the longest x1 2.55 us: project(): pl.pallas_call(lambda *refs: other_body(places, len(other), *refs), out_s...]
  transfers between devices with their start and end apart: 27 -> 26, of which waited for: 12 -> 18; matrix products, arithmetic and copies ran while one was open for 2% -> 2% of each run, Pallas kernels for 12% -> 8%
where the time goes in v5:
time: 86.7 us; the launch traced here: 86.2 us
  starting transfers between devices  48.7 us (56%)
  waiting for transfers between devices  22.2 us (26%)
  Pallas kernels  9.88 us (11%)
  local copies, waits for them, and re-layouts  4.28 us (5%)
    ppermute x24, starting transfers between devices, move(): lax.ppermute(value, axis, ring({'ylo': 2, 'z': 8, 'core': 2, 'x': 4, 'yhi...  34.3 us
    ppermute x24, waiting for transfers between devices, move(): lax.ppermute(value, axis, ring({'ylo': 2, 'z': 8, 'core': 2, 'x': 4, 'yhi...  21.4 us
    ppermute x1, starting transfers between devices, swap(): return lax.ppermute(block, ('ylo', 'z', 'core', 'x', 'yhi'), pairs)  7.29 us
    all_to_all x1, starting transfers between devices, shards(): lax.all_to_all(jnp.broadcast_to(chip[None], (16, MODES, HALF)), ('ylo', '...  7.05 us
    unnamed x19, local copies, waits for them, and re-layouts  3.45 us
    pallas_call x1, Pallas kernels, shards(): pl.pallas_call(sums_body, out_shape=[tiled, half, half], in_specs=[pl.Blo...  2.93 us
    pallas_call x1, Pallas kernels, project(): pl.pallas_call(lambda *refs: other_body(places, len(other), *refs), out_s...  2.55 us
    pallas_call x1, Pallas kernels, project(): pl.pallas_call(lambda *refs: own_body(places, len(own), *refs), out_shape...  2.08 us
  transfers between devices with their start and end apart: 26, of which 18 were waited for; matrix products, arithmetic and copies ran while one was open for 2% of the time, Pallas kernels for 8%

profile of v5, /device:TPU:1, one launch (start us, length us, event | category | flops | bytes accessed | tf_op | source)
XLA Modules:
  0.0 86.2 jit_solution(12088039881233763876)
XLA Ops:
  0.0 7.3 %collective-permute-start = (bf16[512,256]{1,0:T(8,128)(2,1)}, bf16[512,256]{1,0:T(8,128)(2,1)S(1)}, u32[]{:S(2)}, u32[]{:S(2)}) collective-permute-start(bf16[512,256]{1,0:T(8,128)(2,1)} %param.11), channel_id=1, source_target_pairs={{0,80},{8,88},{16,64},{24,72},{32,241},{40,249},{48,225},{56,233},... | collective-permute-start | bytes 786440 | tf_op jit(solution)/shard_map/ppermute | solution.py:252
  7.3 2.9 %shard_map.64 = (f32[4,256,128]{2,1,0:T(8,128)}, f32[16,256]{1,0:T(8,128)}, f32[16,256]{1,0:T(8,128)}) custom-call(bf16[256,512]{1,0:T(8,128)(2,1)} %inner_hbm.2, bf16[256,512]{1,0:T(8,128)(2,1)} %values_hbm.3, f32[16,512]{1,0:T(8,128)} %decays.1), custom_call_target="tpu_custom_call" | custom-call | flops 4194304 | bytes 2097152 | tf_op jit(solution)/shard_map/pallas_call | solution.py:271
  11.3 1.0 %collective-permute-done.1 = f32[16,256]{1,0:T(8,128)S(1)} collective-permute-done((f32[16,256]{1,0:T(8,128)}, f32[16,256]{1,0:T(8,128)S(1)}, u32[]{:S(2)}, u32[]{:S(2)}) %collective-permute-start.1) | collective-permute-done | bytes 16416 | tf_op jit(solution)/shard_map/ppermute | solution.py:256
  13.8 7.0 %all-to-all-start = ((f32[16,16,256]{2,1,0:T(8,128)}), f32[16,16,256]{2,1,0:T(8,128)S(1)}, u32[]{:S(2)}, u32[]{:S(2)}) async-start(f32[16,16,256]{2,1,0:T(8,128)} %broadcast_in_dim.13), calls=%async_computation | async-start | bytes 524288 | tf_op jit(solution)/shard_map/all_to_all | solution.py:286
  20.9 2.7 %collective-permute-start.5 = (bf16[1,512,256]{2,1,0:T(8,128)(2,1)S(1)}, bf16[1,512,256]{2,1,0:T(8,128)(2,1)S(1)}, u32[]{:S(2)}, u32[]{:S(2)}) collective-permute-start(bf16[1,512,256]{2,1,0:T(8,128)(2,1)S(1)} %bitcast.146), channel_id=1, source_target_pairs={{0,112},{16,0},{32,16},{48,32},{64,48},{80,64},{96,80},{112,96},{1... | collective-permute-start | bytes 786440 | tf_op jit(solution)/shard_map/ppermute | solution.py:256
  23.5 1.2 %collective-permute-start.3 = (bf16[1,512,256]{2,1,0:T(8,128)(2,1)S(1)}, bf16[1,512,256]{2,1,0:T(8,128)(2,1)S(1)}, u32[]{:S(2)}, u32[]{:S(2)}) collective-permute-start(bf16[1,512,256]{2,1,0:T(8,128)(2,1)S(1)} %bitcast.148), channel_id=1, source_target_pairs={{0,128},{128,0},{1,129},{129,1},{2,130},{130,2},{3,131},{131,3},{4... | collective-permute-start | bytes 786440 | tf_op jit(solution)/shard_map/ppermute | solution.py:256
  29.8 3.4 %collective-permute-start.2 = (f32[16,256]{1,0:T(8,128)S(1)}, f32[16,256]{1,0:T(8,128)S(1)}, u32[]{:S(2)}, u32[]{:S(2)}) collective-permute-start(f32[16,256]{1,0:T(8,128)S(1)} %get-tuple-element.71), channel_id=1, source_target_pairs={{0,8},{8,0},{1,9},{9,1},{2,10},{10,2},{3,11},{11,3},{4,12},{12,4},... | collective-permute-start | bytes 49160 | tf_op jit(solution)/shard_map/ppermute | solution.py:256
  34.0 1.1 %shard_map.66 = bf16[1,256,512]{2,1,0:T(8,128)(2,1)S(1)} custom-call(bf16[256,512]{1,0:T(8,128)(2,1)S(1)} %copy-done.3, f32[4,256,128]{2,1,0:T(8,128)S(1)} %copy-done, f32[4,256,128]{2,1,0:T(8,128)S(1)} %shard_map.65.local, f32[16,256]{1,0:T(8,128)S(1)} %fusion.31.near, f32[16,256]{1,0:T(8,128)S(1)} %collective-permute-done.2.far, f32[16,512]{1,0:T(8,128)S(1)} %copy-done.7, ...), custom_call_target="tpu_custom_call" | custom-call | tf_op jit(solution)/shard_map/pallas_call | solution.py:26
  35.8 2.4 %collective-permute-start.8 = (bf16[1,512,256]{2,1,0:T(8,128)(2,1)S(1)}, bf16[1,512,256]{2,1,0:T(8,128)(2,1)S(1)}, u32[]{:S(2)}, u32[]{:S(2)}) collective-permute-start(bf16[1,512,256]{2,1,0:T(8,128)(2,1)S(1)} %collective-permute-done.5.refs_3_), channel_id=1, source_target_pairs={{0,112},{16,0},{32,16},{48,32},{64,48},{80,64},{96,80},{112,96},{1... | collective-permute-start | bytes 786440 | tf_op jit(solution)/shard_map/ppermute | solution.py:256
  38.2 2.0 %collective-permute-start.6 = (bf16[1,256,512]{2,1,0:T(8,128)(2,1)S(1)}, bf16[1,256,512]{2,1,0:T(8,128)(2,1)S(1)}, u32[]{:S(2)}, u32[]{:S(2)}) collective-permute-start(bf16[1,256,512]{2,1,0:T(8,128)(2,1)S(1)} %shard_map.66), channel_id=1, source_target_pairs={{0,1},{1,0},{2,3},{3,2},{4,5},{5,4},{6,7},{7,6},{8,9},{9,8},{10,11... | collective-permute-start | bytes 786440 | tf_op jit(solution)/shard_map/ppermute | solution.py:256
  41.7 1.8 %collective-permute-done.7.refs_4_ = bf16[1,512,256]{2,1,0:T(8,128)(2,1)S(1)} collective-permute-done((bf16[1,512,256]{2,1,0:T(8,128)(2,1)S(1)}, bf16[1,512,256]{2,1,0:T(8,128)(2,1)S(1)}, u32[]{:S(2)}, u32[]{:S(2)}) %collective-permute-start.7) | collective-permute-done | bytes 262176 | tf_op jit(solution)/shard_map/ppermute | solution.py:256
  43.5 2.4 %collective-permute-done.6 = bf16[1,256,512]{2,1,0:T(8,128)(2,1)S(1)} collective-permute-done((bf16[1,256,512]{2,1,0:T(8,128)(2,1)S(1)}, bf16[1,256,512]{2,1,0:T(8,128)(2,1)S(1)}, u32[]{:S(2)}, u32[]{:S(2)}) %collective-permute-start.6) | collective-permute-done | bytes 262176 | tf_op jit(solution)/shard_map/ppermute | solution.py:256
  45.9 1.2 %collective-permute-start.13 = (bf16[1,512,256]{2,1,0:T(8,128)(2,1)S(1)}, bf16[1,512,256]{2,1,0:T(8,128)(2,1)S(1)}, u32[]{:S(2)}, u32[]{:S(2)}) collective-permute-start(bf16[1,512,256]{2,1,0:T(8,128)(2,1)S(1)} %collective-permute-done.7.refs_4_), channel_id=1, source_target_pairs={{0,128},{128,0},{1,129},{129,1},{2,130},{130,2},{3,131},{131,3},{4... | collective-permute-start | bytes 786440 | tf_op jit(solution)/shard_map/ppermute | solution.py:256
  48.9 1.5 %collective-permute-start.14 = (bf16[1,512,256]{2,1,0:T(8,128)(2,1)S(1)}, bf16[1,512,256]{2,1,0:T(8,128)(2,1)S(1)}, u32[]{:S(2)}, u32[]{:S(2)}) collective-permute-start(bf16[1,512,256]{2,1,0:T(8,128)(2,1)S(1)} %collective-permute-done.8.refs_5_), channel_id=1, source_target_pairs={{0,128},{128,0},{1,129},{129,1},{2,130},{130,2},{3,131},{131,3},{4... | collective-permute-start | bytes 786440 | tf_op jit(solution)/shard_map/ppermute | solution.py:256
  51.1 1.6 %collective-permute-start.12 = (bf16[1,512,256]{2,1,0:T(8,128)(2,1)S(1)}, bf16[1,512,256]{2,1,0:T(8,128)(2,1)S(1)}, u32[]{:S(2)}, u32[]{:S(2)}) collective-permute-start(bf16[1,512,256]{2,1,0:T(8,128)(2,1)S(1)} %collective-permute-done.8.refs_5_), channel_id=1, source_target_pairs={{0,112},{16,0},{32,16},{48,32},{64,48},{80,64},{96,80},{112,96},{1... | collective-permute-start | bytes 786440 | tf_op jit(solution)/shard_map/ppermute | solution.py:256
  52.8 1.5 %collective-permute-done.11.refs_0_ = bf16[1,512,256]{2,1,0:T(8,128)(2,1)S(1)} collective-permute-done((bf16[1,512,256]{2,1,0:T(8,128)(2,1)S(1)}, bf16[1,512,256]{2,1,0:T(8,128)(2,1)S(1)}, u32[]{:S(2)}, u32[]{:S(2)}) %collective-permute-start.11) | collective-permute-done | bytes 262176 | tf_op jit(solution)/shard_map/ppermute | solution.py:256
  54.4 2.8 %collective-permute-done.14.refs_3_ = bf16[1,512,256]{2,1,0:T(8,128)(2,1)S(1)} collective-permute-done((bf16[1,512,256]{2,1,0:T(8,128)(2,1)S(1)}, bf16[1,512,256]{2,1,0:T(8,128)(2,1)S(1)}, u32[]{:S(2)}, u32[]{:S(2)}) %collective-permute-start.14) | collective-permute-done | bytes 262176 | tf_op jit(solution)/shard_map/ppermute | solution.py:256
  57.3 2.7 %collective-permute-start.21 = (bf16[1,512,256]{2,1,0:T(8,128)(2,1)S(1)}, bf16[1,512,256]{2,1,0:T(8,128)(2,1)S(1)}, u32[]{:S(2)}, u32[]{:S(2)}) collective-permute-start(bf16[1,512,256]{2,1,0:T(8,128)(2,1)S(1)} %collective-permute-done.14.refs_3_), channel_id=1, source_target_pairs={{0,112},{16,0},{32,16},{48,32},{64,48},{80,64},{96,80},{112,96},{1... | collective-permute-start | bytes 786440 | tf_op jit(solution)/shard_map/ppermute | solution.py:256
  62.2 2.6 %collective-permute-start.19 = (bf16[256,512]{1,0:T(8,128)(2,1)S(1)}, bf16[256,512]{1,0:T(8,128)(2,1)S(1)}, u32[]{:S(2)}, u32[]{:S(2)}) collective-permute-start(bf16[256,512]{1,0:T(8,128)(2,1)S(1)} %get-tuple-element.73.refs_5_), channel_id=1, source_target_pairs={{0,6},{2,0},{4,2},{6,4},{1,7},{3,1},{5,3},{7,5},{8,14},{10,8},{12,... | collective-permute-start | bytes 786440 | tf_op jit(solution)/shard_map/ppermute | solution.py:256
  65.9 1.6 %collective-permute-done.22.refs_9_ = bf16[1,512,256]{2,1,0:T(8,128)(2,1)S(1)} collective-permute-done((bf16[1,512,256]{2,1,0:T(8,128)(2,1)S(1)}, bf16[1,512,256]{2,1,0:T(8,128)(2,1)S(1)}, u32[]{:S(2)}, u32[]{:S(2)}) %collective-permute-start.22) | collective-permute-done | bytes 262176 | tf_op jit(solution)/shard_map/ppermute | solution.py:256
  68.4 8.2 %collective-permute-start.24 = (bf16[10,512,256]{2,1,0:T(8,128)(2,1)S(1)}, bf16[10,512,256]{2,1,0:T(8,128)(2,1)S(1)}, u32[]{:S(2)}, u32[]{:S(2)}) collective-permute-start(bf16[10,512,256]{2,1,0:T(8,128)(2,1)S(1)} %shard_map.68.refs_9_), channel_id=1, source_target_pairs={{0,8},{8,0},{1,9},{9,1},{2,10},{10,2},{3,11},{11,3},{4,12},{12,4},... | collective-permute-start | bytes 7864328 | tf_op jit(solution)/shard_map/ppermute | solution.py:256
  76.8 2.1 %shard_map.69 = (f32[2,256,256]{2,1,0:T(8,128)S(1)}, bf16[256,4096]{1,0:T(8,128)(2,1)S(1)}) custom-call(bf16[256,512]{1,0:T(8,128)(2,1)S(1)} %bitcast.144, bf16[256,512]{1,0:T(8,128)(2,1)S(1)} %bitcast.145, bf16[256,512]{1,0:T(8,128)(2,1)S(1)} %get-tuple-element.76.refs_2_, bf16[256,512]{1,0:T(8,128)(2,1)S(1)} %get-tuple-element.75.refs_3_, ...), custom_call_target="tpu_custom_call" | custom-call | flops 1073741824 | bytes 6291456 | tf_op jit(solution)/shard_map/pallas_call | solution.py:218
  78.9 4.6 %collective-permute-done.23.refs_2_ = bf16[6,512,256]{2,1,0:T(8,128)(2,1)S(1)} collective-permute-done((bf16[6,512,256]{2,1,0:T(8,128)(2,1)S(1)}, bf16[6,512,256]{2,1,0:T(8,128)(2,1)S(1)}, u32[]{:S(2)}, u32[]{:S(2)}) %collective-permute-start.23) | collective-permute-done | bytes 1572896 | tf_op jit(solution)/shard_map/ppermute | solution.py:256
  83.5 2.6 %shard_map.70 = bf16[256,1024]{1,0:T(8,128)(2,1)} custom-call(f32[2,256,256]{2,1,0:T(8,128)S(1)} %get-tuple-element.69.refs_0_, bf16[256,4096]{1,0:T(8,128)(2,1)S(1)} %get-tuple-element.70.refs_1_, bf16[6,512,256]{2,1,0:T(8,128)(2,1)S(1)} %collective-permute-done.23.refs_2_, bf16[10,512,256]{2,1,0:T(8,128)(2,1)S(1)} %collective-permute-done.24.refs_3_), custom_call_target="tpu_custom_call" | custom-call | flops 1073741824 | bytes 6291456 | tf_op jit(solution)/shard_map/pallas_call | solution.py:227
  (61 shorter events, 17.7 us)
Async XLA Ops:
  0.0 20.9 %collective-permute-start = (bf16[512,256]{1,0:T(8,128)(2,1)}, bf16[512,256]{1,0:T(8,128)(2,1)S(1)}, u32[]{:S(2)}, u32[]{:S(2)}) collective-permute-start(bf16[512,256]{1,0:T(8,128)(2,1)} %param.11), channel_id=1, source_target_pairs={{0,80},{8,88},{16,64},{24,72},{32,241},{40,249},{48,225},{56,233},... | collective-permute-start | bytes 786440 | tf_op jit(solution)/shard_map/ppermute | solution.py:252
  13.8 16.0 %all-to-all-start = ((f32[16,16,256]{2,1,0:T(8,128)}), f32[16,16,256]{2,1,0:T(8,128)S(1)}, u32[]{:S(2)}, u32[]{:S(2)}) async-start(f32[16,16,256]{2,1,0:T(8,128)} %broadcast_in_dim.13), calls=%async_computation | async-start | bytes 524288 | tf_op jit(solution)/shard_map/all_to_all | solution.py:286
  20.9 14.3 %collective-permute-start.5 = (bf16[1,512,256]{2,1,0:T(8,128)(2,1)S(1)}, bf16[1,512,256]{2,1,0:T(8,128)(2,1)S(1)}, u32[]{:S(2)}, u32[]{:S(2)}) collective-permute-start(bf16[1,512,256]{2,1,0:T(8,128)(2,1)S(1)} %bitcast.146), channel_id=1, source_target_pairs={{0,112},{16,0},{32,16},{48,32},{64,48},{80,64},{96,80},{112,96},{1... | collective-permute-start | bytes 786440 | tf_op jit(solution)/shard_map/ppermute | solution.py:256
  23.5 12.0 %collective-permute-start.4 = (bf16[1,512,256]{2,1,0:T(8,128)(2,1)S(1)}, bf16[1,512,256]{2,1,0:T(8,128)(2,1)S(1)}, u32[]{:S(2)}, u32[]{:S(2)}) collective-permute-start(bf16[1,512,256]{2,1,0:T(8,128)(2,1)S(1)} %bitcast.147), channel_id=1, source_target_pairs={{0,16},{16,32},{32,48},{48,64},{64,80},{80,96},{96,112},{112,0},{1... | collective-permute-start | bytes 786440 | tf_op jit(solution)/shard_map/ppermute | solution.py:256
  23.5 12.0 %collective-permute-start.3 = (bf16[1,512,256]{2,1,0:T(8,128)(2,1)S(1)}, bf16[1,512,256]{2,1,0:T(8,128)(2,1)S(1)}, u32[]{:S(2)}, u32[]{:S(2)}) collective-permute-start(bf16[1,512,256]{2,1,0:T(8,128)(2,1)S(1)} %bitcast.148), channel_id=1, source_target_pairs={{0,128},{128,0},{1,129},{129,1},{2,130},{130,2},{3,131},{131,3},{4... | collective-permute-start | bytes 786440 | tf_op jit(solution)/shard_map/ppermute | solution.py:256
  35.5 8.0 %collective-permute-start.7 = (bf16[1,512,256]{2,1,0:T(8,128)(2,1)S(1)}, bf16[1,512,256]{2,1,0:T(8,128)(2,1)S(1)}, u32[]{:S(2)}, u32[]{:S(2)}) collective-permute-start(bf16[1,512,256]{2,1,0:T(8,128)(2,1)S(1)} %collective-permute-done.4.refs_2_), channel_id=1, source_target_pairs={{0,16},{16,32},{32,48},{48,64},{64,80},{80,96},{96,112},{112,0},{1... | collective-permute-start | bytes 786440 | tf_op jit(solution)/shard_map/ppermute | solution.py:256
  35.8 7.7 %collective-permute-start.8 = (bf16[1,512,256]{2,1,0:T(8,128)(2,1)S(1)}, bf16[1,512,256]{2,1,0:T(8,128)(2,1)S(1)}, u32[]{:S(2)}, u32[]{:S(2)}) collective-permute-start(bf16[1,512,256]{2,1,0:T(8,128)(2,1)S(1)} %collective-permute-done.5.refs_3_), channel_id=1, source_target_pairs={{0,112},{16,0},{32,16},{48,32},{64,48},{80,64},{96,80},{112,96},{1... | collective-permute-start | bytes 786440 | tf_op jit(solution)/shard_map/ppermute | solution.py:256
  38.2 7.7 %collective-permute-start.6 = (bf16[1,256,512]{2,1,0:T(8,128)(2,1)S(1)}, bf16[1,256,512]{2,1,0:T(8,128)(2,1)S(1)}, u32[]{:S(2)}, u32[]{:S(2)}) collective-permute-start(bf16[1,256,512]{2,1,0:T(8,128)(2,1)S(1)} %shard_map.66), channel_id=1, source_target_pairs={{0,1},{1,0},{2,3},{3,2},{4,5},{5,4},{6,7},{7,6},{8,9},{9,8},{10,11... | collective-permute-start | bytes 786440 | tf_op jit(solution)/shard_map/ppermute | solution.py:256
  40.2 8.3 %collective-permute-start.17 = (bf16[1,512,256]{2,1,0:T(8,128)(2,1)S(1)}, bf16[1,512,256]{2,1,0:T(8,128)(2,1)S(1)}, u32[]{:S(2)}, u32[]{:S(2)}) collective-permute-start(bf16[1,512,256]{2,1,0:T(8,128)(2,1)S(1)} %collective-permute-done.3.refs_1_), channel_id=1, source_target_pairs={{0,112},{16,0},{32,16},{48,32},{64,48},{80,64},{96,80},{112,96},{1... | collective-permute-start | bytes 786440 | tf_op jit(solution)/shard_map/ppermute | solution.py:256
  40.9 8.1 %collective-permute-start.16 = (bf16[1,512,256]{2,1,0:T(8,128)(2,1)S(1)}, bf16[1,512,256]{2,1,0:T(8,128)(2,1)S(1)}, u32[]{:S(2)}, u32[]{:S(2)}) collective-permute-start(bf16[1,512,256]{2,1,0:T(8,128)(2,1)S(1)} %collective-permute-done.3.refs_1_), channel_id=1, source_target_pairs={{0,16},{16,32},{32,48},{48,64},{64,80},{80,96},{96,112},{112,0},{1... | collective-permute-start | bytes 786440 | tf_op jit(solution)/shard_map/ppermute | solution.py:256
  45.9 5.2 %collective-permute-start.13 = (bf16[1,512,256]{2,1,0:T(8,128)(2,1)S(1)}, bf16[1,512,256]{2,1,0:T(8,128)(2,1)S(1)}, u32[]{:S(2)}, u32[]{:S(2)}) collective-permute-start(bf16[1,512,256]{2,1,0:T(8,128)(2,1)S(1)} %collective-permute-done.7.refs_4_), channel_id=1, source_target_pairs={{0,128},{128,0},{1,129},{129,1},{2,130},{130,2},{3,131},{131,3},{4... | collective-permute-start | bytes 786440 | tf_op jit(solution)/shard_map/ppermute | solution.py:256
  47.1 12.8 %collective-permute-start.10 = (bf16[2,256,512]{2,1,0:T(8,128)(2,1)S(1)}, bf16[2,256,512]{2,1,0:T(8,128)(2,1)S(1)}, u32[]{:S(2)}, u32[]{:S(2)}) collective-permute-start(bf16[2,256,512]{2,1,0:T(8,128)(2,1)S(1)} %constant_dynamic-update-slice_fusion), channel_id=1, source_target_pairs={{0,6},{2,0},{4,2},{6,4},{1,7},{3,1},{5,3},{7,5},{8,14},{10,8},{12,... | collective-permute-start | bytes 1572872 | tf_op jit(solution)/shard_map/ppermute | solution.py:256
  47.8 6.4 %collective-permute-start.11 = (bf16[1,512,256]{2,1,0:T(8,128)(2,1)S(1)}, bf16[1,512,256]{2,1,0:T(8,128)(2,1)S(1)}, u32[]{:S(2)}, u32[]{:S(2)}) collective-permute-start(bf16[1,512,256]{2,1,0:T(8,128)(2,1)S(1)} %collective-permute-done.7.refs_4_), channel_id=1, source_target_pairs={{0,16},{16,32},{32,48},{48,64},{64,80},{80,96},{96,112},{112,0},{1... | collective-permute-start | bytes 786440 | tf_op jit(solution)/shard_map/ppermute | solution.py:256
  48.5 12.0 %collective-permute-start.9 = (bf16[2,256,512]{2,1,0:T(8,128)(2,1)S(1)}, bf16[2,256,512]{2,1,0:T(8,128)(2,1)S(1)}, u32[]{:S(2)}, u32[]{:S(2)}) collective-permute-start(bf16[2,256,512]{2,1,0:T(8,128)(2,1)S(1)} %constant_dynamic-update-slice_fusion), channel_id=1, source_target_pairs={{0,2},{2,4},{4,6},{6,0},{1,3},{3,5},{5,7},{7,1},{8,10},{10,12},{12... | collective-permute-start | bytes 1572872 | tf_op jit(solution)/shard_map/ppermute | solution.py:256
  48.9 8.3 %collective-permute-start.14 = (bf16[1,512,256]{2,1,0:T(8,128)(2,1)S(1)}, bf16[1,512,256]{2,1,0:T(8,128)(2,1)S(1)}, u32[]{:S(2)}, u32[]{:S(2)}) collective-permute-start(bf16[1,512,256]{2,1,0:T(8,128)(2,1)S(1)} %collective-permute-done.8.refs_5_), channel_id=1, source_target_pairs={{0,128},{128,0},{1,129},{129,1},{2,130},{130,2},{3,131},{131,3},{4... | collective-permute-start | bytes 786440 | tf_op jit(solution)/shard_map/ppermute | solution.py:256
  51.1 6.1 %collective-permute-start.12 = (bf16[1,512,256]{2,1,0:T(8,128)(2,1)S(1)}, bf16[1,512,256]{2,1,0:T(8,128)(2,1)S(1)}, u32[]{:S(2)}, u32[]{:S(2)}) collective-permute-start(bf16[1,512,256]{2,1,0:T(8,128)(2,1)S(1)} %collective-permute-done.8.refs_5_), channel_id=1, source_target_pairs={{0,112},{16,0},{32,16},{48,32},{64,48},{80,64},{96,80},{112,96},{1... | collective-permute-start | bytes 786440 | tf_op jit(solution)/shard_map/ppermute | solution.py:256
  54.2 6.9 %collective-permute-start.15 = (bf16[1,512,256]{2,1,0:T(8,128)(2,1)S(1)}, bf16[1,512,256]{2,1,0:T(8,128)(2,1)S(1)}, u32[]{:S(2)}, u32[]{:S(2)}) collective-permute-start(bf16[1,512,256]{2,1,0:T(8,128)(2,1)S(1)} %collective-permute-done.11.refs_0_), channel_id=1, source_target_pairs={{0,16},{16,32},{32,48},{48,64},{64,80},{80,96},{96,112},{112,0},{1... | collective-permute-start | bytes 786440 | tf_op jit(solution)/shard_map/ppermute | solution.py:256
  57.3 7.6 %collective-permute-start.20 = (bf16[1,512,256]{2,1,0:T(8,128)(2,1)S(1)}, bf16[1,512,256]{2,1,0:T(8,128)(2,1)S(1)}, u32[]{:S(2)}, u32[]{:S(2)}) collective-permute-start(bf16[1,512,256]{2,1,0:T(8,128)(2,1)S(1)} %collective-permute-done.13.refs_2_), channel_id=1, source_target_pairs={{0,16},{16,32},{32,48},{48,64},{64,80},{80,96},{96,112},{112,0},{1... | collective-permute-start | bytes 786440 | tf_op jit(solution)/shard_map/ppermute | solution.py:256
  57.3 8.6 %collective-permute-start.21 = (bf16[1,512,256]{2,1,0:T(8,128)(2,1)S(1)}, bf16[1,512,256]{2,1,0:T(8,128)(2,1)S(1)}, u32[]{:S(2)}, u32[]{:S(2)}) collective-permute-start(bf16[1,512,256]{2,1,0:T(8,128)(2,1)S(1)} %collective-permute-done.14.refs_3_), channel_id=1, source_target_pairs={{0,112},{16,0},{32,16},{48,32},{64,48},{80,64},{96,80},{112,96},{1... | collective-permute-start | bytes 786440 | tf_op jit(solution)/shard_map/ppermute | solution.py:256
  61.2 6.8 %collective-permute-start.18 = (bf16[256,512]{1,0:T(8,128)(2,1)S(1)}, bf16[256,512]{1,0:T(8,128)(2,1)S(1)}, u32[]{:S(2)}, u32[]{:S(2)}) collective-permute-start(bf16[256,512]{1,0:T(8,128)(2,1)S(1)} %get-tuple-element.76.refs_2_), channel_id=1, source_target_pairs={{0,2},{2,4},{4,6},{6,0},{1,3},{3,5},{5,7},{7,1},{8,10},{10,12},{12... | collective-permute-start | bytes 786440 | tf_op jit(solution)/shard_map/ppermute | solution.py:256
  61.9 5.6 %collective-permute-start.22 = (bf16[1,512,256]{2,1,0:T(8,128)(2,1)S(1)}, bf16[1,512,256]{2,1,0:T(8,128)(2,1)S(1)}, u32[]{:S(2)}, u32[]{:S(2)}) collective-permute-start(bf16[1,512,256]{2,1,0:T(8,128)(2,1)S(1)} %collective-permute-done.15.refs_4_), channel_id=1, source_target_pairs={{0,128},{128,0},{1,129},{129,1},{2,130},{130,2},{3,131},{131,3},{4... | collective-permute-start | bytes 786440 | tf_op jit(solution)/shard_map/ppermute | solution.py:256
  62.2 5.9 %collective-permute-start.19 = (bf16[256,512]{1,0:T(8,128)(2,1)S(1)}, bf16[256,512]{1,0:T(8,128)(2,1)S(1)}, u32[]{:S(2)}, u32[]{:S(2)}) collective-permute-start(bf16[256,512]{1,0:T(8,128)(2,1)S(1)} %get-tuple-element.73.refs_5_), channel_id=1, source_target_pairs={{0,6},{2,0},{4,2},{6,4},{1,7},{3,1},{5,3},{7,5},{8,14},{10,8},{12,... | collective-permute-start | bytes 786440 | tf_op jit(solution)/shard_map/ppermute | solution.py:256
  68.4 15.0 %collective-permute-start.24 = (bf16[10,512,256]{2,1,0:T(8,128)(2,1)S(1)}, bf16[10,512,256]{2,1,0:T(8,128)(2,1)S(1)}, u32[]{:S(2)}, u32[]{:S(2)}) collective-permute-start(bf16[10,512,256]{2,1,0:T(8,128)(2,1)S(1)} %shard_map.68.refs_9_), channel_id=1, source_target_pairs={{0,8},{8,0},{1,9},{9,1},{2,10},{10,2},{3,11},{11,3},{4,12},{12,4},... | collective-permute-start | bytes 7864328 | tf_op jit(solution)/shard_map/ppermute | solution.py:256
  76.7 6.8 %collective-permute-start.23 = (bf16[6,512,256]{2,1,0:T(8,128)(2,1)S(1)}, bf16[6,512,256]{2,1,0:T(8,128)(2,1)S(1)}, u32[]{:S(2)}, u32[]{:S(2)}) collective-permute-start(bf16[6,512,256]{2,1,0:T(8,128)(2,1)S(1)} %shard_map.67.refs_8_), channel_id=1, source_target_pairs={{0,8},{8,0},{1,9},{9,1},{2,10},{10,2},{3,11},{11,3},{4,12},{12,4},... | collective-permute-start | bytes 4718600 | tf_op jit(solution)/shard_map/ppermute | solution.py:256
  (11 other events, 37.9 us)

commit v6 on v5

--- a/solution.py
+++ b/solution.py
@@ -214,7 +214,7 @@
     blocks = [pltpu.VMEM((2, 8, 512, 256), BF16)]
     sems = [pltpu.SemaphoreType.DMA((16,))]
     params = pltpu.CompilerParams(vmem_limit_bytes=VMEM_LIMIT)
-    cost = pl.CostEstimate(flops=1 << 30, bytes_accessed=6 << 20, transcendentals=0)
+    cost = pl.CostEstimate(flops=1 << 36, bytes_accessed=6 << 20, transcendentals=0)
     total, gated = pl.pallas_call(
         lambda *refs: own_body(places, len(own), *refs),
         out_shape=[jax.ShapeDtypeStruct((2, ROWS, 256), F32), jax.ShapeDtypeStruct((ROWS, 8 * CHANS), BF16)],
@@ -316,7 +316,7 @@
     early, places = early + [up_a, down_a], places + [(0, 6), (0, 2)]
     side = move(gated, "yhi", 1)
     side, *early = together(side, *early)
-    early = bundle(early)
+    early = bundle(early, 1 << 36)
 
     up_b, down_b = move(up_a, "ylo", 1), move(down_a, "ylo", 1)
     up_a, down_a = move(up_a, "z", 1), move(down_a, "z", -1)

time: 86.7 us -> 84.1 us (0.970)
  waiting for transfers between devices: 22.2 us -> 16.6 us
  starting transfers between devices: 48.7 us -> 51.6 us
    ppermute x24, waiting for transfers between devices: 21.4 us -> 15.8 us  [move(): lax.ppermute(value, axis, ring({'ylo': 2, 'z': 8, 'core': 2, 'x': 4, 'yhi...]
    ppermute x24, starting transfers between devices: 34.3 us -> 37.3 us  [move(): lax.ppermute(value, axis, ring({'ylo': 2, 'z': 8, 'core': 2, 'x': 4, 'yhi...]
  transfers between devices with their start and end apart: 26 -> 26, of which waited for: 18 -> 15; matrix products, arithmetic and copies ran while one was open for 2% -> 2% of each run, Pallas kernels for 8% -> 9%
where the time goes in v6:
time: 84.1 us; the launch traced here: 83.6 us
  starting transfers between devices  51.6 us (61%)
  waiting for transfers between devices  16.6 us (20%)
  Pallas kernels  9.89 us (12%)
  local copies, waits for them, and re-layouts  4.28 us (5%)
    ppermute x24, starting transfers between devices, move(): lax.ppermute(value, axis, ring({'ylo': 2, 'z': 8, 'core': 2, 'x': 4, 'yhi...  37.3 us
    ppermute x24, waiting for transfers between devices, move(): lax.ppermute(value, axis, ring({'ylo': 2, 'z': 8, 'core': 2, 'x': 4, 'yhi...  15.8 us
    ppermute x1, starting transfers between devices, swap(): return lax.ppermute(block, ('ylo', 'z', 'core', 'x', 'yhi'), pairs)  7.29 us
    all_to_all x1, starting transfers between devices, shards(): lax.all_to_all(jnp.broadcast_to(chip[None], (16, MODES, HALF)), ('ylo', '...  7.05 us
    unnamed x19, local copies, waits for them, and re-layouts  3.45 us
    pallas_call x1, Pallas kernels, shards(): pl.pallas_call(sums_body, out_shape=[tiled, half, half], in_specs=[pl.Blo...  2.93 us
    pallas_call x1, Pallas kernels, project(): pl.pallas_call(lambda *refs: other_body(places, len(other), *refs), out_s...  2.55 us
    pallas_call x1, Pallas kernels, project(): pl.pallas_call(lambda *refs: own_body(places, len(own), *refs), out_shape...  2.09 us
  transfers between devices with their start and end apart: 26, of which 15 were waited for; matrix products, arithmetic and copies ran while one was open for 2% of the time, Pallas kernels for 9%

profile of v6, /device:TPU:1, one launch (start us, length us, event | category | flops | bytes accessed | tf_op | source)
XLA Modules:
  0.0 83.6 jit_solution(12228388740233140826)
XLA Ops:
  0.0 7.3 %collective-permute-start = (bf16[512,256]{1,0:T(8,128)(2,1)}, bf16[512,256]{1,0:T(8,128)(2,1)S(1)}, u32[]{:S(2)}, u32[]{:S(2)}) collective-permute-start(bf16[512,256]{1,0:T(8,128)(2,1)} %param.11), channel_id=1, source_target_pairs={{0,80},{8,88},{16,64},{24,72},{32,241},{40,249},{48,225},{56,233},... | collective-permute-start | bytes 786440 | tf_op jit(solution)/shard_map/ppermute | solution.py:252
  7.3 2.9 %shard_map.64 = (f32[4,256,128]{2,1,0:T(8,128)}, f32[16,256]{1,0:T(8,128)}, f32[16,256]{1,0:T(8,128)}) custom-call(bf16[256,512]{1,0:T(8,128)(2,1)} %inner_hbm.2, bf16[256,512]{1,0:T(8,128)(2,1)} %values_hbm.3, f32[16,512]{1,0:T(8,128)} %decays.1), custom_call_target="tpu_custom_call" | custom-call | flops 4194304 | bytes 2097152 | tf_op jit(solution)/shard_map/pallas_call | solution.py:271
  13.8 7.0 %all-to-all-start = ((f32[16,16,256]{2,1,0:T(8,128)}), f32[16,16,256]{2,1,0:T(8,128)S(1)}, u32[]{:S(2)}, u32[]{:S(2)}) async-start(f32[16,16,256]{2,1,0:T(8,128)} %broadcast_in_dim.13), calls=%async_computation | async-start | bytes 524288 | tf_op jit(solution)/shard_map/all_to_all | solution.py:286
  20.9 2.7 %collective-permute-start.5 = (bf16[1,512,256]{2,1,0:T(8,128)(2,1)S(1)}, bf16[1,512,256]{2,1,0:T(8,128)(2,1)S(1)}, u32[]{:S(2)}, u32[]{:S(2)}) collective-permute-start(bf16[1,512,256]{2,1,0:T(8,128)(2,1)S(1)} %bitcast.146), channel_id=1, source_target_pairs={{0,112},{16,0},{32,16},{48,32},{64,48},{80,64},{96,80},{112,96},{1... | collective-permute-start | bytes 786440 | tf_op jit(solution)/shard_map/ppermute | solution.py:256
  23.5 1.2 %collective-permute-start.3 = (bf16[1,512,256]{2,1,0:T(8,128)(2,1)S(1)}, bf16[1,512,256]{2,1,0:T(8,128)(2,1)S(1)}, u32[]{:S(2)}, u32[]{:S(2)}) collective-permute-start(bf16[1,512,256]{2,1,0:T(8,128)(2,1)S(1)} %bitcast.148), channel_id=1, source_target_pairs={{0,128},{128,0},{1,129},{129,1},{2,130},{130,2},{3,131},{131,3},{4... | collective-permute-start | bytes 786440 | tf_op jit(solution)/shard_map/ppermute | solution.py:256
  29.8 3.4 %collective-permute-start.2 = (f32[16,256]{1,0:T(8,128)S(1)}, f32[16,256]{1,0:T(8,128)S(1)}, u32[]{:S(2)}, u32[]{:S(2)}) collective-permute-start(f32[16,256]{1,0:T(8,128)S(1)} %get-tuple-element.71), channel_id=1, source_target_pairs={{0,8},{8,0},{1,9},{9,1},{2,10},{10,2},{3,11},{11,3},{4,12},{12,4},... | collective-permute-start | bytes 49160 | tf_op jit(solution)/shard_map/ppermute | solution.py:256
  35.8 2.4 %collective-permute-start.8 = (bf16[1,512,256]{2,1,0:T(8,128)(2,1)S(1)}, bf16[1,512,256]{2,1,0:T(8,128)(2,1)S(1)}, u32[]{:S(2)}, u32[]{:S(2)}) collective-permute-start(bf16[1,512,256]{2,1,0:T(8,128)(2,1)S(1)} %collective-permute-done.5.refs_3_), channel_id=1, source_target_pairs={{0,112},{16,0},{32,16},{48,32},{64,48},{80,64},{96,80},{112,96},{1... | collective-permute-start | bytes 786440 | tf_op jit(solution)/shard_map/ppermute | solution.py:256
  38.2 2.0 %collective-permute-start.6 = (bf16[1,256,512]{2,1,0:T(8,128)(2,1)S(1)}, bf16[1,256,512]{2,1,0:T(8,128)(2,1)S(1)}, u32[]{:S(2)}, u32[]{:S(2)}) collective-permute-start(bf16[1,256,512]{2,1,0:T(8,128)(2,1)S(1)} %shard_map.66), channel_id=1, source_target_pairs={{0,1},{1,0},{2,3},{3,2},{4,5},{5,4},{6,7},{7,6},{8,9},{9,8},{10,11... | collective-permute-start | bytes 786440 | tf_op jit(solution)/shard_map/ppermute | solution.py:256
  41.7 1.8 %collective-permute-done.7.refs_4_ = bf16[1,512,256]{2,1,0:T(8,128)(2,1)S(1)} collective-permute-done((bf16[1,512,256]{2,1,0:T(8,128)(2,1)S(1)}, bf16[1,512,256]{2,1,0:T(8,128)(2,1)S(1)}, u32[]{:S(2)}, u32[]{:S(2)}) %collective-permute-start.7) | collective-permute-done | bytes 262176 | tf_op jit(solution)/shard_map/ppermute | solution.py:256
  43.5 1.2 %collective-permute-start.13 = (bf16[1,512,256]{2,1,0:T(8,128)(2,1)S(1)}, bf16[1,512,256]{2,1,0:T(8,128)(2,1)S(1)}, u32[]{:S(2)}, u32[]{:S(2)}) collective-permute-start(bf16[1,512,256]{2,1,0:T(8,128)(2,1)S(1)} %collective-permute-done.7.refs_4_), channel_id=1, source_target_pairs={{0,128},{128,0},{1,129},{129,1},{2,130},{130,2},{3,131},{131,3},{4... | collective-permute-start | bytes 786440 | tf_op jit(solution)/shard_map/ppermute | solution.py:256
  47.0 1.5 %collective-permute-done.17.refs_6_ = bf16[1,512,256]{2,1,0:T(8,128)(2,1)S(1)} collective-permute-done((bf16[1,512,256]{2,1,0:T(8,128)(2,1)S(1)}, bf16[1,512,256]{2,1,0:T(8,128)(2,1)S(1)}, u32[]{:S(2)}, u32[]{:S(2)}) %collective-permute-start.17) | collective-permute-done | bytes 262176 | tf_op jit(solution)/shard_map/ppermute | solution.py:256
  48.9 1.5 %collective-permute-start.14 = (bf16[1,512,256]{2,1,0:T(8,128)(2,1)S(1)}, bf16[1,512,256]{2,1,0:T(8,128)(2,1)S(1)}, u32[]{:S(2)}, u32[]{:S(2)}) collective-permute-start(bf16[1,512,256]{2,1,0:T(8,128)(2,1)S(1)} %collective-permute-done.8.refs_5_), channel_id=1, source_target_pairs={{0,128},{128,0},{1,129},{129,1},{2,130},{130,2},{3,131},{131,3},{4... | collective-permute-start | bytes 786440 | tf_op jit(solution)/shard_map/ppermute | solution.py:256
  51.4 1.4 %collective-permute-start.12 = (bf16[1,512,256]{2,1,0:T(8,128)(2,1)S(1)}, bf16[1,512,256]{2,1,0:T(8,128)(2,1)S(1)}, u32[]{:S(2)}, u32[]{:S(2)}) collective-permute-start(bf16[1,512,256]{2,1,0:T(8,128)(2,1)S(1)} %collective-permute-done.8.refs_5_), channel_id=1, source_target_pairs={{0,112},{16,0},{32,16},{48,32},{64,48},{80,64},{96,80},{112,96},{1... | collective-permute-start | bytes 786440 | tf_op jit(solution)/shard_map/ppermute | solution.py:256
  52.7 1.4 %collective-permute-done.11.refs_0_ = bf16[1,512,256]{2,1,0:T(8,128)(2,1)S(1)} collective-permute-done((bf16[1,512,256]{2,1,0:T(8,128)(2,1)S(1)}, bf16[1,512,256]{2,1,0:T(8,128)(2,1)S(1)}, u32[]{:S(2)}, u32[]{:S(2)}) %collective-permute-start.11) | collective-permute-done | bytes 262176 | tf_op jit(solution)/shard_map/ppermute | solution.py:256
  54.3 1.8 %collective-permute-done.14.refs_3_ = bf16[1,512,256]{2,1,0:T(8,128)(2,1)S(1)} collective-permute-done((bf16[1,512,256]{2,1,0:T(8,128)(2,1)S(1)}, bf16[1,512,256]{2,1,0:T(8,128)(2,1)S(1)}, u32[]{:S(2)}, u32[]{:S(2)}) %collective-permute-start.14) | collective-permute-done | bytes 262176 | tf_op jit(solution)/shard_map/ppermute | solution.py:256
  56.9 2.6 %collective-permute-start.21 = (bf16[1,512,256]{2,1,0:T(8,128)(2,1)S(1)}, bf16[1,512,256]{2,1,0:T(8,128)(2,1)S(1)}, u32[]{:S(2)}, u32[]{:S(2)}) collective-permute-start(bf16[1,512,256]{2,1,0:T(8,128)(2,1)S(1)} %collective-permute-done.14.refs_3_), channel_id=1, source_target_pairs={{0,112},{16,0},{32,16},{48,32},{64,48},{80,64},{96,80},{112,96},{1... | collective-permute-start | bytes 786440 | tf_op jit(solution)/shard_map/ppermute | solution.py:256
  59.5 1.6 %collective-permute-done.9 = bf16[2,256,512]{2,1,0:T(8,128)(2,1)S(1)} collective-permute-done((bf16[2,256,512]{2,1,0:T(8,128)(2,1)S(1)}, bf16[2,256,512]{2,1,0:T(8,128)(2,1)S(1)}, u32[]{:S(2)}, u32[]{:S(2)}) %collective-permute-start.9) | collective-permute-done | bytes 524320 | tf_op jit(solution)/shard_map/ppermute | solution.py:256
  61.3 2.4 %collective-permute-start.22 = (bf16[1,512,256]{2,1,0:T(8,128)(2,1)S(1)}, bf16[1,512,256]{2,1,0:T(8,128)(2,1)S(1)}, u32[]{:S(2)}, u32[]{:S(2)}) collective-permute-start(bf16[1,512,256]{2,1,0:T(8,128)(2,1)S(1)} %collective-permute-done.15.refs_4_), channel_id=1, source_target_pairs={{0,128},{128,0},{1,129},{129,1},{2,130},{130,2},{3,131},{131,3},{4... | collective-permute-start | bytes 786440 | tf_op jit(solution)/shard_map/ppermute | solution.py:256
  63.7 2.4 %collective-permute-start.19 = (bf16[256,512]{1,0:T(8,128)(2,1)S(1)}, bf16[256,512]{1,0:T(8,128)(2,1)S(1)}, u32[]{:S(2)}, u32[]{:S(2)}) collective-permute-start(bf16[256,512]{1,0:T(8,128)(2,1)S(1)} %get-tuple-element.73.refs_5_), channel_id=1, source_target_pairs={{0,6},{2,0},{4,2},{6,4},{1,7},{3,1},{5,3},{7,5},{8,14},{10,8},{12,... | collective-permute-start | bytes 786440 | tf_op jit(solution)/shard_map/ppermute | solution.py:256
  66.2 5.9 %collective-permute-start.23 = (bf16[6,512,256]{2,1,0:T(8,128)(2,1)S(1)}, bf16[6,512,256]{2,1,0:T(8,128)(2,1)S(1)}, u32[]{:S(2)}, u32[]{:S(2)}) collective-permute-start(bf16[6,512,256]{2,1,0:T(8,128)(2,1)S(1)} %shard_map.67.refs_8_), channel_id=1, source_target_pairs={{0,8},{8,0},{1,9},{9,1},{2,10},{10,2},{3,11},{11,3},{4,12},{12,4},... | collective-permute-start | bytes 4718600 | tf_op jit(solution)/shard_map/ppermute | solution.py:256
  72.4 3.9 %collective-permute-start.24 = (bf16[10,512,256]{2,1,0:T(8,128)(2,1)S(1)}, bf16[10,512,256]{2,1,0:T(8,128)(2,1)S(1)}, u32[]{:S(2)}, u32[]{:S(2)}) collective-permute-start(bf16[10,512,256]{2,1,0:T(8,128)(2,1)S(1)} %shard_map.68.refs_9_), channel_id=1, source_target_pairs={{0,8},{8,0},{1,9},{9,1},{2,10},{10,2},{3,11},{11,3},{4,12},{12,4},... | collective-permute-start | bytes 7864328 | tf_op jit(solution)/shard_map/ppermute | solution.py:256
  76.3 2.1 %shard_map.69 = (f32[2,256,256]{2,1,0:T(8,128)S(1)}, bf16[256,4096]{1,0:T(8,128)(2,1)S(1)}) custom-call(bf16[256,512]{1,0:T(8,128)(2,1)S(1)} %bitcast.144, bf16[256,512]{1,0:T(8,128)(2,1)S(1)} %bitcast.145, bf16[256,512]{1,0:T(8,128)(2,1)S(1)} %get-tuple-element.76.refs_2_, bf16[256,512]{1,0:T(8,128)(2,1)S(1)} %get-tuple-element.75.refs_3_, ...), custom_call_target="tpu_custom_call" | custom-call | flops 68719476736 | bytes 6291456 | tf_op jit(solution)/shard_map/pallas_call | solution.py:218
  78.5 2.4 %collective-permute-done.24.refs_3_ = bf16[10,512,256]{2,1,0:T(8,128)(2,1)S(1)} collective-permute-done((bf16[10,512,256]{2,1,0:T(8,128)(2,1)S(1)}, bf16[10,512,256]{2,1,0:T(8,128)(2,1)S(1)}, u32[]{:S(2)}, u32[]{:S(2)}) %collective-permute-start.24) | collective-permute-done | bytes 2621472 | tf_op jit(solution)/shard_map/ppermute | solution.py:256
  80.9 2.6 %shard_map.70 = bf16[256,1024]{1,0:T(8,128)(2,1)} custom-call(f32[2,256,256]{2,1,0:T(8,128)S(1)} %get-tuple-element.69.refs_0_, bf16[256,4096]{1,0:T(8,128)(2,1)S(1)} %get-tuple-element.70.refs_1_, bf16[6,512,256]{2,1,0:T(8,128)(2,1)S(1)} %collective-permute-done.23.refs_2_, bf16[10,512,256]{2,1,0:T(8,128)(2,1)S(1)} %collective-permute-done.24.refs_3_), custom_call_target="tpu_custom_call" | custom-call | flops 68719476736 | bytes 6291456 | tf_op jit(solution)/shard_map/pallas_call | solution.py:227
  (61 shorter events, 17.9 us)
Async XLA Ops:
  0.0 20.9 %collective-permute-start = (bf16[512,256]{1,0:T(8,128)(2,1)}, bf16[512,256]{1,0:T(8,128)(2,1)S(1)}, u32[]{:S(2)}, u32[]{:S(2)}) collective-permute-start(bf16[512,256]{1,0:T(8,128)(2,1)} %param.11), channel_id=1, source_target_pairs={{0,80},{8,88},{16,64},{24,72},{32,241},{40,249},{48,225},{56,233},... | collective-permute-start | bytes 786440 | tf_op jit(solution)/shard_map/ppermute | solution.py:252
  13.8 16.0 %all-to-all-start = ((f32[16,16,256]{2,1,0:T(8,128)}), f32[16,16,256]{2,1,0:T(8,128)S(1)}, u32[]{:S(2)}, u32[]{:S(2)}) async-start(f32[16,16,256]{2,1,0:T(8,128)} %broadcast_in_dim.13), calls=%async_computation | async-start | bytes 524288 | tf_op jit(solution)/shard_map/all_to_all | solution.py:286
  20.9 14.3 %collective-permute-start.5 = (bf16[1,512,256]{2,1,0:T(8,128)(2,1)S(1)}, bf16[1,512,256]{2,1,0:T(8,128)(2,1)S(1)}, u32[]{:S(2)}, u32[]{:S(2)}) collective-permute-start(bf16[1,512,256]{2,1,0:T(8,128)(2,1)S(1)} %bitcast.146), channel_id=1, source_target_pairs={{0,112},{16,0},{32,16},{48,32},{64,48},{80,64},{96,80},{112,96},{1... | collective-permute-start | bytes 786440 | tf_op jit(solution)/shard_map/ppermute | solution.py:256
  23.5 12.0 %collective-permute-start.4 = (bf16[1,512,256]{2,1,0:T(8,128)(2,1)S(1)}, bf16[1,512,256]{2,1,0:T(8,128)(2,1)S(1)}, u32[]{:S(2)}, u32[]{:S(2)}) collective-permute-start(bf16[1,512,256]{2,1,0:T(8,128)(2,1)S(1)} %bitcast.147), channel_id=1, source_target_pairs={{0,16},{16,32},{32,48},{48,64},{64,80},{80,96},{96,112},{112,0},{1... | collective-permute-start | bytes 786440 | tf_op jit(solution)/shard_map/ppermute | solution.py:256
  23.5 12.0 %collective-permute-start.3 = (bf16[1,512,256]{2,1,0:T(8,128)(2,1)S(1)}, bf16[1,512,256]{2,1,0:T(8,128)(2,1)S(1)}, u32[]{:S(2)}, u32[]{:S(2)}) collective-permute-start(bf16[1,512,256]{2,1,0:T(8,128)(2,1)S(1)} %bitcast.148), channel_id=1, source_target_pairs={{0,128},{128,0},{1,129},{129,1},{2,130},{130,2},{3,131},{131,3},{4... | collective-permute-start | bytes 786440 | tf_op jit(solution)/shard_map/ppermute | solution.py:256
  35.5 8.0 %collective-permute-start.7 = (bf16[1,512,256]{2,1,0:T(8,128)(2,1)S(1)}, bf16[1,512,256]{2,1,0:T(8,128)(2,1)S(1)}, u32[]{:S(2)}, u32[]{:S(2)}) collective-permute-start(bf16[1,512,256]{2,1,0:T(8,128)(2,1)S(1)} %collective-permute-done.4.refs_2_), channel_id=1, source_target_pairs={{0,16},{16,32},{32,48},{48,64},{64,80},{80,96},{96,112},{112,0},{1... | collective-permute-start | bytes 786440 | tf_op jit(solution)/shard_map/ppermute | solution.py:256
  35.8 8.9 %collective-permute-start.8 = (bf16[1,512,256]{2,1,0:T(8,128)(2,1)S(1)}, bf16[1,512,256]{2,1,0:T(8,128)(2,1)S(1)}, u32[]{:S(2)}, u32[]{:S(2)}) collective-permute-start(bf16[1,512,256]{2,1,0:T(8,128)(2,1)S(1)} %collective-permute-done.5.refs_3_), channel_id=1, source_target_pairs={{0,112},{16,0},{32,16},{48,32},{64,48},{80,64},{96,80},{112,96},{1... | collective-permute-start | bytes 786440 | tf_op jit(solution)/shard_map/ppermute | solution.py:256
  38.2 7.7 %collective-permute-start.6 = (bf16[1,256,512]{2,1,0:T(8,128)(2,1)S(1)}, bf16[1,256,512]{2,1,0:T(8,128)(2,1)S(1)}, u32[]{:S(2)}, u32[]{:S(2)}) collective-permute-start(bf16[1,256,512]{2,1,0:T(8,128)(2,1)S(1)} %shard_map.66), channel_id=1, source_target_pairs={{0,1},{1,0},{2,3},{3,2},{4,5},{5,4},{6,7},{7,6},{8,9},{9,8},{10,11... | collective-permute-start | bytes 786440 | tf_op jit(solution)/shard_map/ppermute | solution.py:256
  40.2 8.3 %collective-permute-start.17 = (bf16[1,512,256]{2,1,0:T(8,128)(2,1)S(1)}, bf16[1,512,256]{2,1,0:T(8,128)(2,1)S(1)}, u32[]{:S(2)}, u32[]{:S(2)}) collective-permute-start(bf16[1,512,256]{2,1,0:T(8,128)(2,1)S(1)} %collective-permute-done.3.refs_1_), channel_id=1, source_target_pairs={{0,112},{16,0},{32,16},{48,32},{64,48},{80,64},{96,80},{112,96},{1... | collective-permute-start | bytes 786440 | tf_op jit(solution)/shard_map/ppermute | solution.py:256
  40.9 8.1 %collective-permute-start.16 = (bf16[1,512,256]{2,1,0:T(8,128)(2,1)S(1)}, bf16[1,512,256]{2,1,0:T(8,128)(2,1)S(1)}, u32[]{:S(2)}, u32[]{:S(2)}) collective-permute-start(bf16[1,512,256]{2,1,0:T(8,128)(2,1)S(1)} %collective-permute-done.3.refs_1_), channel_id=1, source_target_pairs={{0,16},{16,32},{32,48},{48,64},{64,80},{80,96},{96,112},{112,0},{1... | collective-permute-start | bytes 786440 | tf_op jit(solution)/shard_map/ppermute | solution.py:256
  43.5 7.9 %collective-permute-start.13 = (bf16[1,512,256]{2,1,0:T(8,128)(2,1)S(1)}, bf16[1,512,256]{2,1,0:T(8,128)(2,1)S(1)}, u32[]{:S(2)}, u32[]{:S(2)}) collective-permute-start(bf16[1,512,256]{2,1,0:T(8,128)(2,1)S(1)} %collective-permute-done.7.refs_4_), channel_id=1, source_target_pairs={{0,128},{128,0},{1,129},{129,1},{2,130},{130,2},{3,131},{131,3},{4... | collective-permute-start | bytes 786440 | tf_op jit(solution)/shard_map/ppermute | solution.py:256
  44.7 9.4 %collective-permute-start.11 = (bf16[1,512,256]{2,1,0:T(8,128)(2,1)S(1)}, bf16[1,512,256]{2,1,0:T(8,128)(2,1)S(1)}, u32[]{:S(2)}, u32[]{:S(2)}) collective-permute-start(bf16[1,512,256]{2,1,0:T(8,128)(2,1)S(1)} %collective-permute-done.7.refs_4_), channel_id=1, source_target_pairs={{0,16},{16,32},{32,48},{48,64},{64,80},{80,96},{96,112},{112,0},{1... | collective-permute-start | bytes 786440 | tf_op jit(solution)/shard_map/ppermute | solution.py:256
  45.9 13.5 %collective-permute-start.10 = (bf16[2,256,512]{2,1,0:T(8,128)(2,1)S(1)}, bf16[2,256,512]{2,1,0:T(8,128)(2,1)S(1)}, u32[]{:S(2)}, u32[]{:S(2)}) collective-permute-start(bf16[2,256,512]{2,1,0:T(8,128)(2,1)S(1)} %constant_dynamic-update-slice_fusion), channel_id=1, source_target_pairs={{0,6},{2,0},{4,2},{6,4},{1,7},{3,1},{5,3},{7,5},{8,14},{10,8},{12,... | collective-permute-start | bytes 1572872 | tf_op jit(solution)/shard_map/ppermute | solution.py:256
  48.5 12.6 %collective-permute-start.9 = (bf16[2,256,512]{2,1,0:T(8,128)(2,1)S(1)}, bf16[2,256,512]{2,1,0:T(8,128)(2,1)S(1)}, u32[]{:S(2)}, u32[]{:S(2)}) collective-permute-start(bf16[2,256,512]{2,1,0:T(8,128)(2,1)S(1)} %constant_dynamic-update-slice_fusion), channel_id=1, source_target_pairs={{0,2},{2,4},{4,6},{6,0},{1,3},{3,5},{5,7},{7,1},{8,10},{10,12},{12... | collective-permute-start | bytes 1572872 | tf_op jit(solution)/shard_map/ppermute | solution.py:256
  48.9 7.2 %collective-permute-start.14 = (bf16[1,512,256]{2,1,0:T(8,128)(2,1)S(1)}, bf16[1,512,256]{2,1,0:T(8,128)(2,1)S(1)}, u32[]{:S(2)}, u32[]{:S(2)}) collective-permute-start(bf16[1,512,256]{2,1,0:T(8,128)(2,1)S(1)} %collective-permute-done.8.refs_5_), channel_id=1, source_target_pairs={{0,128},{128,0},{1,129},{129,1},{2,130},{130,2},{3,131},{131,3},{4... | collective-permute-start | bytes 786440 | tf_op jit(solution)/shard_map/ppermute | solution.py:256
  51.4 5.5 %collective-permute-start.12 = (bf16[1,512,256]{2,1,0:T(8,128)(2,1)S(1)}, bf16[1,512,256]{2,1,0:T(8,128)(2,1)S(1)}, u32[]{:S(2)}, u32[]{:S(2)}) collective-permute-start(bf16[1,512,256]{2,1,0:T(8,128)(2,1)S(1)} %collective-permute-done.8.refs_5_), channel_id=1, source_target_pairs={{0,112},{16,0},{32,16},{48,32},{64,48},{80,64},{96,80},{112,96},{1... | collective-permute-start | bytes 786440 | tf_op jit(solution)/shard_map/ppermute | solution.py:256
  54.1 7.0 %collective-permute-start.15 = (bf16[1,512,256]{2,1,0:T(8,128)(2,1)S(1)}, bf16[1,512,256]{2,1,0:T(8,128)(2,1)S(1)}, u32[]{:S(2)}, u32[]{:S(2)}) collective-permute-start(bf16[1,512,256]{2,1,0:T(8,128)(2,1)S(1)} %collective-permute-done.11.refs_0_), channel_id=1, source_target_pairs={{0,16},{16,32},{32,48},{48,64},{64,80},{80,96},{96,112},{112,0},{1... | collective-permute-start | bytes 786440 | tf_op jit(solution)/shard_map/ppermute | solution.py:256
  56.1 10.1 %collective-permute-start.20 = (bf16[1,512,256]{2,1,0:T(8,128)(2,1)S(1)}, bf16[1,512,256]{2,1,0:T(8,128)(2,1)S(1)}, u32[]{:S(2)}, u32[]{:S(2)}) collective-permute-start(bf16[1,512,256]{2,1,0:T(8,128)(2,1)S(1)} %collective-permute-done.13.refs_2_), channel_id=1, source_target_pairs={{0,16},{16,32},{32,48},{48,64},{64,80},{80,96},{96,112},{112,0},{1... | collective-permute-start | bytes 786440 | tf_op jit(solution)/shard_map/ppermute | solution.py:256
  56.9 15.2 %collective-permute-start.21 = (bf16[1,512,256]{2,1,0:T(8,128)(2,1)S(1)}, bf16[1,512,256]{2,1,0:T(8,128)(2,1)S(1)}, u32[]{:S(2)}, u32[]{:S(2)}) collective-permute-start(bf16[1,512,256]{2,1,0:T(8,128)(2,1)S(1)} %collective-permute-done.14.refs_3_), channel_id=1, source_target_pairs={{0,112},{16,0},{32,16},{48,32},{64,48},{80,64},{96,80},{112,96},{1... | collective-permute-start | bytes 786440 | tf_op jit(solution)/shard_map/ppermute | solution.py:256
  61.1 10.9 %collective-permute-start.18 = (bf16[256,512]{1,0:T(8,128)(2,1)S(1)}, bf16[256,512]{1,0:T(8,128)(2,1)S(1)}, u32[]{:S(2)}, u32[]{:S(2)}) collective-permute-start(bf16[256,512]{1,0:T(8,128)(2,1)S(1)} %get-tuple-element.76.refs_2_), channel_id=1, source_target_pairs={{0,2},{2,4},{4,6},{6,0},{1,3},{3,5},{5,7},{7,1},{8,10},{10,12},{12... | collective-permute-start | bytes 786440 | tf_op jit(solution)/shard_map/ppermute | solution.py:256
  61.3 10.8 %collective-permute-start.22 = (bf16[1,512,256]{2,1,0:T(8,128)(2,1)S(1)}, bf16[1,512,256]{2,1,0:T(8,128)(2,1)S(1)}, u32[]{:S(2)}, u32[]{:S(2)}) collective-permute-start(bf16[1,512,256]{2,1,0:T(8,128)(2,1)S(1)} %collective-permute-done.15.refs_4_), channel_id=1, source_target_pairs={{0,128},{128,0},{1,129},{129,1},{2,130},{130,2},{3,131},{131,3},{4... | collective-permute-start | bytes 786440 | tf_op jit(solution)/shard_map/ppermute | solution.py:256
  63.7 8.4 %collective-permute-start.19 = (bf16[256,512]{1,0:T(8,128)(2,1)S(1)}, bf16[256,512]{1,0:T(8,128)(2,1)S(1)}, u32[]{:S(2)}, u32[]{:S(2)}) collective-permute-start(bf16[256,512]{1,0:T(8,128)(2,1)S(1)} %get-tuple-element.73.refs_5_), channel_id=1, source_target_pairs={{0,6},{2,0},{4,2},{6,4},{1,7},{3,1},{5,3},{7,5},{8,14},{10,8},{12,... | collective-permute-start | bytes 786440 | tf_op jit(solution)/shard_map/ppermute | solution.py:256
  66.2 12.2 %collective-permute-start.23 = (bf16[6,512,256]{2,1,0:T(8,128)(2,1)S(1)}, bf16[6,512,256]{2,1,0:T(8,128)(2,1)S(1)}, u32[]{:S(2)}, u32[]{:S(2)}) collective-permute-start(bf16[6,512,256]{2,1,0:T(8,128)(2,1)S(1)} %shard_map.67.refs_8_), channel_id=1, source_target_pairs={{0,8},{8,0},{1,9},{9,1},{2,10},{10,2},{3,11},{11,3},{4,12},{12,4},... | collective-permute-start | bytes 4718600 | tf_op jit(solution)/shard_map/ppermute | solution.py:256
  72.4 8.5 %collective-permute-start.24 = (bf16[10,512,256]{2,1,0:T(8,128)(2,1)S(1)}, bf16[10,512,256]{2,1,0:T(8,128)(2,1)S(1)}, u32[]{:S(2)}, u32[]{:S(2)}) collective-permute-start(bf16[10,512,256]{2,1,0:T(8,128)(2,1)S(1)} %shard_map.68.refs_9_), channel_id=1, source_target_pairs={{0,8},{8,0},{1,9},{9,1},{2,10},{10,2},{3,11},{11,3},{4,12},{12,4},... | collective-permute-start | bytes 7864328 | tf_op jit(solution)/shard_map/ppermute | solution.py:256
  (11 other events, 37.9 us)

commit v7 on v6

--- a/solution.py
+++ b/solution.py
@@ -214,7 +214,7 @@
     blocks = [pltpu.VMEM((2, 8, 512, 256), BF16)]
     sems = [pltpu.SemaphoreType.DMA((16,))]
     params = pltpu.CompilerParams(vmem_limit_bytes=VMEM_LIMIT)
-    cost = pl.CostEstimate(flops=1 << 36, bytes_accessed=6 << 20, transcendentals=0)
+    cost = pl.CostEstimate(flops=1 << 35, bytes_accessed=6 << 20, transcendentals=0)
     total, gated = pl.pallas_call(
         lambda *refs: own_body(places, len(own), *refs),
         out_shape=[jax.ShapeDtypeStruct((2, ROWS, 256), F32), jax.ShapeDtypeStruct((ROWS, 8 * CHANS), BF16)],
@@ -332,7 +332,7 @@
     places += [(1, 5), (1, 3), (1, 4)]
     far_same, far_cross, *late = together(far_same, far_cross, *late)
     pieces = [v[dy] for v in (pair, pair_up, pair_down) for dy in range(2)] + [far_same, far_cross]
-    stacks = [early, bundle(middle + late)]
+    stacks = [early, bundle(middle, 1 << 36), bundle(late)]
     return project(places, pieces, stacks, [move(stack, "core", 1) for stack in stacks])
 
 

time: 84.1 us -> 83.6 us (level)
  waiting for transfers between devices: 16.6 us -> 14.7 us
  starting transfers between devices: 51.6 us -> 53 us
    ppermute x24 -> x25, waiting for transfers between devices: 15.8 us -> 14.1 us  [move(): lax.ppermute(value, axis, ring({'ylo': 2, 'z': 8, 'core': 2, 'x': 4, 'yhi...]
    ppermute x24 -> x25, starting transfers between devices: 37.3 us -> 38.7 us  [move(): lax.ppermute(value, axis, ring({'ylo': 2, 'z': 8, 'core': 2, 'x': 4, 'yhi...]
  transfers between devices with their start and end apart: 26 -> 27, of which waited for: 15 -> 9; matrix products, arithmetic and copies ran while one was open for 2% -> 2% of each run, Pallas kernels for 9% -> 9%
where the time goes in v7:
time: 83.6 us; the launch traced here: 83.2 us
  starting transfers between devices  53 us (63%)
  waiting for transfers between devices  14.7 us (18%)
  Pallas kernels  9.99 us (12%)
  local copies, waits for them, and re-layouts  4.28 us (5%)
    ppermute x25, starting transfers between devices, move(): lax.ppermute(value, axis, ring({'ylo': 2, 'z': 8, 'core': 2, 'x': 4, 'yhi...  38.7 us
    ppermute x25, waiting for transfers between devices, move(): lax.ppermute(value, axis, ring({'ylo': 2, 'z': 8, 'core': 2, 'x': 4, 'yhi...  14.1 us
    ppermute x1, starting transfers between devices, swap(): return lax.ppermute(block, ('ylo', 'z', 'core', 'x', 'yhi'), pairs)  7.29 us
    all_to_all x1, starting transfers between devices, shards(): lax.all_to_all(jnp.broadcast_to(chip[None], (16, MODES, HALF)), ('ylo', '...  7.05 us
    unnamed x19, local copies, waits for them, and re-layouts  3.45 us
    pallas_call x1, Pallas kernels, shards(): pl.pallas_call(sums_body, out_shape=[tiled, half, half], in_specs=[pl.Blo...  2.93 us
    pallas_call x1, Pallas kernels, project(): pl.pallas_call(lambda *refs: other_body(places, len(other), *refs), out_s...  2.66 us
    pallas_call x1, Pallas kernels, project(): pl.pallas_call(lambda *refs: own_body(places, len(own), *refs), out_shape...  2.08 us
  transfers between devices with their start and end apart: 27, of which 9 were waited for; matrix products, arithmetic and copies ran while one was open for 2% of the time, Pallas kernels for 9%

profile of v7, /device:TPU:1, one launch (start us, length us, event | category | flops | bytes accessed | tf_op | source)
XLA Modules:
  0.0 83.2 jit_solution(5783890548247096393)
XLA Ops:
  0.0 7.3 %collective-permute-start = (bf16[512,256]{1,0:T(8,128)(2,1)}, bf16[512,256]{1,0:T(8,128)(2,1)S(1)}, u32[]{:S(2)}, u32[]{:S(2)}) collective-permute-start(bf16[512,256]{1,0:T(8,128)(2,1)} %param.11), channel_id=1, source_target_pairs={{0,80},{8,88},{16,64},{24,72},{32,241},{40,249},{48,225},{56,233},... | collective-permute-start | bytes 786440 | tf_op jit(solution)/shard_map/ppermute | solution.py:252
  7.3 2.9 %shard_map.64 = (f32[4,256,128]{2,1,0:T(8,128)}, f32[16,256]{1,0:T(8,128)}, f32[16,256]{1,0:T(8,128)}) custom-call(bf16[256,512]{1,0:T(8,128)(2,1)} %inner_hbm.2, bf16[256,512]{1,0:T(8,128)(2,1)} %values_hbm.3, f32[16,512]{1,0:T(8,128)} %decays.1), custom_call_target="tpu_custom_call" | custom-call | flops 4194304 | bytes 2097152 | tf_op jit(solution)/shard_map/pallas_call | solution.py:271
  13.8 7.0 %all-to-all-start = ((f32[16,16,256]{2,1,0:T(8,128)}), f32[16,16,256]{2,1,0:T(8,128)S(1)}, u32[]{:S(2)}, u32[]{:S(2)}) async-start(f32[16,16,256]{2,1,0:T(8,128)} %broadcast_in_dim.13), calls=%async_computation | async-start | bytes 524288 | tf_op jit(solution)/shard_map/all_to_all | solution.py:286
  20.9 1.5 %collective-permute-start.3 = (bf16[1,512,256]{2,1,0:T(8,128)(2,1)S(1)}, bf16[1,512,256]{2,1,0:T(8,128)(2,1)S(1)}, u32[]{:S(2)}, u32[]{:S(2)}) collective-permute-start(bf16[1,512,256]{2,1,0:T(8,128)(2,1)S(1)} %bitcast.146), channel_id=1, source_target_pairs={{0,128},{128,0},{1,129},{129,1},{2,130},{130,2},{3,131},{131,3},{4... | collective-permute-start | bytes 786440 | tf_op jit(solution)/shard_map/ppermute | solution.py:256
  22.3 1.2 %collective-permute-start.4 = (bf16[1,512,256]{2,1,0:T(8,128)(2,1)S(1)}, bf16[1,512,256]{2,1,0:T(8,128)(2,1)S(1)}, u32[]{:S(2)}, u32[]{:S(2)}) collective-permute-start(bf16[1,512,256]{2,1,0:T(8,128)(2,1)S(1)} %bitcast.147), channel_id=1, source_target_pairs={{0,16},{16,32},{32,48},{48,64},{64,80},{80,96},{96,112},{112,0},{1... | collective-permute-start | bytes 786440 | tf_op jit(solution)/shard_map/ppermute | solution.py:256
  23.5 1.5 %collective-permute-start.5 = (bf16[1,512,256]{2,1,0:T(8,128)(2,1)S(1)}, bf16[1,512,256]{2,1,0:T(8,128)(2,1)S(1)}, u32[]{:S(2)}, u32[]{:S(2)}) collective-permute-start(bf16[1,512,256]{2,1,0:T(8,128)(2,1)S(1)} %bitcast.148), channel_id=1, source_target_pairs={{0,112},{16,0},{32,16},{48,32},{64,48},{80,64},{96,80},{112,96},{1... | collective-permute-start | bytes 786440 | tf_op jit(solution)/shard_map/ppermute | solution.py:256
  29.8 3.3 %collective-permute-start.2 = (f32[16,256]{1,0:T(8,128)S(1)}, f32[16,256]{1,0:T(8,128)S(1)}, u32[]{:S(2)}, u32[]{:S(2)}) collective-permute-start(f32[16,256]{1,0:T(8,128)S(1)} %get-tuple-element.71), channel_id=1, source_target_pairs={{0,8},{8,0},{1,9},{9,1},{2,10},{10,2},{3,11},{11,3},{4,12},{12,4},... | collective-permute-start | bytes 49160 | tf_op jit(solution)/shard_map/ppermute | solution.py:256
  34.0 1.1 %shard_map.66 = bf16[1,256,512]{2,1,0:T(8,128)(2,1)S(1)} custom-call(bf16[256,512]{1,0:T(8,128)(2,1)S(1)} %copy-done.3, f32[4,256,128]{2,1,0:T(8,128)S(1)} %copy-done, f32[4,256,128]{2,1,0:T(8,128)S(1)} %shard_map.65.local, f32[16,256]{1,0:T(8,128)S(1)} %fusion.31.near, f32[16,256]{1,0:T(8,128)S(1)} %collective-permute-done.2.far, f32[16,512]{1,0:T(8,128)S(1)} %copy-done.7, ...), custom_call_target="tpu_custom_call" | custom-call | tf_op jit(solution)/shard_map/pallas_call | solution.py:26
  35.8 2.1 %collective-permute-start.8 = (bf16[1,512,256]{2,1,0:T(8,128)(2,1)S(1)}, bf16[1,512,256]{2,1,0:T(8,128)(2,1)S(1)}, u32[]{:S(2)}, u32[]{:S(2)}) collective-permute-start(bf16[1,512,256]{2,1,0:T(8,128)(2,1)S(1)} %collective-permute-done.5.refs_3_), channel_id=1, source_target_pairs={{0,112},{16,0},{32,16},{48,32},{64,48},{80,64},{96,80},{112,96},{1... | collective-permute-start | bytes 786440 | tf_op jit(solution)/shard_map/ppermute | solution.py:256
  37.9 2.0 %collective-permute-start.6 = (bf16[1,256,512]{2,1,0:T(8,128)(2,1)S(1)}, bf16[1,256,512]{2,1,0:T(8,128)(2,1)S(1)}, u32[]{:S(2)}, u32[]{:S(2)}) collective-permute-start(bf16[1,256,512]{2,1,0:T(8,128)(2,1)S(1)} %shard_map.66), channel_id=1, source_target_pairs={{0,1},{1,0},{2,3},{3,2},{4,5},{5,4},{6,7},{7,6},{8,9},{9,8},{10,11... | collective-permute-start | bytes 786440 | tf_op jit(solution)/shard_map/ppermute | solution.py:256
  40.0 2.7 %collective-permute-start.17 = (bf16[1,512,256]{2,1,0:T(8,128)(2,1)S(1)}, bf16[1,512,256]{2,1,0:T(8,128)(2,1)S(1)}, u32[]{:S(2)}, u32[]{:S(2)}) collective-permute-start(bf16[1,512,256]{2,1,0:T(8,128)(2,1)S(1)} %collective-permute-done.3.refs_1_), channel_id=1, source_target_pairs={{0,112},{16,0},{32,16},{48,32},{64,48},{80,64},{96,80},{112,96},{1... | collective-permute-start | bytes 786440 | tf_op jit(solution)/shard_map/ppermute | solution.py:256
  43.0 2.7 %collective-permute-start.12 = (bf16[1,512,256]{2,1,0:T(8,128)(2,1)S(1)}, bf16[1,512,256]{2,1,0:T(8,128)(2,1)S(1)}, u32[]{:S(2)}, u32[]{:S(2)}) collective-permute-start(bf16[1,512,256]{2,1,0:T(8,128)(2,1)S(1)} %collective-permute-done.8.refs_5_), channel_id=1, source_target_pairs={{0,112},{16,0},{32,16},{48,32},{64,48},{80,64},{96,80},{112,96},{1... | collective-permute-start | bytes 786440 | tf_op jit(solution)/shard_map/ppermute | solution.py:256
  46.8 1.9 %collective-permute-done.16.refs_5_ = bf16[1,512,256]{2,1,0:T(8,128)(2,1)S(1)} collective-permute-done((bf16[1,512,256]{2,1,0:T(8,128)(2,1)S(1)}, bf16[1,512,256]{2,1,0:T(8,128)(2,1)S(1)}, u32[]{:S(2)}, u32[]{:S(2)}) %collective-permute-start.16) | collective-permute-done | bytes 262176 | tf_op jit(solution)/shard_map/ppermute | solution.py:256
  48.7 1.3 %collective-permute-start.13 = (bf16[1,512,256]{2,1,0:T(8,128)(2,1)S(1)}, bf16[1,512,256]{2,1,0:T(8,128)(2,1)S(1)}, u32[]{:S(2)}, u32[]{:S(2)}) collective-permute-start(bf16[1,512,256]{2,1,0:T(8,128)(2,1)S(1)} %collective-permute-done.7.refs_4_), channel_id=1, source_target_pairs={{0,128},{128,0},{1,129},{129,1},{2,130},{130,2},{3,131},{131,3},{4... | collective-permute-start | bytes 786440 | tf_op jit(solution)/shard_map/ppermute | solution.py:256
  50.0 4.3 %collective-permute-done.11.refs_0_ = bf16[1,512,256]{2,1,0:T(8,128)(2,1)S(1)} collective-permute-done((bf16[1,512,256]{2,1,0:T(8,128)(2,1)S(1)}, bf16[1,512,256]{2,1,0:T(8,128)(2,1)S(1)}, u32[]{:S(2)}, u32[]{:S(2)}) %collective-permute-start.11) | collective-permute-done | bytes 262176 | tf_op jit(solution)/shard_map/ppermute | solution.py:256
  54.3 1.3 %collective-permute-start.14 = (bf16[1,512,256]{2,1,0:T(8,128)(2,1)S(1)}, bf16[1,512,256]{2,1,0:T(8,128)(2,1)S(1)}, u32[]{:S(2)}, u32[]{:S(2)}) collective-permute-start(bf16[1,512,256]{2,1,0:T(8,128)(2,1)S(1)} %collective-permute-done.8.refs_5_), channel_id=1, source_target_pairs={{0,128},{128,0},{1,129},{129,1},{2,130},{130,2},{3,131},{131,3},{4... | collective-permute-start | bytes 786440 | tf_op jit(solution)/shard_map/ppermute | solution.py:256
  56.4 1.2 %collective-permute-start.20 = (bf16[1,512,256]{2,1,0:T(8,128)(2,1)S(1)}, bf16[1,512,256]{2,1,0:T(8,128)(2,1)S(1)}, u32[]{:S(2)}, u32[]{:S(2)}) collective-permute-start(bf16[1,512,256]{2,1,0:T(8,128)(2,1)S(1)} %collective-permute-done.13.refs_2_), channel_id=1, source_target_pairs={{0,16},{16,32},{32,48},{48,64},{64,80},{80,96},{96,112},{112,0},{1... | collective-permute-start | bytes 786440 | tf_op jit(solution)/shard_map/ppermute | solution.py:256
  57.7 5.0 %collective-permute-done.14.refs_3_ = bf16[1,512,256]{2,1,0:T(8,128)(2,1)S(1)} collective-permute-done((bf16[1,512,256]{2,1,0:T(8,128)(2,1)S(1)}, bf16[1,512,256]{2,1,0:T(8,128)(2,1)S(1)}, u32[]{:S(2)}, u32[]{:S(2)}) %collective-permute-start.14) | collective-permute-done | bytes 262176 | tf_op jit(solution)/shard_map/ppermute | solution.py:256
  62.6 1.8 %collective-permute-start.21 = (bf16[1,512,256]{2,1,0:T(8,128)(2,1)S(1)}, bf16[1,512,256]{2,1,0:T(8,128)(2,1)S(1)}, u32[]{:S(2)}, u32[]{:S(2)}) collective-permute-start(bf16[1,512,256]{2,1,0:T(8,128)(2,1)S(1)} %collective-permute-done.14.refs_3_), channel_id=1, source_target_pairs={{0,112},{16,0},{32,16},{48,32},{64,48},{80,64},{96,80},{112,96},{1... | collective-permute-start | bytes 786440 | tf_op jit(solution)/shard_map/ppermute | solution.py:256
  64.6 2.7 %collective-permute-start.19 = (bf16[256,512]{1,0:T(8,128)(2,1)S(1)}, bf16[256,512]{1,0:T(8,128)(2,1)S(1)}, u32[]{:S(2)}, u32[]{:S(2)}) collective-permute-start(bf16[256,512]{1,0:T(8,128)(2,1)S(1)} %get-tuple-element.73.refs_5_), channel_id=1, source_target_pairs={{0,6},{2,0},{4,2},{6,4},{1,7},{3,1},{5,3},{7,5},{8,14},{10,8},{12,... | collective-permute-start | bytes 786440 | tf_op jit(solution)/shard_map/ppermute | solution.py:256
  68.1 4.5 %collective-permute-start.24 = (bf16[7,512,256]{2,1,0:T(8,128)(2,1)S(1)}, bf16[7,512,256]{2,1,0:T(8,128)(2,1)S(1)}, u32[]{:S(2)}, u32[]{:S(2)}) collective-permute-start(bf16[7,512,256]{2,1,0:T(8,128)(2,1)S(1)} %shard_map.68.refs_9_), channel_id=1, source_target_pairs={{0,8},{8,0},{1,9},{9,1},{2,10},{10,2},{3,11},{11,3},{4,12},{12,4},... | collective-permute-start | bytes 5505032 | tf_op jit(solution)/shard_map/ppermute | solution.py:256
  73.0 5.2 %collective-permute-start.25 = (bf16[3,512,256]{2,1,0:T(8,128)(2,1)S(1)}, bf16[3,512,256]{2,1,0:T(8,128)(2,1)S(1)}, u32[]{:S(2)}, u32[]{:S(2)}) collective-permute-start(bf16[3,512,256]{2,1,0:T(8,128)(2,1)S(1)} %shard_map.69.refs_10_), channel_id=1, source_target_pairs={{0,8},{8,0},{1,9},{9,1},{2,10},{10,2},{3,11},{11,3},{4,12},{12,4},... | collective-permute-start | bytes 2359304 | tf_op jit(solution)/shard_map/ppermute | solution.py:256
  78.2 2.1 %shard_map.70 = (f32[2,256,256]{2,1,0:T(8,128)S(1)}, bf16[256,4096]{1,0:T(8,128)(2,1)S(1)}) custom-call(bf16[256,512]{1,0:T(8,128)(2,1)S(1)} %bitcast.144, bf16[256,512]{1,0:T(8,128)(2,1)S(1)} %bitcast.145, bf16[256,512]{1,0:T(8,128)(2,1)S(1)} %get-tuple-element.76.refs_2_, bf16[256,512]{1,0:T(8,128)(2,1)S(1)} %get-tuple-element.75.refs_3_, ...), custom_call_target="tpu_custom_call" | custom-call | flops 34359738368 | bytes 6291456 | tf_op jit(solution)/shard_map/pallas_call | solution.py:218
  80.4 2.7 %shard_map.71 = bf16[256,1024]{1,0:T(8,128)(2,1)} custom-call(f32[2,256,256]{2,1,0:T(8,128)S(1)} %get-tuple-element.69.refs_0_, bf16[256,4096]{1,0:T(8,128)(2,1)S(1)} %get-tuple-element.70.refs_1_, bf16[6,512,256]{2,1,0:T(8,128)(2,1)S(1)} %collective-permute-done.23.refs_2_, bf16[7,512,256]{2,1,0:T(8,128)(2,1)S(1)} %collective-permute-done.24.refs_3_, ...), custom_call_target="tpu_custom_call" | custom-call | flops 34359738368 | bytes 6291456 | tf_op jit(solution)/shard_map/pallas_call | solution.py:227
  (64 shorter events, 13.4 us)
Async XLA Ops:
  0.0 20.9 %collective-permute-start = (bf16[512,256]{1,0:T(8,128)(2,1)}, bf16[512,256]{1,0:T(8,128)(2,1)S(1)}, u32[]{:S(2)}, u32[]{:S(2)}) collective-permute-start(bf16[512,256]{1,0:T(8,128)(2,1)} %param.11), channel_id=1, source_target_pairs={{0,80},{8,88},{16,64},{24,72},{32,241},{40,249},{48,225},{56,233},... | collective-permute-start | bytes 786440 | tf_op jit(solution)/shard_map/ppermute | solution.py:252
  13.8 16.0 %all-to-all-start = ((f32[16,16,256]{2,1,0:T(8,128)}), f32[16,16,256]{2,1,0:T(8,128)S(1)}, u32[]{:S(2)}, u32[]{:S(2)}) async-start(f32[16,16,256]{2,1,0:T(8,128)} %broadcast_in_dim.13), calls=%async_computation | async-start | bytes 524288 | tf_op jit(solution)/shard_map/all_to_all | solution.py:286
  20.9 14.3 %collective-permute-start.3 = (bf16[1,512,256]{2,1,0:T(8,128)(2,1)S(1)}, bf16[1,512,256]{2,1,0:T(8,128)(2,1)S(1)}, u32[]{:S(2)}, u32[]{:S(2)}) collective-permute-start(bf16[1,512,256]{2,1,0:T(8,128)(2,1)S(1)} %bitcast.146), channel_id=1, source_target_pairs={{0,128},{128,0},{1,129},{129,1},{2,130},{130,2},{3,131},{131,3},{4... | collective-permute-start | bytes 786440 | tf_op jit(solution)/shard_map/ppermute | solution.py:256
  22.3 12.8 %collective-permute-start.4 = (bf16[1,512,256]{2,1,0:T(8,128)(2,1)S(1)}, bf16[1,512,256]{2,1,0:T(8,128)(2,1)S(1)}, u32[]{:S(2)}, u32[]{:S(2)}) collective-permute-start(bf16[1,512,256]{2,1,0:T(8,128)(2,1)S(1)} %bitcast.147), channel_id=1, source_target_pairs={{0,16},{16,32},{32,48},{48,64},{64,80},{80,96},{96,112},{112,0},{1... | collective-permute-start | bytes 786440 | tf_op jit(solution)/shard_map/ppermute | solution.py:256
  23.5 11.7 %collective-permute-start.5 = (bf16[1,512,256]{2,1,0:T(8,128)(2,1)S(1)}, bf16[1,512,256]{2,1,0:T(8,128)(2,1)S(1)}, u32[]{:S(2)}, u32[]{:S(2)}) collective-permute-start(bf16[1,512,256]{2,1,0:T(8,128)(2,1)S(1)} %bitcast.148), channel_id=1, source_target_pairs={{0,112},{16,0},{32,16},{48,32},{64,48},{80,64},{96,80},{112,96},{1... | collective-permute-start | bytes 786440 | tf_op jit(solution)/shard_map/ppermute | solution.py:256
  35.2 7.8 %collective-permute-start.7 = (bf16[1,512,256]{2,1,0:T(8,128)(2,1)S(1)}, bf16[1,512,256]{2,1,0:T(8,128)(2,1)S(1)}, u32[]{:S(2)}, u32[]{:S(2)}) collective-permute-start(bf16[1,512,256]{2,1,0:T(8,128)(2,1)S(1)} %collective-permute-done.4.refs_2_), channel_id=1, source_target_pairs={{0,16},{16,32},{32,48},{48,64},{64,80},{80,96},{96,112},{112,0},{1... | collective-permute-start | bytes 786440 | tf_op jit(solution)/shard_map/ppermute | solution.py:256
  35.8 7.2 %collective-permute-start.8 = (bf16[1,512,256]{2,1,0:T(8,128)(2,1)S(1)}, bf16[1,512,256]{2,1,0:T(8,128)(2,1)S(1)}, u32[]{:S(2)}, u32[]{:S(2)}) collective-permute-start(bf16[1,512,256]{2,1,0:T(8,128)(2,1)S(1)} %collective-permute-done.5.refs_3_), channel_id=1, source_target_pairs={{0,112},{16,0},{32,16},{48,32},{64,48},{80,64},{96,80},{112,96},{1... | collective-permute-start | bytes 786440 | tf_op jit(solution)/shard_map/ppermute | solution.py:256
  37.9 7.8 %collective-permute-start.6 = (bf16[1,256,512]{2,1,0:T(8,128)(2,1)S(1)}, bf16[1,256,512]{2,1,0:T(8,128)(2,1)S(1)}, u32[]{:S(2)}, u32[]{:S(2)}) collective-permute-start(bf16[1,256,512]{2,1,0:T(8,128)(2,1)S(1)} %shard_map.66), channel_id=1, source_target_pairs={{0,1},{1,0},{2,3},{3,2},{4,5},{5,4},{6,7},{7,6},{8,9},{9,8},{10,11... | collective-permute-start | bytes 786440 | tf_op jit(solution)/shard_map/ppermute | solution.py:256
  40.0 8.7 %collective-permute-start.16 = (bf16[1,512,256]{2,1,0:T(8,128)(2,1)S(1)}, bf16[1,512,256]{2,1,0:T(8,128)(2,1)S(1)}, u32[]{:S(2)}, u32[]{:S(2)}) collective-permute-start(bf16[1,512,256]{2,1,0:T(8,128)(2,1)S(1)} %collective-permute-done.3.refs_1_), channel_id=1, source_target_pairs={{0,16},{16,32},{32,48},{48,64},{64,80},{80,96},{96,112},{112,0},{1... | collective-permute-start | bytes 786440 | tf_op jit(solution)/shard_map/ppermute | solution.py:256
  40.0 8.7 %collective-permute-start.17 = (bf16[1,512,256]{2,1,0:T(8,128)(2,1)S(1)}, bf16[1,512,256]{2,1,0:T(8,128)(2,1)S(1)}, u32[]{:S(2)}, u32[]{:S(2)}) collective-permute-start(bf16[1,512,256]{2,1,0:T(8,128)(2,1)S(1)} %collective-permute-done.3.refs_1_), channel_id=1, source_target_pairs={{0,112},{16,0},{32,16},{48,32},{64,48},{80,64},{96,80},{112,96},{1... | collective-permute-start | bytes 786440 | tf_op jit(solution)/shard_map/ppermute | solution.py:256
  43.0 11.3 %collective-permute-start.11 = (bf16[1,512,256]{2,1,0:T(8,128)(2,1)S(1)}, bf16[1,512,256]{2,1,0:T(8,128)(2,1)S(1)}, u32[]{:S(2)}, u32[]{:S(2)}) collective-permute-start(bf16[1,512,256]{2,1,0:T(8,128)(2,1)S(1)} %collective-permute-done.7.refs_4_), channel_id=1, source_target_pairs={{0,16},{16,32},{32,48},{48,64},{64,80},{80,96},{96,112},{112,0},{1... | collective-permute-start | bytes 786440 | tf_op jit(solution)/shard_map/ppermute | solution.py:256
  43.0 12.6 %collective-permute-start.12 = (bf16[1,512,256]{2,1,0:T(8,128)(2,1)S(1)}, bf16[1,512,256]{2,1,0:T(8,128)(2,1)S(1)}, u32[]{:S(2)}, u32[]{:S(2)}) collective-permute-start(bf16[1,512,256]{2,1,0:T(8,128)(2,1)S(1)} %collective-permute-done.8.refs_5_), channel_id=1, source_target_pairs={{0,112},{16,0},{32,16},{48,32},{64,48},{80,64},{96,80},{112,96},{1... | collective-permute-start | bytes 786440 | tf_op jit(solution)/shard_map/ppermute | solution.py:256
  45.7 18.7 %collective-permute-start.10 = (bf16[2,256,512]{2,1,0:T(8,128)(2,1)S(1)}, bf16[2,256,512]{2,1,0:T(8,128)(2,1)S(1)}, u32[]{:S(2)}, u32[]{:S(2)}) collective-permute-start(bf16[2,256,512]{2,1,0:T(8,128)(2,1)S(1)} %constant_dynamic-update-slice_fusion), channel_id=1, source_target_pairs={{0,6},{2,0},{4,2},{6,4},{1,7},{3,1},{5,3},{7,5},{8,14},{10,8},{12,... | collective-permute-start | bytes 1572872 | tf_op jit(solution)/shard_map/ppermute | solution.py:256
  48.7 15.8 %collective-permute-start.9 = (bf16[2,256,512]{2,1,0:T(8,128)(2,1)S(1)}, bf16[2,256,512]{2,1,0:T(8,128)(2,1)S(1)}, u32[]{:S(2)}, u32[]{:S(2)}) collective-permute-start(bf16[2,256,512]{2,1,0:T(8,128)(2,1)S(1)} %constant_dynamic-update-slice_fusion), channel_id=1, source_target_pairs={{0,2},{2,4},{4,6},{6,0},{1,3},{3,5},{5,7},{7,1},{8,10},{10,12},{12... | collective-permute-start | bytes 1572872 | tf_op jit(solution)/shard_map/ppermute | solution.py:256
  48.7 7.7 %collective-permute-start.13 = (bf16[1,512,256]{2,1,0:T(8,128)(2,1)S(1)}, bf16[1,512,256]{2,1,0:T(8,128)(2,1)S(1)}, u32[]{:S(2)}, u32[]{:S(2)}) collective-permute-start(bf16[1,512,256]{2,1,0:T(8,128)(2,1)S(1)} %collective-permute-done.7.refs_4_), channel_id=1, source_target_pairs={{0,128},{128,0},{1,129},{129,1},{2,130},{130,2},{3,131},{131,3},{4... | collective-permute-start | bytes 786440 | tf_op jit(solution)/shard_map/ppermute | solution.py:256
  54.3 8.3 %collective-permute-start.14 = (bf16[1,512,256]{2,1,0:T(8,128)(2,1)S(1)}, bf16[1,512,256]{2,1,0:T(8,128)(2,1)S(1)}, u32[]{:S(2)}, u32[]{:S(2)}) collective-permute-start(bf16[1,512,256]{2,1,0:T(8,128)(2,1)S(1)} %collective-permute-done.8.refs_5_), channel_id=1, source_target_pairs={{0,128},{128,0},{1,129},{129,1},{2,130},{130,2},{3,131},{131,3},{4... | collective-permute-start | bytes 786440 | tf_op jit(solution)/shard_map/ppermute | solution.py:256
  55.6 8.8 %collective-permute-start.15 = (bf16[1,512,256]{2,1,0:T(8,128)(2,1)S(1)}, bf16[1,512,256]{2,1,0:T(8,128)(2,1)S(1)}, u32[]{:S(2)}, u32[]{:S(2)}) collective-permute-start(bf16[1,512,256]{2,1,0:T(8,128)(2,1)S(1)} %collective-permute-done.11.refs_0_), channel_id=1, source_target_pairs={{0,16},{16,32},{32,48},{48,64},{64,80},{80,96},{96,112},{112,0},{1... | collective-permute-start | bytes 786440 | tf_op jit(solution)/shard_map/ppermute | solution.py:256
  56.4 11.7 %collective-permute-start.20 = (bf16[1,512,256]{2,1,0:T(8,128)(2,1)S(1)}, bf16[1,512,256]{2,1,0:T(8,128)(2,1)S(1)}, u32[]{:S(2)}, u32[]{:S(2)}) collective-permute-start(bf16[1,512,256]{2,1,0:T(8,128)(2,1)S(1)} %collective-permute-done.13.refs_2_), channel_id=1, source_target_pairs={{0,16},{16,32},{32,48},{48,64},{64,80},{80,96},{96,112},{112,0},{1... | collective-permute-start | bytes 786440 | tf_op jit(solution)/shard_map/ppermute | solution.py:256
  62.6 10.0 %collective-permute-start.21 = (bf16[1,512,256]{2,1,0:T(8,128)(2,1)S(1)}, bf16[1,512,256]{2,1,0:T(8,128)(2,1)S(1)}, u32[]{:S(2)}, u32[]{:S(2)}) collective-permute-start(bf16[1,512,256]{2,1,0:T(8,128)(2,1)S(1)} %collective-permute-done.14.refs_3_), channel_id=1, source_target_pairs={{0,112},{16,0},{32,16},{48,32},{64,48},{80,64},{96,80},{112,96},{1... | collective-permute-start | bytes 786440 | tf_op jit(solution)/shard_map/ppermute | solution.py:256
  64.5 8.2 %collective-permute-start.18 = (bf16[256,512]{1,0:T(8,128)(2,1)S(1)}, bf16[256,512]{1,0:T(8,128)(2,1)S(1)}, u32[]{:S(2)}, u32[]{:S(2)}) collective-permute-start(bf16[256,512]{1,0:T(8,128)(2,1)S(1)} %get-tuple-element.76.refs_2_), channel_id=1, source_target_pairs={{0,2},{2,4},{4,6},{6,0},{1,3},{3,5},{5,7},{7,1},{8,10},{10,12},{12... | collective-permute-start | bytes 786440 | tf_op jit(solution)/shard_map/ppermute | solution.py:256
  64.6 8.0 %collective-permute-start.19 = (bf16[256,512]{1,0:T(8,128)(2,1)S(1)}, bf16[256,512]{1,0:T(8,128)(2,1)S(1)}, u32[]{:S(2)}, u32[]{:S(2)}) collective-permute-start(bf16[256,512]{1,0:T(8,128)(2,1)S(1)} %get-tuple-element.73.refs_5_), channel_id=1, source_target_pairs={{0,6},{2,0},{4,2},{6,4},{1,7},{3,1},{5,3},{7,5},{8,14},{10,8},{12,... | collective-permute-start | bytes 786440 | tf_op jit(solution)/shard_map/ppermute | solution.py:256
  68.1 12.2 %collective-permute-start.24 = (bf16[7,512,256]{2,1,0:T(8,128)(2,1)S(1)}, bf16[7,512,256]{2,1,0:T(8,128)(2,1)S(1)}, u32[]{:S(2)}, u32[]{:S(2)}) collective-permute-start(bf16[7,512,256]{2,1,0:T(8,128)(2,1)S(1)} %shard_map.68.refs_9_), channel_id=1, source_target_pairs={{0,8},{8,0},{1,9},{9,1},{2,10},{10,2},{3,11},{11,3},{4,12},{12,4},... | collective-permute-start | bytes 5505032 | tf_op jit(solution)/shard_map/ppermute | solution.py:256
  72.6 7.8 %collective-permute-start.23 = (bf16[6,512,256]{2,1,0:T(8,128)(2,1)S(1)}, bf16[6,512,256]{2,1,0:T(8,128)(2,1)S(1)}, u32[]{:S(2)}, u32[]{:S(2)}) collective-permute-start(bf16[6,512,256]{2,1,0:T(8,128)(2,1)S(1)} %shard_map.67.refs_8_), channel_id=1, source_target_pairs={{0,8},{8,0},{1,9},{9,1},{2,10},{10,2},{3,11},{11,3},{4,12},{12,4},... | collective-permute-start | bytes 4718600 | tf_op jit(solution)/shard_map/ppermute | solution.py:256
  73.0 7.3 %collective-permute-start.25 = (bf16[3,512,256]{2,1,0:T(8,128)(2,1)S(1)}, bf16[3,512,256]{2,1,0:T(8,128)(2,1)S(1)}, u32[]{:S(2)}, u32[]{:S(2)}) collective-permute-start(bf16[3,512,256]{2,1,0:T(8,128)(2,1)S(1)} %shard_map.69.refs_10_), channel_id=1, source_target_pairs={{0,8},{8,0},{1,9},{9,1},{2,10},{10,2},{3,11},{11,3},{4,12},{12,4},... | collective-permute-start | bytes 2359304 | tf_op jit(solution)/shard_map/ppermute | solution.py:256
  (12 other events, 42.2 us)

commit v8 on v7

--- a/solution.py
+++ b/solution.py
@@ -34,11 +34,15 @@
     )(*args)
 
 
+def signal_tile(inner, values, sig, lt):
+    cols = slice(lt * LANES, (lt + 1) * LANES)
+    product = inner[:, cols].astype(F32) * values[:, cols].astype(F32)
+    sig[lt] = product.astype(BF16).astype(F32)
+
+
 def signal_into(inner, values, sig):
     for lt in range(TILES):
-        cols = slice(lt * LANES, (lt + 1) * LANES)
-        product = inner[:, cols].astype(F32) * values[:, cols].astype(F32)
-        sig[lt] = product.astype(BF16).astype(F32)
+        signal_tile(inner, values, sig, lt)
 
 
 def load(sems, *pairs):
@@ -50,10 +54,19 @@
 
 
 def sums_body(inner_hbm, values_hbm, decays_hbm, sums, keep, send, sig, inner, values, decays, sems):
-    load(sems, (decays_hbm, decays), (inner_hbm, inner), (values_hbm, values))
-    signal_into(inner, values, sig)
-    for lt in range(TILES):
-        cols = slice(lt * LANES, (lt + 1) * LANES)
+    copies = [pltpu.make_async_copy(decays_hbm, decays, sems.at[2 * TILES])]
+    for lt in range(TILES):
+        cols = slice(lt * LANES, (lt + 1) * LANES)
+        for i, (source, target) in enumerate(((inner_hbm, inner), (values_hbm, values))):
+            copies.append(pltpu.make_async_copy(source.at[:, cols], target.at[:, cols], sems.at[2 * lt + i]))
+    for copy in copies:
+        copy.start()
+    copies[0].wait()
+    for lt in range(TILES):
+        cols = slice(lt * LANES, (lt + 1) * LANES)
+        copies[1 + 2 * lt].wait()
+        copies[2 + 2 * lt].wait()
+        signal_tile(inner, values, sig, lt)
         fade = jnp.exp(-decays[:, cols])
         for group in range(0, MODES, 8):
             step = [jnp.broadcast_to(fade[r : r + 1], (BLOCKS, LANES)) for r in range(group, group + 8)]
@@ -273,7 +286,7 @@
         out_shape=[tiled, half, half],
         in_specs=[pl.BlockSpec(memory_space=pl.ANY)] * 3,
         out_specs=whole(3),
-        scratch_shapes=[tile_scratch, shard, shard, modes, pltpu.SemaphoreType.DMA((3,))],
+        scratch_shapes=[tile_scratch, shard, shard, modes, pltpu.SemaphoreType.DMA((2 * TILES + 1,))],
         compiler_params=full,
         cost_estimate=pl.CostEstimate(flops=work, bytes_accessed=2 << 20, transcendentals=0),
     )(inner_gate, values, decays)

time: 83.6 us -> 83.6 us (level)
  no operation moved by 1% of the time
where the time goes in v8:
time: 83.6 us; the launch traced here: 83.1 us
  starting transfers between devices  53 us (63%)
  waiting for transfers between devices  14.7 us (18%)
  Pallas kernels  9.9 us (12%)
  local copies, waits for them, and re-layouts  4.28 us (5%)
    ppermute x25, starting transfers between devices, move(): lax.ppermute(value, axis, ring({'ylo': 2, 'z': 8, 'core': 2, 'x': 4, 'yhi...  38.7 us
    ppermute x25, waiting for transfers between devices, move(): lax.ppermute(value, axis, ring({'ylo': 2, 'z': 8, 'core': 2, 'x': 4, 'yhi...  14.1 us
    ppermute x1, starting transfers between devices, swap(): return lax.ppermute(block, ('ylo', 'z', 'core', 'x', 'yhi'), pairs)  7.29 us
    all_to_all x1, starting transfers between devices, shards(): lax.all_to_all(jnp.broadcast_to(chip[None], (16, MODES, HALF)), ('ylo', '...  7.05 us
    unnamed x19, local copies, waits for them, and re-layouts  3.45 us
    pallas_call x1, Pallas kernels, shards(): pl.pallas_call(sums_body, out_shape=[tiled, half, half], in_specs=[pl.Blo...  2.84 us
    pallas_call x1, Pallas kernels, project(): pl.pallas_call(lambda *refs: other_body(places, len(other), *refs), out_s...  2.66 us
    pallas_call x1, Pallas kernels, project(): pl.pallas_call(lambda *refs: own_body(places, len(own), *refs), out_shape...  2.08 us
  transfers between devices with their start and end apart: 27, of which 9 were waited for; matrix products, arithmetic and copies ran while one was open for 2% of the time, Pallas kernels for 9%

profile of v8, /device:TPU:1, one launch (start us, length us, event | category | flops | bytes accessed | tf_op | source)
XLA Modules:
  0.0 83.1 jit_solution(5628348451809053485)
XLA Ops:
  0.0 7.3 %collective-permute-start = (bf16[512,256]{1,0:T(8,128)(2,1)}, bf16[512,256]{1,0:T(8,128)(2,1)S(1)}, u32[]{:S(2)}, u32[]{:S(2)}) collective-permute-start(bf16[512,256]{1,0:T(8,128)(2,1)} %param.11), channel_id=1, source_target_pairs={{0,80},{8,88},{16,64},{24,72},{32,241},{40,249},{48,225},{56,233},... | collective-permute-start | bytes 786440 | tf_op jit(solution)/shard_map/ppermute | solution.py:265
  7.3 2.8 %shard_map.64 = (f32[4,256,128]{2,1,0:T(8,128)}, f32[16,256]{1,0:T(8,128)}, f32[16,256]{1,0:T(8,128)}) custom-call(bf16[256,512]{1,0:T(8,128)(2,1)} %inner_hbm.2, bf16[256,512]{1,0:T(8,128)(2,1)} %values_hbm.3, f32[16,512]{1,0:T(8,128)} %decays.1), custom_call_target="tpu_custom_call" | custom-call | flops 4194304 | bytes 2097152 | tf_op jit(solution)/shard_map/pallas_call | solution.py:284
  13.7 7.0 %all-to-all-start = ((f32[16,16,256]{2,1,0:T(8,128)}), f32[16,16,256]{2,1,0:T(8,128)S(1)}, u32[]{:S(2)}, u32[]{:S(2)}) async-start(f32[16,16,256]{2,1,0:T(8,128)} %broadcast_in_dim.13), calls=%async_computation | async-start | bytes 524288 | tf_op jit(solution)/shard_map/all_to_all | solution.py:299
  20.8 1.5 %collective-permute-start.3 = (bf16[1,512,256]{2,1,0:T(8,128)(2,1)S(1)}, bf16[1,512,256]{2,1,0:T(8,128)(2,1)S(1)}, u32[]{:S(2)}, u32[]{:S(2)}) collective-permute-start(bf16[1,512,256]{2,1,0:T(8,128)(2,1)S(1)} %bitcast.146), channel_id=1, source_target_pairs={{0,128},{128,0},{1,129},{129,1},{2,130},{130,2},{3,131},{131,3},{4... | collective-permute-start | bytes 786440 | tf_op jit(solution)/shard_map/ppermute | solution.py:269
  22.2 1.2 %collective-permute-start.4 = (bf16[1,512,256]{2,1,0:T(8,128)(2,1)S(1)}, bf16[1,512,256]{2,1,0:T(8,128)(2,1)S(1)}, u32[]{:S(2)}, u32[]{:S(2)}) collective-permute-start(bf16[1,512,256]{2,1,0:T(8,128)(2,1)S(1)} %bitcast.147), channel_id=1, source_target_pairs={{0,16},{16,32},{32,48},{48,64},{64,80},{80,96},{96,112},{112,0},{1... | collective-permute-start | bytes 786440 | tf_op jit(solution)/shard_map/ppermute | solution.py:269
  23.4 1.5 %collective-permute-start.5 = (bf16[1,512,256]{2,1,0:T(8,128)(2,1)S(1)}, bf16[1,512,256]{2,1,0:T(8,128)(2,1)S(1)}, u32[]{:S(2)}, u32[]{:S(2)}) collective-permute-start(bf16[1,512,256]{2,1,0:T(8,128)(2,1)S(1)} %bitcast.148), channel_id=1, source_target_pairs={{0,112},{16,0},{32,16},{48,32},{64,48},{80,64},{96,80},{112,96},{1... | collective-permute-start | bytes 786440 | tf_op jit(solution)/shard_map/ppermute | solution.py:269
  29.7 3.3 %collective-permute-start.2 = (f32[16,256]{1,0:T(8,128)S(1)}, f32[16,256]{1,0:T(8,128)S(1)}, u32[]{:S(2)}, u32[]{:S(2)}) collective-permute-start(f32[16,256]{1,0:T(8,128)S(1)} %get-tuple-element.71), channel_id=1, source_target_pairs={{0,8},{8,0},{1,9},{9,1},{2,10},{10,2},{3,11},{11,3},{4,12},{12,4},... | collective-permute-start | bytes 49160 | tf_op jit(solution)/shard_map/ppermute | solution.py:269
  33.9 1.1 %shard_map.66 = bf16[1,256,512]{2,1,0:T(8,128)(2,1)S(1)} custom-call(bf16[256,512]{1,0:T(8,128)(2,1)S(1)} %copy-done.3, f32[4,256,128]{2,1,0:T(8,128)S(1)} %copy-done, f32[4,256,128]{2,1,0:T(8,128)S(1)} %shard_map.65.local, f32[16,256]{1,0:T(8,128)S(1)} %fusion.31.near, f32[16,256]{1,0:T(8,128)S(1)} %collective-permute-done.2.far, f32[16,512]{1,0:T(8,128)S(1)} %copy-done.7, ...), custom_call_target="tpu_custom_call" | custom-call | tf_op jit(solution)/shard_map/pallas_call | solution.py:26
  35.7 2.1 %collective-permute-start.8 = (bf16[1,512,256]{2,1,0:T(8,128)(2,1)S(1)}, bf16[1,512,256]{2,1,0:T(8,128)(2,1)S(1)}, u32[]{:S(2)}, u32[]{:S(2)}) collective-permute-start(bf16[1,512,256]{2,1,0:T(8,128)(2,1)S(1)} %collective-permute-done.5.refs_3_), channel_id=1, source_target_pairs={{0,112},{16,0},{32,16},{48,32},{64,48},{80,64},{96,80},{112,96},{1... | collective-permute-start | bytes 786440 | tf_op jit(solution)/shard_map/ppermute | solution.py:269
  37.9 2.0 %collective-permute-start.6 = (bf16[1,256,512]{2,1,0:T(8,128)(2,1)S(1)}, bf16[1,256,512]{2,1,0:T(8,128)(2,1)S(1)}, u32[]{:S(2)}, u32[]{:S(2)}) collective-permute-start(bf16[1,256,512]{2,1,0:T(8,128)(2,1)S(1)} %shard_map.66), channel_id=1, source_target_pairs={{0,1},{1,0},{2,3},{3,2},{4,5},{5,4},{6,7},{7,6},{8,9},{9,8},{10,11... | collective-permute-start | bytes 786440 | tf_op jit(solution)/shard_map/ppermute | solution.py:269
  39.9 2.7 %collective-permute-start.17 = (bf16[1,512,256]{2,1,0:T(8,128)(2,1)S(1)}, bf16[1,512,256]{2,1,0:T(8,128)(2,1)S(1)}, u32[]{:S(2)}, u32[]{:S(2)}) collective-permute-start(bf16[1,512,256]{2,1,0:T(8,128)(2,1)S(1)} %collective-permute-done.3.refs_1_), channel_id=1, source_target_pairs={{0,112},{16,0},{32,16},{48,32},{64,48},{80,64},{96,80},{112,96},{1... | collective-permute-start | bytes 786440 | tf_op jit(solution)/shard_map/ppermute | solution.py:269
  42.9 2.7 %collective-permute-start.12 = (bf16[1,512,256]{2,1,0:T(8,128)(2,1)S(1)}, bf16[1,512,256]{2,1,0:T(8,128)(2,1)S(1)}, u32[]{:S(2)}, u32[]{:S(2)}) collective-permute-start(bf16[1,512,256]{2,1,0:T(8,128)(2,1)S(1)} %collective-permute-done.8.refs_5_), channel_id=1, source_target_pairs={{0,112},{16,0},{32,16},{48,32},{64,48},{80,64},{96,80},{112,96},{1... | collective-permute-start | bytes 786440 | tf_op jit(solution)/shard_map/ppermute | solution.py:269
  46.8 1.9 %collective-permute-done.16.refs_5_ = bf16[1,512,256]{2,1,0:T(8,128)(2,1)S(1)} collective-permute-done((bf16[1,512,256]{2,1,0:T(8,128)(2,1)S(1)}, bf16[1,512,256]{2,1,0:T(8,128)(2,1)S(1)}, u32[]{:S(2)}, u32[]{:S(2)}) %collective-permute-start.16) | collective-permute-done | bytes 262176 | tf_op jit(solution)/shard_map/ppermute | solution.py:269
  48.6 1.3 %collective-permute-start.13 = (bf16[1,512,256]{2,1,0:T(8,128)(2,1)S(1)}, bf16[1,512,256]{2,1,0:T(8,128)(2,1)S(1)}, u32[]{:S(2)}, u32[]{:S(2)}) collective-permute-start(bf16[1,512,256]{2,1,0:T(8,128)(2,1)S(1)} %collective-permute-done.7.refs_4_), channel_id=1, source_target_pairs={{0,128},{128,0},{1,129},{129,1},{2,130},{130,2},{3,131},{131,3},{4... | collective-permute-start | bytes 786440 | tf_op jit(solution)/shard_map/ppermute | solution.py:269
  49.9 4.3 %collective-permute-done.11.refs_0_ = bf16[1,512,256]{2,1,0:T(8,128)(2,1)S(1)} collective-permute-done((bf16[1,512,256]{2,1,0:T(8,128)(2,1)S(1)}, bf16[1,512,256]{2,1,0:T(8,128)(2,1)S(1)}, u32[]{:S(2)}, u32[]{:S(2)}) %collective-permute-start.11) | collective-permute-done | bytes 262176 | tf_op jit(solution)/shard_map/ppermute | solution.py:269
  54.2 1.3 %collective-permute-start.14 = (bf16[1,512,256]{2,1,0:T(8,128)(2,1)S(1)}, bf16[1,512,256]{2,1,0:T(8,128)(2,1)S(1)}, u32[]{:S(2)}, u32[]{:S(2)}) collective-permute-start(bf16[1,512,256]{2,1,0:T(8,128)(2,1)S(1)} %collective-permute-done.8.refs_5_), channel_id=1, source_target_pairs={{0,128},{128,0},{1,129},{129,1},{2,130},{130,2},{3,131},{131,3},{4... | collective-permute-start | bytes 786440 | tf_op jit(solution)/shard_map/ppermute | solution.py:269
  56.3 1.2 %collective-permute-start.20 = (bf16[1,512,256]{2,1,0:T(8,128)(2,1)S(1)}, bf16[1,512,256]{2,1,0:T(8,128)(2,1)S(1)}, u32[]{:S(2)}, u32[]{:S(2)}) collective-permute-start(bf16[1,512,256]{2,1,0:T(8,128)(2,1)S(1)} %collective-permute-done.13.refs_2_), channel_id=1, source_target_pairs={{0,16},{16,32},{32,48},{48,64},{64,80},{80,96},{96,112},{112,0},{1... | collective-permute-start | bytes 786440 | tf_op jit(solution)/shard_map/ppermute | solution.py:269
  57.6 5.0 %collective-permute-done.14.refs_3_ = bf16[1,512,256]{2,1,0:T(8,128)(2,1)S(1)} collective-permute-done((bf16[1,512,256]{2,1,0:T(8,128)(2,1)S(1)}, bf16[1,512,256]{2,1,0:T(8,128)(2,1)S(1)}, u32[]{:S(2)}, u32[]{:S(2)}) %collective-permute-start.14) | collective-permute-done | bytes 262176 | tf_op jit(solution)/shard_map/ppermute | solution.py:269
  62.5 1.8 %collective-permute-start.21 = (bf16[1,512,256]{2,1,0:T(8,128)(2,1)S(1)}, bf16[1,512,256]{2,1,0:T(8,128)(2,1)S(1)}, u32[]{:S(2)}, u32[]{:S(2)}) collective-permute-start(bf16[1,512,256]{2,1,0:T(8,128)(2,1)S(1)} %collective-permute-done.14.refs_3_), channel_id=1, source_target_pairs={{0,112},{16,0},{32,16},{48,32},{64,48},{80,64},{96,80},{112,96},{1... | collective-permute-start | bytes 786440 | tf_op jit(solution)/shard_map/ppermute | solution.py:269
  64.6 2.7 %collective-permute-start.19 = (bf16[256,512]{1,0:T(8,128)(2,1)S(1)}, bf16[256,512]{1,0:T(8,128)(2,1)S(1)}, u32[]{:S(2)}, u32[]{:S(2)}) collective-permute-start(bf16[256,512]{1,0:T(8,128)(2,1)S(1)} %get-tuple-element.73.refs_5_), channel_id=1, source_target_pairs={{0,6},{2,0},{4,2},{6,4},{1,7},{3,1},{5,3},{7,5},{8,14},{10,8},{12,... | collective-permute-start | bytes 786440 | tf_op jit(solution)/shard_map/ppermute | solution.py:269
  68.0 4.5 %collective-permute-start.24 = (bf16[7,512,256]{2,1,0:T(8,128)(2,1)S(1)}, bf16[7,512,256]{2,1,0:T(8,128)(2,1)S(1)}, u32[]{:S(2)}, u32[]{:S(2)}) collective-permute-start(bf16[7,512,256]{2,1,0:T(8,128)(2,1)S(1)} %shard_map.68.refs_9_), channel_id=1, source_target_pairs={{0,8},{8,0},{1,9},{9,1},{2,10},{10,2},{3,11},{11,3},{4,12},{12,4},... | collective-permute-start | bytes 5505032 | tf_op jit(solution)/shard_map/ppermute | solution.py:269
  72.9 5.2 %collective-permute-start.25 = (bf16[3,512,256]{2,1,0:T(8,128)(2,1)S(1)}, bf16[3,512,256]{2,1,0:T(8,128)(2,1)S(1)}, u32[]{:S(2)}, u32[]{:S(2)}) collective-permute-start(bf16[3,512,256]{2,1,0:T(8,128)(2,1)S(1)} %shard_map.69.refs_10_), channel_id=1, source_target_pairs={{0,8},{8,0},{1,9},{9,1},{2,10},{10,2},{3,11},{11,3},{4,12},{12,4},... | collective-permute-start | bytes 2359304 | tf_op jit(solution)/shard_map/ppermute | solution.py:269
  78.1 2.1 %shard_map.70 = (f32[2,256,256]{2,1,0:T(8,128)S(1)}, bf16[256,4096]{1,0:T(8,128)(2,1)S(1)}) custom-call(bf16[256,512]{1,0:T(8,128)(2,1)S(1)} %bitcast.144, bf16[256,512]{1,0:T(8,128)(2,1)S(1)} %bitcast.145, bf16[256,512]{1,0:T(8,128)(2,1)S(1)} %get-tuple-element.76.refs_2_, bf16[256,512]{1,0:T(8,128)(2,1)S(1)} %get-tuple-element.75.refs_3_, ...), custom_call_target="tpu_custom_call" | custom-call | flops 34359738368 | bytes 6291456 | tf_op jit(solution)/shard_map/pallas_call | solution.py:231
  80.3 2.7 %shard_map.71 = bf16[256,1024]{1,0:T(8,128)(2,1)} custom-call(f32[2,256,256]{2,1,0:T(8,128)S(1)} %get-tuple-element.69.refs_0_, bf16[256,4096]{1,0:T(8,128)(2,1)S(1)} %get-tuple-element.70.refs_1_, bf16[6,512,256]{2,1,0:T(8,128)(2,1)S(1)} %collective-permute-done.23.refs_2_, bf16[7,512,256]{2,1,0:T(8,128)(2,1)S(1)} %collective-permute-done.24.refs_3_, ...), custom_call_target="tpu_custom_call" | custom-call | flops 34359738368 | bytes 6291456 | tf_op jit(solution)/shard_map/pallas_call | solution.py:240
  (64 shorter events, 13.4 us)
Async XLA Ops:
  0.0 20.8 %collective-permute-start = (bf16[512,256]{1,0:T(8,128)(2,1)}, bf16[512,256]{1,0:T(8,128)(2,1)S(1)}, u32[]{:S(2)}, u32[]{:S(2)}) collective-permute-start(bf16[512,256]{1,0:T(8,128)(2,1)} %param.11), channel_id=1, source_target_pairs={{0,80},{8,88},{16,64},{24,72},{32,241},{40,249},{48,225},{56,233},... | collective-permute-start | bytes 786440 | tf_op jit(solution)/shard_map/ppermute | solution.py:265
  13.7 16.0 %all-to-all-start = ((f32[16,16,256]{2,1,0:T(8,128)}), f32[16,16,256]{2,1,0:T(8,128)S(1)}, u32[]{:S(2)}, u32[]{:S(2)}) async-start(f32[16,16,256]{2,1,0:T(8,128)} %broadcast_in_dim.13), calls=%async_computation | async-start | bytes 524288 | tf_op jit(solution)/shard_map/all_to_all | solution.py:299
  20.8 14.3 %collective-permute-start.3 = (bf16[1,512,256]{2,1,0:T(8,128)(2,1)S(1)}, bf16[1,512,256]{2,1,0:T(8,128)(2,1)S(1)}, u32[]{:S(2)}, u32[]{:S(2)}) collective-permute-start(bf16[1,512,256]{2,1,0:T(8,128)(2,1)S(1)} %bitcast.146), channel_id=1, source_target_pairs={{0,128},{128,0},{1,129},{129,1},{2,130},{130,2},{3,131},{131,3},{4... | collective-permute-start | bytes 786440 | tf_op jit(solution)/shard_map/ppermute | solution.py:269
  22.2 12.8 %collective-permute-start.4 = (bf16[1,512,256]{2,1,0:T(8,128)(2,1)S(1)}, bf16[1,512,256]{2,1,0:T(8,128)(2,1)S(1)}, u32[]{:S(2)}, u32[]{:S(2)}) collective-permute-start(bf16[1,512,256]{2,1,0:T(8,128)(2,1)S(1)} %bitcast.147), channel_id=1, source_target_pairs={{0,16},{16,32},{32,48},{48,64},{64,80},{80,96},{96,112},{112,0},{1... | collective-permute-start | bytes 786440 | tf_op jit(solution)/shard_map/ppermute | solution.py:269
  23.4 11.7 %collective-permute-start.5 = (bf16[1,512,256]{2,1,0:T(8,128)(2,1)S(1)}, bf16[1,512,256]{2,1,0:T(8,128)(2,1)S(1)}, u32[]{:S(2)}, u32[]{:S(2)}) collective-permute-start(bf16[1,512,256]{2,1,0:T(8,128)(2,1)S(1)} %bitcast.148), channel_id=1, source_target_pairs={{0,112},{16,0},{32,16},{48,32},{64,48},{80,64},{96,80},{112,96},{1... | collective-permute-start | bytes 786440 | tf_op jit(solution)/shard_map/ppermute | solution.py:269
  35.1 7.8 %collective-permute-start.7 = (bf16[1,512,256]{2,1,0:T(8,128)(2,1)S(1)}, bf16[1,512,256]{2,1,0:T(8,128)(2,1)S(1)}, u32[]{:S(2)}, u32[]{:S(2)}) collective-permute-start(bf16[1,512,256]{2,1,0:T(8,128)(2,1)S(1)} %collective-permute-done.4.refs_2_), channel_id=1, source_target_pairs={{0,16},{16,32},{32,48},{48,64},{64,80},{80,96},{96,112},{112,0},{1... | collective-permute-start | bytes 786440 | tf_op jit(solution)/shard_map/ppermute | solution.py:269
  35.7 7.2 %collective-permute-start.8 = (bf16[1,512,256]{2,1,0:T(8,128)(2,1)S(1)}, bf16[1,512,256]{2,1,0:T(8,128)(2,1)S(1)}, u32[]{:S(2)}, u32[]{:S(2)}) collective-permute-start(bf16[1,512,256]{2,1,0:T(8,128)(2,1)S(1)} %collective-permute-done.5.refs_3_), channel_id=1, source_target_pairs={{0,112},{16,0},{32,16},{48,32},{64,48},{80,64},{96,80},{112,96},{1... | collective-permute-start | bytes 786440 | tf_op jit(solution)/shard_map/ppermute | solution.py:269
  37.9 7.8 %collective-permute-start.6 = (bf16[1,256,512]{2,1,0:T(8,128)(2,1)S(1)}, bf16[1,256,512]{2,1,0:T(8,128)(2,1)S(1)}, u32[]{:S(2)}, u32[]{:S(2)}) collective-permute-start(bf16[1,256,512]{2,1,0:T(8,128)(2,1)S(1)} %shard_map.66), channel_id=1, source_target_pairs={{0,1},{1,0},{2,3},{3,2},{4,5},{5,4},{6,7},{7,6},{8,9},{9,8},{10,11... | collective-permute-start | bytes 786440 | tf_op jit(solution)/shard_map/ppermute | solution.py:269
  39.9 8.7 %collective-permute-start.16 = (bf16[1,512,256]{2,1,0:T(8,128)(2,1)S(1)}, bf16[1,512,256]{2,1,0:T(8,128)(2,1)S(1)}, u32[]{:S(2)}, u32[]{:S(2)}) collective-permute-start(bf16[1,512,256]{2,1,0:T(8,128)(2,1)S(1)} %collective-permute-done.3.refs_1_), channel_id=1, source_target_pairs={{0,16},{16,32},{32,48},{48,64},{64,80},{80,96},{96,112},{112,0},{1... | collective-permute-start | bytes 786440 | tf_op jit(solution)/shard_map/ppermute | solution.py:269
  39.9 8.7 %collective-permute-start.17 = (bf16[1,512,256]{2,1,0:T(8,128)(2,1)S(1)}, bf16[1,512,256]{2,1,0:T(8,128)(2,1)S(1)}, u32[]{:S(2)}, u32[]{:S(2)}) collective-permute-start(bf16[1,512,256]{2,1,0:T(8,128)(2,1)S(1)} %collective-permute-done.3.refs_1_), channel_id=1, source_target_pairs={{0,112},{16,0},{32,16},{48,32},{64,48},{80,64},{96,80},{112,96},{1... | collective-permute-start | bytes 786440 | tf_op jit(solution)/shard_map/ppermute | solution.py:269
  42.9 11.3 %collective-permute-start.11 = (bf16[1,512,256]{2,1,0:T(8,128)(2,1)S(1)}, bf16[1,512,256]{2,1,0:T(8,128)(2,1)S(1)}, u32[]{:S(2)}, u32[]{:S(2)}) collective-permute-start(bf16[1,512,256]{2,1,0:T(8,128)(2,1)S(1)} %collective-permute-done.7.refs_4_), channel_id=1, source_target_pairs={{0,16},{16,32},{32,48},{48,64},{64,80},{80,96},{96,112},{112,0},{1... | collective-permute-start | bytes 786440 | tf_op jit(solution)/shard_map/ppermute | solution.py:269
  42.9 12.6 %collective-permute-start.12 = (bf16[1,512,256]{2,1,0:T(8,128)(2,1)S(1)}, bf16[1,512,256]{2,1,0:T(8,128)(2,1)S(1)}, u32[]{:S(2)}, u32[]{:S(2)}) collective-permute-start(bf16[1,512,256]{2,1,0:T(8,128)(2,1)S(1)} %collective-permute-done.8.refs_5_), channel_id=1, source_target_pairs={{0,112},{16,0},{32,16},{48,32},{64,48},{80,64},{96,80},{112,96},{1... | collective-permute-start | bytes 786440 | tf_op jit(solution)/shard_map/ppermute | solution.py:269
  45.7 18.7 %collective-permute-start.10 = (bf16[2,256,512]{2,1,0:T(8,128)(2,1)S(1)}, bf16[2,256,512]{2,1,0:T(8,128)(2,1)S(1)}, u32[]{:S(2)}, u32[]{:S(2)}) collective-permute-start(bf16[2,256,512]{2,1,0:T(8,128)(2,1)S(1)} %constant_dynamic-update-slice_fusion), channel_id=1, source_target_pairs={{0,6},{2,0},{4,2},{6,4},{1,7},{3,1},{5,3},{7,5},{8,14},{10,8},{12,... | collective-permute-start | bytes 1572872 | tf_op jit(solution)/shard_map/ppermute | solution.py:269
  48.6 15.8 %collective-permute-start.9 = (bf16[2,256,512]{2,1,0:T(8,128)(2,1)S(1)}, bf16[2,256,512]{2,1,0:T(8,128)(2,1)S(1)}, u32[]{:S(2)}, u32[]{:S(2)}) collective-permute-start(bf16[2,256,512]{2,1,0:T(8,128)(2,1)S(1)} %constant_dynamic-update-slice_fusion), channel_id=1, source_target_pairs={{0,2},{2,4},{4,6},{6,0},{1,3},{3,5},{5,7},{7,1},{8,10},{10,12},{12... | collective-permute-start | bytes 1572872 | tf_op jit(solution)/shard_map/ppermute | solution.py:269
  48.6 7.7 %collective-permute-start.13 = (bf16[1,512,256]{2,1,0:T(8,128)(2,1)S(1)}, bf16[1,512,256]{2,1,0:T(8,128)(2,1)S(1)}, u32[]{:S(2)}, u32[]{:S(2)}) collective-permute-start(bf16[1,512,256]{2,1,0:T(8,128)(2,1)S(1)} %collective-permute-done.7.refs_4_), channel_id=1, source_target_pairs={{0,128},{128,0},{1,129},{129,1},{2,130},{130,2},{3,131},{131,3},{4... | collective-permute-start | bytes 786440 | tf_op jit(solution)/shard_map/ppermute | solution.py:269
  54.2 8.3 %collective-permute-start.14 = (bf16[1,512,256]{2,1,0:T(8,128)(2,1)S(1)}, bf16[1,512,256]{2,1,0:T(8,128)(2,1)S(1)}, u32[]{:S(2)}, u32[]{:S(2)}) collective-permute-start(bf16[1,512,256]{2,1,0:T(8,128)(2,1)S(1)} %collective-permute-done.8.refs_5_), channel_id=1, source_target_pairs={{0,128},{128,0},{1,129},{129,1},{2,130},{130,2},{3,131},{131,3},{4... | collective-permute-start | bytes 786440 | tf_op jit(solution)/shard_map/ppermute | solution.py:269
  55.5 8.8 %collective-permute-start.15 = (bf16[1,512,256]{2,1,0:T(8,128)(2,1)S(1)}, bf16[1,512,256]{2,1,0:T(8,128)(2,1)S(1)}, u32[]{:S(2)}, u32[]{:S(2)}) collective-permute-start(bf16[1,512,256]{2,1,0:T(8,128)(2,1)S(1)} %collective-permute-done.11.refs_0_), channel_id=1, source_target_pairs={{0,16},{16,32},{32,48},{48,64},{64,80},{80,96},{96,112},{112,0},{1... | collective-permute-start | bytes 786440 | tf_op jit(solution)/shard_map/ppermute | solution.py:269
  56.3 11.7 %collective-permute-start.20 = (bf16[1,512,256]{2,1,0:T(8,128)(2,1)S(1)}, bf16[1,512,256]{2,1,0:T(8,128)(2,1)S(1)}, u32[]{:S(2)}, u32[]{:S(2)}) collective-permute-start(bf16[1,512,256]{2,1,0:T(8,128)(2,1)S(1)} %collective-permute-done.13.refs_2_), channel_id=1, source_target_pairs={{0,16},{16,32},{32,48},{48,64},{64,80},{80,96},{96,112},{112,0},{1... | collective-permute-start | bytes 786440 | tf_op jit(solution)/shard_map/ppermute | solution.py:269
  62.5 10.0 %collective-permute-start.21 = (bf16[1,512,256]{2,1,0:T(8,128)(2,1)S(1)}, bf16[1,512,256]{2,1,0:T(8,128)(2,1)S(1)}, u32[]{:S(2)}, u32[]{:S(2)}) collective-permute-start(bf16[1,512,256]{2,1,0:T(8,128)(2,1)S(1)} %collective-permute-done.14.refs_3_), channel_id=1, source_target_pairs={{0,112},{16,0},{32,16},{48,32},{64,48},{80,64},{96,80},{112,96},{1... | collective-permute-start | bytes 786440 | tf_op jit(solution)/shard_map/ppermute | solution.py:269
  64.4 8.2 %collective-permute-start.18 = (bf16[256,512]{1,0:T(8,128)(2,1)S(1)}, bf16[256,512]{1,0:T(8,128)(2,1)S(1)}, u32[]{:S(2)}, u32[]{:S(2)}) collective-permute-start(bf16[256,512]{1,0:T(8,128)(2,1)S(1)} %get-tuple-element.76.refs_2_), channel_id=1, source_target_pairs={{0,2},{2,4},{4,6},{6,0},{1,3},{3,5},{5,7},{7,1},{8,10},{10,12},{12... | collective-permute-start | bytes 786440 | tf_op jit(solution)/shard_map/ppermute | solution.py:269
  64.6 8.0 %collective-permute-start.19 = (bf16[256,512]{1,0:T(8,128)(2,1)S(1)}, bf16[256,512]{1,0:T(8,128)(2,1)S(1)}, u32[]{:S(2)}, u32[]{:S(2)}) collective-permute-start(bf16[256,512]{1,0:T(8,128)(2,1)S(1)} %get-tuple-element.73.refs_5_), channel_id=1, source_target_pairs={{0,6},{2,0},{4,2},{6,4},{1,7},{3,1},{5,3},{7,5},{8,14},{10,8},{12,... | collective-permute-start | bytes 786440 | tf_op jit(solution)/shard_map/ppermute | solution.py:269
  68.0 12.2 %collective-permute-start.24 = (bf16[7,512,256]{2,1,0:T(8,128)(2,1)S(1)}, bf16[7,512,256]{2,1,0:T(8,128)(2,1)S(1)}, u32[]{:S(2)}, u32[]{:S(2)}) collective-permute-start(bf16[7,512,256]{2,1,0:T(8,128)(2,1)S(1)} %shard_map.68.refs_9_), channel_id=1, source_target_pairs={{0,8},{8,0},{1,9},{9,1},{2,10},{10,2},{3,11},{11,3},{4,12},{12,4},... | collective-permute-start | bytes 5505032 | tf_op jit(solution)/shard_map/ppermute | solution.py:269
  72.5 7.8 %collective-permute-start.23 = (bf16[6,512,256]{2,1,0:T(8,128)(2,1)S(1)}, bf16[6,512,256]{2,1,0:T(8,128)(2,1)S(1)}, u32[]{:S(2)}, u32[]{:S(2)}) collective-permute-start(bf16[6,512,256]{2,1,0:T(8,128)(2,1)S(1)} %shard_map.67.refs_8_), channel_id=1, source_target_pairs={{0,8},{8,0},{1,9},{9,1},{2,10},{10,2},{3,11},{11,3},{4,12},{12,4},... | collective-permute-start | bytes 4718600 | tf_op jit(solution)/shard_map/ppermute | solution.py:269
  72.9 7.3 %collective-permute-start.25 = (bf16[3,512,256]{2,1,0:T(8,128)(2,1)S(1)}, bf16[3,512,256]{2,1,0:T(8,128)(2,1)S(1)}, u32[]{:S(2)}, u32[]{:S(2)}) collective-permute-start(bf16[3,512,256]{2,1,0:T(8,128)(2,1)S(1)} %shard_map.69.refs_10_), channel_id=1, source_target_pairs={{0,8},{8,0},{1,9},{9,1},{2,10},{10,2},{3,11},{11,3},{4,12},{12,4},... | collective-permute-start | bytes 2359304 | tf_op jit(solution)/shard_map/ppermute | solution.py:269
  (12 other events, 42.2 us)
